TPU v7x, 32 devices: a whole 2x2x4 slice. The times are simulated.
32 devices in a mesh: pole: 2 (over x), row: 4 (over y, core), col: 4 (over z).
Axes of the slice: x: 2, y: 2, z: 4, core: 2. Of those that a mesh axis runs over, the one named last changes fastest.
Arguments:
- inverse_tile: float32 [2, 2, 4608, 4608], P('pole', None, 'row', 'col'), may hold values from -0.0625 to 0.0625
- lower_factor: float32 [2, 2, 256, 4608], P('pole', None, 'row', 'col'), may hold values from -6 to 6
- upper_factor: float32 [2, 2, 256, 4608], P('pole', None, 'col', 'row'), may hold values from -1.5 to 1.5
- pivot_inverse: float32 [2, 2, 256, 256], P('pole', None, 'row', 'col'), may hold values from -48 to 48
- pole_weights: float32 [2, 2], P('pole'), may hold values from -3 to 3
- block_owners: int32 [576, 6], replicated, may hold values from 0 to 31, all different within a row; in each aligned block of 18 rows (0 to 17, 18 to 35, ...) at most 4 rows name the same one
- basis_ancestor: float32 [4608, 4096], P(None, ('pole', 'row', 'col')), may hold values from -3 to 3
- basis_super: float32 [256, 4096], P(None, ('pole', 'row', 'col')), may hold values from -0.09375 to 0.09375
Outputs:
- upper_density: float32 [256, 4608], P(('pole', 'row'), 'col')
- charge: float32 [4096], P(('pole', 'row', 'col'))
Inputs may be any that keep to these rules, and one draw needn't show every extreme that they name: `block_owners`: each row names 6 different owners. Among the rows k * 18 to (k + 1) * 18 - 1, for each k, no owner is named more than 4 times, and in every draw some owner is named exactly 4 times there. Every owner is named by some row.
All inputs are finite; a program needn't handle non-finite values.
Results may differ from a plain program's by a relative error of at most 0.0003.
Values sent between devices are 32-bit elements; how exact they have to be, the bound alone decides.
No kernel may reach another device: no remote copies, remote signals or barrier semaphores. Data moves between devices by JAX's collectives and lax.ppermute only.
A program may use at most 64 MiB of HBM per device.

v0:
```python
import jax
import jax.numpy as jnp
from jax import lax
from jax.sharding import PartitionSpec as P

NB = 18
TOPK = 6


def contract_last(left, right):
    return lax.dot_general(
        left,
        right,
        (((1,), (1,)), ((), ())),
        precision=lax.Precision.HIGHEST,
        preferred_element_type=jnp.float32,
    )


def matmul(left, right):
    return jnp.dot(left, right, precision=lax.Precision.HIGHEST, preferred_element_type=jnp.float32)


def body(
    inverse_tile,
    lower_factor,
    upper_factor,
    pivot_inverse,
    pole_weights,
    block_owners,
    basis_ancestor,
    basis_super,
):
    tile_re = inverse_tile[0, 0]
    tile_im = inverse_tile[0, 1]
    weight_re = pole_weights[0, 0]
    weight_im = pole_weights[0, 1]
    tile_cols = tile_re.shape[1]
    super_width = basis_super.shape[0]
    fragment = lax.all_gather(lower_factor, "row", axis=2, tiled=True)
    frag_re = fragment[0, 0]
    frag_im = fragment[0, 1]
    prod_re = contract_last(tile_re, frag_re) - contract_last(tile_im, frag_im)
    prod_im = contract_last(tile_re, frag_im) + contract_last(tile_im, frag_re)
    tile_lower = jnp.stack([prod_re, prod_im])
    lower_re = tile_lower[0]
    lower_im = tile_lower[1]
    fragment = lax.all_gather(upper_factor, "col", axis=2, tiled=True)
    frag_re = fragment[0, 0]
    frag_im = fragment[0, 1]
    first_re = matmul(frag_re, tile_re) - matmul(frag_im, tile_im)
    first_im = matmul(frag_re, tile_im) + matmul(frag_im, tile_re)
    second_re = matmul(frag_re, lower_re) - matmul(frag_im, lower_im)
    second_im = matmul(frag_re, lower_im) + matmul(frag_im, lower_re)
    upper_all = jnp.stack(
        [jnp.concatenate([first_re, second_re], 1), jnp.concatenate([first_im, second_im], 1)]
    )
    lower_term = -(weight_re * lower_im + weight_im * lower_re)
    upper_term = -(
        weight_re * upper_all[1, :, :tile_cols] + weight_im * upper_all[0, :, :tile_cols]
    )
    pivot_term = weight_re * upper_all[1, :, tile_cols:] + weight_im * upper_all[0, :, tile_cols:]
    piece_rows = pivot_inverse.shape[2]
    piece_cols = pivot_inverse.shape[3]
    pivot_piece = weight_re * pivot_inverse[0, 1] + weight_im * pivot_inverse[0, 0]
    placed = lax.dynamic_update_slice(
        jnp.zeros_like(pivot_term),
        pivot_piece,
        (lax.axis_index("row") * piece_rows, lax.axis_index("col") * piece_cols),
    )
    pivot_term = pivot_term + placed
    lower_rows = lax.psum_scatter(lower_term, ("pole", "col"), scatter_dimension=0, tiled=True)
    upper_density = lax.psum_scatter(upper_term, ("pole", "row"), scatter_dimension=0, tiled=True)
    pivot_density = lax.psum(pivot_term, ("pole", "row", "col"))
    n_pole = lax.axis_size("pole")
    n_row = lax.axis_size("row")
    n_col = lax.axis_size("col")
    devices_all = n_pole * n_row * n_col
    capacity = max(2, (NB * TOPK + devices_all - 1) // devices_all)
    rows_here = lower_rows.shape[0]
    block_rows = rows_here // NB
    position = (
        lax.axis_index("row") * (n_pole * n_col)
        + lax.axis_index("pole") * n_col
        + lax.axis_index("col")
    )
    first_block = position * NB
    owners_here = lax.dynamic_slice_in_dim(block_owners, first_block, NB, 0)
    flat_owner = owners_here.reshape(-1)
    one_hot = (flat_owner[:, None] == jnp.arange(devices_all, dtype=jnp.int32)[None, :]).astype(
        jnp.int32
    )
    earlier = jnp.cumsum(one_hot, 0) - one_hot
    slot_rank = jnp.sum(earlier * one_hot, 1)
    slot_index = (flat_owner * capacity + slot_rank).reshape(NB, TOPK)
    selector = jnp.sum(
        (
            slot_index[:, :, None]
            == jnp.arange(devices_all * capacity, dtype=jnp.int32)[None, None, :]
        ).astype(jnp.int32),
        1,
    )
    block_values = lower_rows.reshape(NB, block_rows * super_width)
    send_values = lax.dot_general(
        selector.astype(jnp.float32),
        block_values,
        (((0,), (0,)), ((), ())),
        precision=lax.Precision.HIGHEST,
        preferred_element_type=jnp.float32,
    )
    block_ids = first_block + jnp.arange(NB, dtype=jnp.int32)
    send_ids = jnp.sum(selector * block_ids[:, None], 0)
    recv_values, recv_ids = (
        lax.all_to_all(
            send_values.reshape(devices_all, capacity, block_rows * super_width),
            ("pole", "row", "col"),
            split_axis=0,
            concat_axis=0,
            tiled=True,
        ),
        lax.all_to_all(
            send_ids.reshape(devices_all, capacity),
            ("pole", "row", "col"),
            split_axis=0,
            concat_axis=0,
            tiled=True,
        ),
    )
    row_ids = (
        recv_ids.reshape(-1)[:, None] * block_rows
        + jnp.arange(block_rows, dtype=jnp.int32)[None, :]
    ).reshape(-1)
    ancestor_rows = jnp.take(basis_ancestor, row_ids, axis=0)
    received = recv_values.reshape(-1, super_width)
    projected = matmul(received, basis_super)
    ancestor_part = jnp.sum(ancestor_rows * projected, 0)
    pivot_part = jnp.sum(basis_super * matmul(pivot_density, basis_super), 0)
    charge = ancestor_part + pivot_part
    return (upper_density, charge)


def solution(mesh):
    placed = (
        P("pole", None, "row", "col"),
        P("pole", None, "row", "col"),
        P("pole", None, "col", "row"),
        P("pole", None, "row", "col"),
        P("pole", None),
        P(),
        P(None, ("pole", "row", "col")),
        P(None, ("pole", "row", "col")),
    )
    return jax.shard_map(
        body,
        mesh=mesh,
        in_specs=placed,
        out_specs=(P(("pole", "row"), "col"), P(("pole", "row", "col"))),
        check_vma=False,
    )
```

profile of v0, /device:TPU:0, one launch (start us, length us, event | category | flops | bytes accessed | tf_op | source)
XLA Modules:
  0.0 335.3 jit_solution(7020914785032292870)
XLA Ops:
  11.1 7.3 %all-to-all-start = ((s32[32,1,4]{2,1,0:T(1,128)}), s32[32,1,4]{2,1,0:T(1,128)S(1)}, u32[]{:S(2)}, u32[]{:S(2)}) async-start(s32[32,1,4]{2,1,0:T(1,128)} %bitcast.13), calls=%async_computation.1 | async-start | bytes 32768 | tf_op jit(solution)/shard_map/all_to_all | solution.py:121
  19.8 16.7 %all-gather.5.cloned.1.call-done = f32[1,2,256,1152]{3,2,1,0:T(8,128)} async-done(((f32[1,2,64,1152]{3,2,1,0:T(8,128)}), f32[1,2,256,1152]{3,2,1,0:T(8,128)}) %all-gather.5.cloned.1.call-update) | async-done | bytes 2359312 | tf_op jit(solution)/shard_map/all_gather | solution.py:40
  36.5 7.3 %fusion.4 = f32[1152,256]{1,0:T(8,128)S(1)} fusion(f32[1,2,1152,1152]{3,2,1,0:T(8,128)} %param.8, f32[1,2,256,1152]{3,2,1,0:T(8,128)} %all-gather.5.cloned.1.call-done), kind=kOutput, calls=%fused_computation.5 | convolution fusion | flops 4076863488 | bytes 7667712 | tf_op jit(solution)/shard_map/dot_general | solution.py:11
  43.8 7.7 %fusion.2 = f32[1152,256]{1,0:T(8,128)S(1)} fusion(f32[1,2,1152,1152]{3,2,1,0:T(8,128)} %param.8, f32[1,2,256,1152]{3,2,1,0:T(8,128)} %all-gather.5.cloned.1.call-done), kind=kOutput, calls=%fused_computation.3 | convolution fusion | flops 4076863488 | bytes 7667712 | tf_op jit(solution)/shard_map/dot_general | solution.py:11
  51.5 4.8 %fusion.27 = f32[1152,256]{1,0:T(8,128)S(1)} fusion(f32[1152,256]{1,0:T(8,128)S(1)} %fusion.4, f32[1,2,1152,1152]{3,2,1,0:T(8,128)S(1)} %copy-done.1, f32[1,2,256,1152]{3,2,1,0:T(8,128)S(1)} %copy-done.4), kind=kOutput, calls=%fused_computation.26 | convolution fusion | flops 4077158400 | bytes 8847360 | tf_op jit(solution)/shard_map/dot_general | solution.py:11
  56.4 7.6 %add_negate_fusion = (f32[1152,256]{1,0:T(8,128)}, f32[1152,256]{1,0:T(8,128)}) fusion(f32[1152,256]{1,0:T(8,128)S(1)} %fusion.27, f32[]{:T(128)} %bitcast.9, f32[]{:T(128)} %bitcast, f32[1152,256]{1,0:T(8,128)S(1)} %fusion.2, f32[1,2,256,1152]{3,2,1,0:T(8,128)S(1)} %copy-done.4, f32[1,2,1152,1152]{3,2,1,0:T(8,128)S(1)} %copy-done.1), kind=kOutput, calls=%fused_computation.41 | convolution fusion | flops 4078338048 | bytes 11206664 | tf_op jit(solution)/shard_map/dot_general | solution.py:11
  64.4 24.0 %all-gather.3.cloned.1.call-done = f32[1,2,256,1152]{3,2,1,0:T(8,128)} async-done(((f32[1,2,64,1152]{3,2,1,0:T(8,128)}), f32[1,2,256,1152]{3,2,1,0:T(8,128)}) %all-gather.3.cloned.1.call-update) | async-done | bytes 2359312 | tf_op jit(solution)/shard_map/all_gather | solution.py:48
  88.5 2.7 fusion.44
  91.2 8.1 %fusion.6 = f32[256,1152]{1,0:T(8,128)S(1)} fusion(f32[1,2,1152,1152]{3,2,1,0:T(8,128)} %param.8, f32[1,2,256,1152]{3,2,1,0:T(8,128)S(1)} %copy-done.2), kind=kOutput, calls=%fused_computation.7 | convolution fusion | flops 4076863488 | bytes 7667712 | tf_op jit(solution)/shard_map/dot_general | solution.py:21
  100.6 1.3 fusion.40
  103.3 8.2 %fusion = f32[256,1152]{1,0:T(8,128)S(1)} fusion(f32[1,2,1152,1152]{3,2,1,0:T(8,128)} %param.8, f32[1,2,256,1152]{3,2,1,0:T(8,128)S(1)} %copy-done.2), kind=kOutput, calls=%fused_computation.1 | convolution fusion | flops 4076863488 | bytes 7667712 | tf_op jit(solution)/shard_map/dot_general | solution.py:21
  111.5 5.5 %fusion.24 = f32[256,1152]{1,0:T(8,128)S(1)} fusion(f32[256,1152]{1,0:T(8,128)S(1)} %fusion.6, f32[1,2,1152,1152]{3,2,1,0:T(8,128)S(1)} %bitcast.82, f32[1,2,256,1152]{3,2,1,0:T(8,128)S(1)} %copy-done.2), kind=kOutput, calls=%fused_computation.25 | convolution fusion | flops 4077158400 | bytes 8847360 | tf_op jit(solution)/shard_map/dot_general | solution.py:21
  117.0 5.8 %fusion.33 = f32[256,1152]{1,0:T(8,128)S(1)} fusion(f32[256,1152]{1,0:T(8,128)S(1)} %fusion, f32[1,2,1152,1152]{3,2,1,0:T(8,128)S(1)} %bitcast.82, f32[1,2,256,1152]{3,2,1,0:T(8,128)S(1)} %copy-done.2), kind=kOutput, calls=%fused_computation.28 | convolution fusion | flops 4077158400 | bytes 8847360 | tf_op jit(solution)/shard_map/dot_general | solution.py:21
  125.4 1.4 bitcast_add_fusion
  128.6 26.1 %reduce-scatter.5.cloned.1.call-done = f32[144,256]{1,0:T(8,128)} async-done(((f32[1152,256]{1,0:T(8,128)}), f32[144,256]{1,0:T(8,128)}) %reduce-scatter.5.cloned.1.call-update) | async-done | bytes 147472 | tf_op jit(solution)/shard_map/reduce_scatter | solution.py:72
  156.6 1.7 copy.38
  158.3 3.6 %all-to-all-start.1 = ((f32[32,4,2048]{2,1,0:T(4,128)}), f32[32,4,2048]{2,1,0:T(4,128)S(1)}, u32[]{:S(2)}, u32[]{:S(2)}) async-start(f32[32,4,2048]{2,1,0:T(4,128)} %copy.38), calls=%async_computation.3 | async-start | bytes 2097152 | tf_op jit(solution)/shard_map/all_to_all | solution.py:114
  161.9 4.1 %fusion.38 = f32[256,1152]{1,0:T(8,128)} fusion(f32[1,256,1408]{2,1,0:T(8,128)} %copy-done.6, f32[1,256,1408]{2,1,0:T(8,128)} %copy-done.5, f32[]{:T(128)} %bitcast.9, f32[]{:T(128)} %bitcast), kind=kLoop, calls=%fused_computation.35 | loop fusion | flops 1179648 | bytes 3538952 | tf_op jit(solution)/shard_map/neg | solution.py:59
  166.6 4.0 %gather_fusion = f32[1024,128]{1,0:T(8,128)} fusion(f32[4608,128]{1,0:T(8,128)S(1)} %copy-done, s32[1024]{0:T(1024)S(1)} %broadcast_clamp_fusion), kind=kCustom, calls=%fused_computation | custom fusion | bytes 1052672 | tf_op jit(solution)/shard_map/jit(_take)/gather | solution.py:133
  170.6 118.5 %all-reduce.2.cloned.1.call-done = f32[256,256]{1,0:T(8,128)} async-done(((f32[256,256]{1,0:T(8,128)}), f32[256,256]{1,0:T(8,128)}) %all-reduce.2.cloned.1.call-update) | async-done | bytes 262160 | tf_op jit(solution)/shard_map/psum | solution.py:74
  289.1 1.3 fusion.42
  290.4 1.5 reshape.95
  291.9 2.4 fusion.39
  294.8 33.8 %reduce-scatter.3.cloned.1.call-done = f32[32,1152]{1,0:T(8,128)} async-done(((f32[256,1152]{1,0:T(8,128)}), f32[32,1152]{1,0:T(8,128)}) %reduce-scatter.3.cloned.1.call-update) | async-done | bytes 147472 | tf_op jit(solution)/shard_map/reduce_scatter | solution.py:73
  (73 shorter events, 15.7 us)
Async XLA Ops:
  7.2 159.4 %copy-start = (f32[4608,128]{1,0:T(8,128)S(1)}, f32[4608,128]{1,0:T(8,128)}, u32[]{:S(2)}) copy-start(f32[4608,128]{1,0:T(8,128)} %param.14) | copy-start | bytes 7077892
  7.2 12.0 %copy-start.11 = (f32[1,2]{1,0:T(1,128)S(1)}, f32[1,2]{1,0:T(1,128)}, u32[]{:S(2)}) copy-start(f32[1,2]{1,0:T(1,128)} %param.12) | copy-start | bytes 28
  7.2 29.3 %all-gather.5.cloned.1.call-start = ((), (), s32[]{:S(2)}) async-start(), calls=%async_computation.5 | async-start | bytes 2949120 | tf_op jit(solution)/shard_map/all_gather | solution.py:40
  7.9 80.6 %all-gather.3.cloned.1.call-start = ((), (), s32[]{:S(2)}) async-start(), calls=%async_computation.4 | async-start | bytes 2949120 | tf_op jit(solution)/shard_map/all_gather | solution.py:48
  11.1 147.2 %all-to-all-start = ((s32[32,1,4]{2,1,0:T(1,128)}), s32[32,1,4]{2,1,0:T(1,128)S(1)}, u32[]{:S(2)}, u32[]{:S(2)}) async-start(s32[32,1,4]{2,1,0:T(1,128)} %bitcast.13), calls=%async_computation.1 | async-start | bytes 32768 | tf_op jit(solution)/shard_map/all_to_all | solution.py:121
  18.4 136.3 %reduce-scatter.5.cloned.1.call-start = ((), (), s32[]{:S(2)}) async-start(), calls=%async_computation.7 | async-start | bytes 1327104 | tf_op jit(solution)/shard_map/reduce_scatter | solution.py:72
  36.5 15.0 %copy-start.1 = (f32[1,2,1152,1152]{3,2,1,0:T(8,128)S(1)}, f32[1,2,1152,1152]{3,2,1,0:T(8,128)}, u32[]{:S(2)}) copy-start(f32[1,2,1152,1152]{3,2,1,0:T(8,128)} %param.8) | copy-start | bytes 31850500
  43.8 7.7 %copy-start.4 = (f32[1,2,256,1152]{3,2,1,0:T(8,128)S(1)}, f32[1,2,256,1152]{3,2,1,0:T(8,128)}, u32[]{:S(2)}) copy-start(f32[1,2,256,1152]{3,2,1,0:T(8,128)} %all-gather.5.cloned.1.call-done) | copy-start | bytes 7077892
  64.0 225.1 %all-reduce.2.cloned.1.call-start = ((), (), s32[]{:S(2)}) async-start(), calls=%async_computation.8 | async-start | bytes 524288 | tf_op jit(solution)/shard_map/psum | solution.py:74
  88.5 2.7 copy-start.2
  91.2 8.1 %copy-start.3 = (f32[1152,256]{1,0:T(8,128)S(1)}, f32[1152,256]{1,0:T(8,128)}, u32[]{:S(2)}) copy-start(f32[1152,256]{1,0:T(8,128)} %get-tuple-element.7) | copy-start | bytes 3538948
  91.2 20.3 %slice-start = ((s8[10616832]{0:T(1024)(128)(4,1)}), s8[4194304]{0:T(1024)(128)(4,1)S(1)}, s32[]{:S(2)}) async-start(s8[10616832]{0:T(1024)(128)(4,1)} %bitcast.81), calls=%async_computation.9 | async-start | bytes 8388608
  99.3 12.1 %slice-start.1 = ((s8[10616832]{0:T(1024)(128)(4,1)}), s8[4194304]{0:T(1024)(128)(4,1)S(1)}, s32[]{:S(2)}) async-start(s8[10616832]{0:T(1024)(128)(4,1)} %bitcast.81), calls=%async_computation.10 | async-start | bytes 8388608
  101.9 9.5 %slice-start.2 = ((s8[10616832]{0:T(1024)(128)(4,1)}), s8[2228224]{0:T(1024)(128)(4,1)S(1)}, s32[]{:S(2)}) async-start(s8[10616832]{0:T(1024)(128)(4,1)} %bitcast.81), calls=%async_computation.11 | async-start | bytes 4456448
  122.8 2.6 copy-start.10
  123.0 1.1 copy-start.5
  123.0 2.4 copy-start.6
  123.0 32.6 %copy-start.9 = (f32[128,18]{1,0:T(8,128)S(1)}, f32[128,18]{1,0:T(8,128)}, u32[]{:S(2)}) copy-start(f32[128,18]{1,0:T(8,128)} %copy.36) | copy-start | bytes 27652
  127.9 0.7 copy-start.7
  158.3 132.1 %all-to-all-start.1 = ((f32[32,4,2048]{2,1,0:T(4,128)}), f32[32,4,2048]{2,1,0:T(4,128)S(1)}, u32[]{:S(2)}, u32[]{:S(2)}) async-start(f32[32,4,2048]{2,1,0:T(4,128)} %copy.38), calls=%async_computation.3 | async-start | bytes 2097152 | tf_op jit(solution)/shard_map/all_to_all | solution.py:114
  161.9 166.7 %reduce-scatter.3.cloned.1.call-start = ((), (), s32[]{:S(2)}) async-start(), calls=%async_computation.6 | async-start | bytes 1327104 | tf_op jit(solution)/shard_map/reduce_scatter | solution.py:73
  166.6 122.5 %copy-start.8 = (f32[256,128]{1,0:T(8,128)S(1)}, f32[256,128]{1,0:T(8,128)}, u32[]{:S(2)}) copy-start(f32[256,128]{1,0:T(8,128)} %param.15) | copy-start | bytes 393220
Sparse Core Ops, SparseCore 0:
  9.6 26.8 all-gather.4
  38.1 50.3 all-gather.2
  91.9 62.7 reduce-scatter.4
  160.0 128.9 all-reduce.1
  292.7 35.8 reduce-scatter.2
where the time goes:
time: 341 us; the launch traced here: 335 us
  waiting for transfers between devices  220 us (65%)
  matrix products  66.2 us (19%)
  local copies, waits for them, and re-layouts  14.6 us (4%)
  between operations  14.5 us (4%)
  starting transfers between devices  11.5 us (3%)
  other arithmetic  8.23 us (2%)
    psum x1, waiting for transfers between devices, body(): pivot_density = lax.psum(pivot_term, ('pole', 'row', 'col'))  118 us
    dot_general x10, matrix products, matmul(): jnp.dot(left, right, precision=lax.Precision.HIGHEST, preferred_element_t...  37.8 us
    reduce_scatter x1, waiting for transfers between devices, body(): lax.psum_scatter(upper_term, ('pole', 'row'), scatter_dimension=0, tiled=...  33.8 us
    dot_general x4, matrix products, contract_last(): lax.dot_general(left, right, (((1,), (1,)), ((), ())), precision=lax.Prec...  27.4 us
    reduce_scatter x1, waiting for transfers between devices, body(): lax.psum_scatter(lower_term, ('pole', 'col'), scatter_dimension=0, tiled=...  26.1 us
    all_gather x1, waiting for transfers between devices, body(): fragment = lax.all_gather(upper_factor, 'col', axis=2, tiled=True)  24 us
    all_gather x1, waiting for transfers between devices, body(): fragment = lax.all_gather(lower_factor, 'row', axis=2, tiled=True)  16.7 us
    all_to_all x1, starting transfers between devices, body(): lax.all_to_all(send_ids.reshape(devices_all, capacity), ('pole', 'row', '...  7.3 us
  transfers between devices with their start and end apart: 7, of which 5 were waited for; matrix products, arithmetic and copies ran while one was open for 26% of the time, Pallas kernels for 0%

commit v1 on v0

v1 whole, which is shorter than its diff:
```python
import jax
import jax.numpy as jnp
from jax import lax
from jax.sharding import PartitionSpec as P

BLOCKS = 18
HIGH = lax.Precision.HIGH


def dot(left, right, contract):
    return lax.dot_general(
        left, right, (contract, ((), ())), precision=HIGH, preferred_element_type=jnp.float32
    )


def permute(x, axis, pairs):
    return lax.ppermute(x, axis, pairs)


def swap(x, axis, mask):
    return lax.ppermute(x, axis, [(i, i ^ mask) for i in range(lax.axis_size(axis))])


def shift(x, axis, by):
    n = lax.axis_size(axis)
    return lax.ppermute(x, axis, [(i, (i + by) % n) for i in range(n)])


def gather_swapped(x, axis):
    n = lax.axis_size(axis)
    held = {0: x}
    bit = n // 2
    while bit:
        held.update({d ^ bit: swap(held[d], axis, bit) for d in list(held)})
        bit //= 2
    return [held[d] for d in range(n)]


def gather_cyclic(x, axis):
    n = lax.axis_size(axis)
    if n != 4:
        return [x] + [shift(x, axis, -p) for p in range(1, n)]
    one, three = shift(x, axis, -1), shift(x, axis, 1)
    leftward = permute(one, axis, [(2, 1), (1, 0)])
    rightward = permute(three, axis, [(1, 2), (2, 3)])
    two = jnp.where(lax.axis_index(axis) < 2, leftward, rightward)
    return [x, one, two, three]


def reduce_scatter_swapped(x, axis, masks):
    total = x[0]
    for term, mask in zip(x[1:], masks, strict=True):
        total = total + swap(term, axis, mask)
    return total


def pick(x, at):
    return lax.dynamic_index_in_dim(x, at, 0, keepdims=False)


def scatter_line(x, axis):
    n = lax.axis_size(axis)
    me = lax.axis_index(axis)
    total = pick(x, me)
    for way in (1, -1):
        arrived = None
        for step in range(1, n):
            at = jnp.mod(me + way * (n - step), n)
            out = pick(x, at)
            if arrived is not None:
                out = out + arrived
            if way > 0:
                pairs = [(i, i + 1) for i in range(step) if i + 1 < n]
            else:
                pairs = [(n - 1 - i, n - 2 - i) for i in range(step) if n - 2 - i >= 0]
            arrived = permute(out, axis, pairs)
        total = total + arrived
    return total


def scatter_swapped(x, axis):
    n = lax.axis_size(axis)
    me = lax.axis_index(axis)
    return reduce_scatter_swapped(
        [pick(x, me ^ d) for d in range(n)], axis, list(range(1, n))
    )


def gather_all(x, axes):
    n = 1
    for axis in axes:
        n *= lax.axis_size(axis)
    spread = jnp.broadcast_to(x[None], (n,) + x.shape)
    return lax.all_to_all(spread, axes, split_axis=0, concat_axis=0, tiled=True)


def body(
    inverse_tile,
    lower_factor,
    upper_factor,
    pivot_inverse,
    pole_weights,
    block_owners,
    basis_ancestor,
    basis_super,
):
    n_pole, n_row, n_col = (lax.axis_size(a) for a in ("pole", "row", "col"))
    pole, row, col = (lax.axis_index(a) for a in ("pole", "row", "col"))
    devices_all = n_pole * n_row * n_col
    weight_re, weight_im = pole_weights[0, 0], pole_weights[0, 1]
    tile_rows, tile_cols = inverse_tile.shape[2:]
    width = basis_super.shape[0]
    piece = lower_factor.shape[2]
    top = block_owners.shape[1]
    capacity = max(2, (BLOCKS * top + devices_all - 1) // devices_all)
    rows_here = tile_rows // (n_pole * n_col)
    block_rows = rows_here // BLOCKS

    lower = gather_swapped(lower_factor[0], "row")
    upper = gather_cyclic(upper_factor[0], "col")

    me = (pole * n_row + row) * n_col + col
    groups = n_row * n_pole * n_col
    hit = jnp.any(block_owners == me, axis=1).reshape(groups, BLOCKS).astype(jnp.int32)
    rank = jnp.cumsum(hit, 1) - hit
    slots = jnp.arange(capacity, dtype=jnp.int32)
    chosen = (rank[:, None, :] == slots[None, :, None]) & (hit[:, None, :] > 0)
    ids = jnp.arange(groups * BLOCKS, dtype=jnp.int32).reshape(groups, 1, BLOCKS)
    slot_ids = jnp.sum(jnp.where(chosen, ids, 0), 2)
    slot_used = jnp.any(chosen, 2)

    def by_device(x):
        x = x.reshape(n_row, n_pole, n_col, capacity)
        return x.transpose(1, 0, 2, 3).reshape(-1)

    slot_ids, slot_used = by_device(slot_ids), by_device(slot_used)
    points = basis_ancestor.shape[1]
    ancestor = jnp.take(
        basis_ancestor.reshape(groups * BLOCKS, block_rows * points), slot_ids, axis=0
    )
    ancestor = jnp.where(slot_used[:, None], ancestor, 0.0).reshape(-1, points)
    position = (row * n_pole + pole) * n_col + col
    owners_here = lax.dynamic_slice_in_dim(block_owners, position * BLOCKS, BLOCKS, 0)
    owned = jnp.any(
        owners_here[:, :, None] == jnp.arange(devices_all, dtype=jnp.int32)[None, None, :], 1
    ).astype(jnp.int32)
    rank_here = jnp.cumsum(owned, 0) - owned
    selector = (
        (owned[:, :, None] > 0) & (rank_here[:, :, None] == slots[None, None, :])
    ).astype(jnp.float32).reshape(BLOCKS, devices_all * capacity)

    tile_re, tile_im = inverse_tile[0, 0], inverse_tile[0, 1]
    lower_re = jnp.concatenate([block[0] for block in lower], 0)
    lower_im = jnp.concatenate([block[1] for block in lower], 0)
    scaled_re = weight_re * lower_re - weight_im * lower_im
    scaled_im = weight_re * lower_im + weight_im * lower_re
    last = ((1,), (1,))
    imag = dot(tile_re, scaled_im, last) + dot(tile_im, scaled_re, last)
    terms = imag.reshape(n_pole, tile_rows // n_pole, width)
    half = scatter_swapped(terms, "pole")
    rows = -scatter_line(half.reshape(n_col, rows_here, width), "col")
    real = dot(tile_re, scaled_re, last) - dot(tile_im, scaled_im, last)

    def ordered(x):
        x = x.reshape(x.shape[0], n_row, piece)
        return jnp.concatenate([pick(x.transpose(1, 0, 2), row ^ d) for d in range(n_row)], 1)

    rows = ordered(rows)
    sent = lax.dot_general(
        selector,
        rows.reshape(BLOCKS, block_rows * width),
        (((0,), (0,)), ((), ())),
        precision=lax.Precision.HIGHEST,
        preferred_element_type=jnp.float32,
    )
    received = lax.all_to_all(
        sent.reshape(devices_all, capacity, block_rows, width),
        ("pole", "row", "col"),
        split_axis=0,
        concat_axis=0,
        tiled=True,
    ).reshape(-1, width)

    upper_re = jnp.concatenate([block[0] for block in upper], 0)
    upper_im = jnp.concatenate([block[1] for block in upper], 0)
    both = jnp.concatenate(
        [
            weight_re * upper_im + weight_im * upper_re,
            weight_re * upper_re - weight_im * upper_im,
        ],
        1,
    )
    product = dot(both, inverse_tile.reshape(2 * tile_rows, tile_cols), ((1,), (0,)))
    out_rows = width // (n_pole * n_row)
    n_far = n_row // 2
    product = product.reshape(n_col, width // n_col, tile_cols)
    product = jnp.concatenate([pick(product, jnp.mod(k - col, n_col)) for k in range(n_col)], 0)
    product = product.reshape(n_pole * n_far, 2, out_rows, tile_cols).transpose(1, 0, 2, 3)
    low, far = row % 2, row // 2
    near = pick(product, low) + swap(pick(product, 1 - low), "row", 1)
    near = near.reshape(n_pole, n_far, out_rows, tile_cols)
    cut = out_rows // 2
    first, second = near[:, :, :cut], near[:, :, cut:]

    def over_far(x):
        return reduce_scatter_swapped(
            [pick(x, far ^ d) for d in range(n_far)], "row", [2 * d for d in range(1, n_far)]
        )

    first = scatter_swapped(over_far(first.transpose(1, 0, 2, 3)), "pole")
    second = over_far(scatter_swapped(second, "pole"))
    upper_density = -jnp.concatenate([first, second], 0)

    pivot = dot(upper_re, imag, ((1,), (0,))) + dot(upper_im, real, ((1,), (0,)))
    pivot = pivot.reshape(n_col, width // n_col, width)
    pivot = jnp.concatenate([pick(pivot, jnp.mod(k - col, n_col)) for k in range(n_col)], 0)
    pivot = ordered(pivot)
    pivot_piece = weight_re * pivot_inverse[0, 1] + weight_im * pivot_inverse[0, 0]
    placed = lax.dynamic_update_slice(
        jnp.zeros_like(pivot),
        pivot_piece,
        (row * pivot_piece.shape[0], col * pivot_piece.shape[1]),
    )
    pivot = pivot + placed
    pivot = lax.all_to_all(
        pivot.reshape(n_pole * n_row, out_rows, width),
        ("pole", "row"),
        split_axis=0,
        concat_axis=0,
        tiled=True,
    )
    pivot = jnp.sum(pivot, 0)
    pivot = pivot + sum(shift(pivot, "col", d) for d in range(1, n_col))
    pivot = gather_all(pivot, ("pole", "row")).reshape(width, width)

    projected = dot(received, basis_super, ((1,), (0,)))
    charge = jnp.sum(ancestor * projected, 0)
    charge = charge + jnp.sum(basis_super * dot(pivot, basis_super, ((1,), (0,))), 0)
    return (upper_density, charge)


def solution(mesh):
    placed = (
        P("pole", None, "row", "col"),
        P("pole", None, "row", "col"),
        P("pole", None, "col", "row"),
        P("pole", None, "row", "col"),
        P("pole", None),
        P(),
        P(None, ("pole", "row", "col")),
        P(None, ("pole", "row", "col")),
    )
    return jax.shard_map(
        body,
        mesh=mesh,
        in_specs=placed,
        out_specs=(P(("pole", "row"), "col"), P(("pole", "row", "col"))),
        check_vma=False,
    )
```

time: 341 us -> 179 us (0.52)
  waiting for transfers between devices: 220 us -> 46.2 us
  starting transfers between devices: 11.5 us -> 50 us
  matrix products: 66.2 us -> 33.1 us
  local copies, waits for them, and re-layouts: 14.6 us -> 29.6 us
  between operations: 14.5 us -> 1.47 us
  other arithmetic: 8.23 us -> 16 us
    psum x1 -> x0, waiting for transfers between devices: 118 us -> none  [body(): pivot_density = lax.psum(pivot_term, ('pole', 'row', 'col'))]
    reduce_scatter x2 -> x0, waiting for transfers between devices: 59.8 us -> none  [the longest x1 33.8 us: body(): lax.psum_scatter(upper_term, ('pole', 'row'), scatter_dimension=0, tiled=...]
    all_gather x2 -> x0, waiting for transfers between devices: 40.7 us -> none  [the longest x1 24 us: body(): fragment = lax.all_gather(upper_factor, 'col', axis=2, tiled=True)]
    ppermute x0 -> x22, starting transfers between devices: none -> 38 us  [the longest x8 15.6 us: permute(): return lax.ppermute(x, axis, pairs)]
    dot_general x15 -> x10, matrix products: 66.2 us -> 33.1 us  [the longest x9 32.6 us: dot(): lax.dot_general(left, right, (contract, ((), ())), precision=HIGH, prefer...]
    ppermute x0 -> x22, waiting for transfers between devices: none -> 32 us  [the longest x5 13.8 us: shift(): return lax.ppermute(x, axis, [(i, (i + by) % n) for i in range(n)])]
    all_to_all x2 -> x3, waiting for transfers between devices: 0.01 us -> 14.2 us  [the longest x1 13.9 us: body(): lax.all_to_all(sent.reshape(devices_all, capacity, block_rows, width), ('...]
    squeeze x0 -> x16, local copies, waits for them, and re-layouts: none -> 9.82 us  [the longest x8 3.99 us: pick(): return lax.dynamic_index_in_dim(x, at, 0, keepdims=False)]
  transfers between devices with their start and end apart: 7 -> 25, of which waited for: 5 -> 11; matrix products, arithmetic and copies ran while one was open for 26% -> 31% of each run, Pallas kernels for 0% -> 0%
where the time goes in v1:
time: 179 us; the launch traced here: 176 us
  starting transfers between devices  50 us (28%)
  waiting for transfers between devices  46.2 us (26%)
  matrix products  33.1 us (18%)
  local copies, waits for them, and re-layouts  29.6 us (17%)
  other arithmetic  16 us (9%)
    dot_general x9, matrix products, dot(): lax.dot_general(left, right, (contract, ((), ())), precision=HIGH, prefer...  32.6 us
    ppermute x8, starting transfers between devices, permute(): return lax.ppermute(x, axis, pairs)  15.6 us
    all_to_all x1, waiting for transfers between devices, body(): lax.all_to_all(sent.reshape(devices_all, capacity, block_rows, width), ('...  13.9 us
    ppermute x5, waiting for transfers between devices, shift(): return lax.ppermute(x, axis, [(i, (i + by) % n) for i in range(n)])  13.8 us
    ppermute x9, starting transfers between devices, swap(): lax.ppermute(x, axis, [(i, i ^ mask) for i in range(lax.axis_size(axis))])  12.9 us
    ppermute x8, waiting for transfers between devices, permute(): return lax.ppermute(x, axis, pairs)  11.2 us
    ppermute x5, starting transfers between devices, shift(): return lax.ppermute(x, axis, [(i, (i + by) % n) for i in range(n)])  9.5 us
    ppermute x9, waiting for transfers between devices, swap(): lax.ppermute(x, axis, [(i, i ^ mask) for i in range(lax.axis_size(axis))])  6.97 us
  transfers between devices with their start and end apart: 25, of which 11 were waited for; matrix products, arithmetic and copies ran while one was open for 31% of the time, Pallas kernels for 0%

profile of v1, /device:TPU:0, one launch (start us, length us, event | category | flops | bytes accessed | tf_op | source)
XLA Modules:
  0.0 176.4 jit_solution(9664586118186936770)
XLA Ops:
  0.6 3.0 %collective-permute-start.10 = (f32[2,64,1152]{2,1,0:T(8,128)}, f32[2,64,1152]{2,1,0:T(8,128)}, u32[]{:S(2)}, u32[]{:S(2)}) collective-permute-start(f32[2,64,1152]{2,1,0:T(8,128)} %bitcast.179), channel_id=1, source_target_pairs={{0,8},{4,12},{8,0},{12,4},{1,9},{5,13},{9,1},{13,5},{2,10},{6,14},... | collective-permute-start | bytes 1769480 | tf_op jit(solution)/shard_map/ppermute | solution.py:21
  5.2 2.2 %collective-permute-start = (f32[2,64,1152]{2,1,0:T(8,128)}, f32[2,64,1152]{2,1,0:T(8,128)}, u32[]{:S(2)}, u32[]{:S(2)}) collective-permute-start(f32[2,64,1152]{2,1,0:T(8,128)} %bitcast.178), channel_id=1, source_target_pairs={{0,3},{1,0},{2,1},{3,2},{4,7},{5,4},{6,5},{7,6},{8,11},{9,8},{10,9... | collective-permute-start | bytes 1769480 | tf_op jit(solution)/shard_map/ppermute | solution.py:26
  14.2 3.4 %reshape.232 = f32[576,1024]{1,0:T(8,128)} reshape(f32[4608,128]{1,0:T(8,128)} %param.14) | data formatting | bytes 4718592 | tf_op jit(solution)/shard_map/reshape | solution.py:139
  23.7 9.9 %collective-permute-done = f32[2,64,1152]{2,1,0:T(8,128)} collective-permute-done((f32[2,64,1152]{2,1,0:T(8,128)}, f32[2,64,1152]{2,1,0:T(8,128)}, u32[]{:S(2)}, u32[]{:S(2)}) %collective-permute-start) | collective-permute-done | bytes 589856 | tf_op jit(solution)/shard_map/ppermute | solution.py:26
  37.4 7.0 %fusion = f32[256,1152]{1,0:T(8,128)S(1)} fusion(f32[1,2,1152,1152]{3,2,1,0:T(8,128)} %param.8, f32[64,1152]{1,0:T(8,128)S(1)} %get-tuple-element.19, f32[64,1152]{1,0:T(8,128)S(1)} %get-tuple-element.17, f32[64,1152]{1,0:T(8,128)S(1)} %get-tuple-element.15, f32[64,1152]{1,0:T(8,128)S(1)} %get-tuple-element.13, f32[64,1152]{1,0:T(8,128)S(1)} %get-tuple-element.18, ...), kind=kOutput, calls=%fused_computation.1 | convolution fusion | flops 2041085952 | bytes 8848384 | tf_op jit(solution)/shard_map/dot_general | solution.py:11
  44.5 4.3 %fusion.2 = f32[256,1152]{1,0:T(8,128)S(1)} fusion(f32[1,2,1152,1152]{3,2,1,0:T(8,128)S(1)} %bitcast.158, f32[64,1152]{1,0:T(8,128)S(1)} %get-tuple-element.19, f32[64,1152]{1,0:T(8,128)S(1)} %get-tuple-element.17, f32[64,1152]{1,0:T(8,128)S(1)} %get-tuple-element.15, f32[64,1152]{1,0:T(8,128)S(1)} %get-tuple-element.13, ...), kind=kOutput, calls=%fused_computation.3 | convolution fusion | flops 2041085952 | bytes 8847368 | tf_op jit(solution)/shard_map/dot_general | solution.py:11
  48.8 2.8 %collective-permute-done.1 = f32[2,64,1152]{2,1,0:T(8,128)S(1)} collective-permute-done((f32[2,64,1152]{2,1,0:T(8,128)}, f32[2,64,1152]{2,1,0:T(8,128)S(1)}, u32[]{:S(2)}, u32[]{:S(2)}) %collective-permute-start.1) | collective-permute-done | bytes 589856 | tf_op jit(solution)/shard_map/ppermute | solution.py:17
  51.7 4.3 %fusion.15 = f32[256,1152]{1,0:T(8,128)S(1)} fusion(f32[256,1152]{1,0:T(8,128)S(1)} %fusion, f32[1,2,1152,1152]{3,2,1,0:T(8,128)S(1)} %bitcast.158, f32[64,1152]{1,0:T(8,128)S(1)} %get-tuple-element.19, f32[64,1152]{1,0:T(8,128)S(1)} %get-tuple-element.17, f32[64,1152]{1,0:T(8,128)S(1)} %get-tuple-element.15, f32[64,1152]{1,0:T(8,128)S(1)} %get-tuple-element.13, ...), kind=kOutput, calls=%fused_computation.14 | convolution fusion | flops 2041380864 | bytes 10027016 | tf_op jit(solution)/shard_map/dot_general | solution.py:11
  56.0 5.5 %fusion.12 = f32[256,1152]{1,0:T(8,128)S(1)} fusion(f32[256,1152]{1,0:T(8,128)S(1)} %fusion.2, f32[1,2,1152,1152]{3,2,1,0:T(8,128)S(1)} %bitcast.158, f32[64,1152]{1,0:T(8,128)S(1)} %get-tuple-element.19, f32[64,1152]{1,0:T(8,128)S(1)} %get-tuple-element.17, f32[64,1152]{1,0:T(8,128)S(1)} %get-tuple-element.15, f32[64,1152]{1,0:T(8,128)} %copy-done.2, ...), kind=kOutput, calls=%fused_computation.13 | convolution fusion | flops 2041380864 | bytes 10027016 | tf_op jit(solution)/shard_map/dot_general | solution.py:11
  62.4 2.6 %multiply_add_fusion.1 = (f32[256,1152]{1,0:T(8,128)S(1)}, f32[256,1152]{1,0:T(8,128)}) fusion(f32[]{:T(128)} %bitcast.6, f32[]{:T(128)} %bitcast, f32[64,1152]{1,0:T(8,128)S(1)} %get-tuple-element.29, f32[64,1152]{1,0:T(8,128)S(1)} %get-tuple-element.27, f32[64,1152]{1,0:T(8,128)S(1)} %get-tuple-element.25, f32[64,1152]{1,0:T(8,128)S(1)} %get-tuple-element.23, ...), kind=kLoop, calls=%fused_computation.28 | loop fusion | flops 3538944 | bytes 4718600 | tf_op jit(solution)/shard_map/add | solution.py:188
  71.1 2.8 %add.341 = f32[256,256]{1,0:T(8,128)} dynamic-update-slice(f32[256,256]{1,0:T(8,128)} %copy-done.6, f32[64,64]{1,0:T(8,128)} %bitcast_add_fusion.11, s32[]{:T(128)S(6)} %select_n.233, s32[]{:T(128)S(6)} %select_n.234) | dynamic-update-slice | bytes 32772 | tf_op jit(solution)/shard_map/add | solution.py:224
  73.9 4.0 %all-to-all-start.1 = ((f32[8,32,256]{2,1,0:T(8,128)}), f32[8,32,256]{2,1,0:T(8,128)}, u32[]{:S(2)}, u32[]{:S(2)}) async-start(f32[8,32,256]{2,1,0:T(8,128)} %bitcast.173), calls=%async_computation.1 | async-start | bytes 524288 | tf_op jit(solution)/shard_map/all_to_all | solution.py:225
  80.7 8.0 %fusion.18 = f32[4,64,1152]{2,1,0:T(8,128)S(1)} fusion(f32[2304,1152,1]{1,0,2:T(8,128)} %bitcast.156, f32[4,64,1152]{2,1,0:T(8,128)S(1)} %bitcast.161, f32[4,64,1152]{2,1,0:T(8,128)S(1)} %bitcast.160), kind=kOutput, calls=%fused_computation.15 | convolution fusion | flops 4077453312 | bytes 14155776 | tf_op jit(solution)/shard_map/dot_general | solution.py:11
  92.3 3.5 %collective-permute-start.20 = (f32[32,256]{1,0:T(8,128)}, f32[32,256]{1,0:T(8,128)S(1)}, u32[]{:S(2)}, u32[]{:S(2)}) collective-permute-start(f32[32,256]{1,0:T(8,128)} %reduce_sum.38), channel_id=1, source_target_pairs={{0,2},{1,3},{2,0},{3,1},{4,6},{5,7},{6,4},{7,5},{8,10},{9,11},{10,... | collective-permute-start | bytes 98312 | tf_op jit(solution)/shard_map/ppermute | solution.py:26
  97.1 2.5 %pad_maximum_fusion.2 = f32[256,1152]{1,0:T(8,128)} fusion(f32[64,1152]{1,0:T(8,128)} %get-tuple-element.5, f32[64,1152]{1,0:T(8,128)} %get-tuple-element.6, f32[64,1152]{1,0:T(8,128)} %get-tuple-element.7, f32[64,1152]{1,0:T(8,128)} %get-tuple-element.4), kind=kLoop, calls=%fused_computation.22 | loop fusion | flops 884736 | bytes 2359296 | tf_op jit(solution)/shard_map/concatenate | solution.py:197
  99.5 2.1 %collective-permute-done.19 = f32[32,256]{1,0:T(8,128)S(1)} collective-permute-done((f32[32,256]{1,0:T(8,128)}, f32[32,256]{1,0:T(8,128)S(1)}, u32[]{:S(2)}, u32[]{:S(2)}) %collective-permute-start.19) | collective-permute-done | bytes 32800 | tf_op jit(solution)/shard_map/ppermute | solution.py:26
  103.2 4.0 %all-to-all-start.2 = ((f32[8,32,256]{2,1,0:T(8,128)}), f32[8,32,256]{2,1,0:T(8,128)}, u32[]{:S(2)}, u32[]{:S(2)}) async-start(f32[8,32,256]{2,1,0:T(8,128)} %broadcast_in_dim.70), calls=%async_computation.2 | async-start | bytes 524288 | tf_op jit(solution)/shard_map/all_to_all | solution.py:94
  120.7 4.4 %collective-permute-start.14 = (f32[144,256]{1,0:T(8,128)S(1)}, f32[144,256]{1,0:T(8,128)S(1)}, u32[]{:S(2)}, u32[]{:S(2)}) collective-permute-start(f32[144,256]{1,0:T(8,128)S(1)} %bitcast_add_fusion.4), channel_id=1, source_target_pairs={{0,1},{1,2},{4,5},{5,6},{8,9},{9,10},{12,13},{13,14},{16,17},{17,1... | collective-permute-start | bytes 442376 | tf_op jit(solution)/shard_map/ppermute | solution.py:17
  128.5 2.2 %collective-permute-start.5 = (f32[2,16,1152]{2,1,0:T(8,128)S(1)}, f32[2,16,1152]{2,1,0:T(8,128)S(1)}, u32[]{:S(2)}, u32[]{:S(2)}) collective-permute-start(f32[2,16,1152]{2,1,0:T(8,128)S(1)} %dynamic-slice_bitcast_fusion.9), channel_id=1, source_target_pairs={{0,8},{4,12},{8,0},{12,4},{1,9},{5,13},{9,1},{13,5},{2,10},{6,14},... | collective-permute-start | bytes 442376 | tf_op jit(solution)/shard_map/ppermute | solution.py:21
  130.7 5.0 %collective-permute-start.15 = (f32[144,256]{1,0:T(8,128)S(1)}, f32[144,256]{1,0:T(8,128)S(1)}, u32[]{:S(2)}, u32[]{:S(2)}) collective-permute-start(f32[144,256]{1,0:T(8,128)S(1)} %get-tuple-element.8), channel_id=1, source_target_pairs={{0,1},{1,2},{2,3},{4,5},{5,6},{6,7},{8,9},{9,10},{10,11},{12,13},{... | collective-permute-start | bytes 442376 | tf_op jit(solution)/shard_map/ppermute | solution.py:17
  138.4 5.1 %collective-permute-done.18 = f32[144,256]{1,0:T(8,128)S(1)} collective-permute-done((f32[144,256]{1,0:T(8,128)S(1)}, f32[144,256]{1,0:T(8,128)S(1)}, u32[]{:S(2)}, u32[]{:S(2)}) %collective-permute-start.18) | collective-permute-done | bytes 147488 | tf_op jit(solution)/shard_map/ppermute | solution.py:17
  146.3 3.9 %all-to-all-start = ((f32[32,4,8,256]{3,2,1,0:T(8,128)}), f32[32,4,8,256]{3,2,1,0:T(8,128)S(1)}, u32[]{:S(2)}, u32[]{:S(2)}) async-start(f32[32,4,8,256]{3,2,1,0:T(8,128)} %copy.56), calls=%async_computation | async-start | bytes 2097152 | tf_op jit(solution)/shard_map/all_to_all | solution.py:176
  153.7 6.9 %collective-permute-done.8 = f32[16,1152]{1,0:T(8,128)S(1)} collective-permute-done((f32[16,1152]{1,0:T(8,128)S(1)}, f32[16,1152]{1,0:T(8,128)S(1)}, u32[]{:S(2)}, u32[]{:S(2)}) %collective-permute-start.8) | collective-permute-done | bytes 73760 | tf_op jit(solution)/shard_map/ppermute | solution.py:21
  161.3 13.9 %all-to-all-done = f32[32,4,8,256]{3,2,1,0:T(8,128)S(1)} async-done(((f32[32,4,8,256]{3,2,1,0:T(8,128)}), f32[32,4,8,256]{3,2,1,0:T(8,128)S(1)}, u32[]{:S(2)}, u32[]{:S(2)}) %all-to-all-start) | async-done | bytes 1048608 | tf_op jit(solution)/shard_map/all_to_all | solution.py:176
  (169 shorter events, 61.5 us)
Async XLA Ops:
  0.6 18.3 %collective-permute-start.10 = (f32[2,64,1152]{2,1,0:T(8,128)}, f32[2,64,1152]{2,1,0:T(8,128)}, u32[]{:S(2)}, u32[]{:S(2)}) collective-permute-start(f32[2,64,1152]{2,1,0:T(8,128)} %bitcast.179), channel_id=1, source_target_pairs={{0,8},{4,12},{8,0},{12,4},{1,9},{5,13},{9,1},{13,5},{2,10},{6,14},... | collective-permute-start | bytes 1769480 | tf_op jit(solution)/shard_map/ppermute | solution.py:21
  3.7 32.6 %collective-permute-start.9 = (f32[2,64,1152]{2,1,0:T(8,128)}, f32[2,64,1152]{2,1,0:T(8,128)}, u32[]{:S(2)}, u32[]{:S(2)}) collective-permute-start(f32[2,64,1152]{2,1,0:T(8,128)} %bitcast.180), channel_id=1, source_target_pairs={{0,4},{4,0},{8,12},{12,8},{1,5},{5,1},{9,13},{13,9},{2,6},{6,2},{1... | collective-permute-start | bytes 1769480 | tf_op jit(solution)/shard_map/ppermute | solution.py:21
  3.7 18.3 %collective-permute-start.2 = (f32[2,64,1152]{2,1,0:T(8,128)}, f32[2,64,1152]{2,1,0:T(8,128)}, u32[]{:S(2)}, u32[]{:S(2)}) collective-permute-start(f32[2,64,1152]{2,1,0:T(8,128)} %bitcast.177), channel_id=1, source_target_pairs={{0,1},{1,2},{2,3},{3,0},{4,5},{5,6},{6,7},{7,4},{8,9},{9,10},{10,1... | collective-permute-start | bytes 1769480 | tf_op jit(solution)/shard_map/ppermute | solution.py:26
  5.2 28.4 %collective-permute-start = (f32[2,64,1152]{2,1,0:T(8,128)}, f32[2,64,1152]{2,1,0:T(8,128)}, u32[]{:S(2)}, u32[]{:S(2)}) collective-permute-start(f32[2,64,1152]{2,1,0:T(8,128)} %bitcast.178), channel_id=1, source_target_pairs={{0,3},{1,0},{2,1},{3,2},{4,7},{5,4},{6,5},{7,6},{8,11},{9,8},{10,9... | collective-permute-start | bytes 1769480 | tf_op jit(solution)/shard_map/ppermute | solution.py:26
  20.1 17.2 %collective-permute-start.11 = (f32[2,64,1152]{2,1,0:T(8,128)}, f32[2,64,1152]{2,1,0:T(8,128)S(1)}, u32[]{:S(2)}, u32[]{:S(2)}) collective-permute-start(f32[2,64,1152]{2,1,0:T(8,128)} %collective-permute-done.10), channel_id=1, source_target_pairs={{0,4},{4,0},{8,12},{12,8},{1,5},{5,1},{9,13},{13,9},{2,6},{6,2},{1... | collective-permute-start | bytes 1769480 | tf_op jit(solution)/shard_map/ppermute | solution.py:21
  23.0 25.7 %collective-permute-start.3 = (f32[2,64,1152]{2,1,0:T(8,128)}, f32[2,64,1152]{2,1,0:T(8,128)S(1)}, u32[]{:S(2)}, u32[]{:S(2)}) collective-permute-start(f32[2,64,1152]{2,1,0:T(8,128)} %collective-permute-done.2), channel_id=1, source_target_pairs={{1,2},{2,3},{5,6},{6,7},{9,10},{10,11},{13,14},{14,15},{17,18},{18... | collective-permute-start | bytes 1769480 | tf_op jit(solution)/shard_map/ppermute | solution.py:17
  34.8 16.8 %collective-permute-start.1 = (f32[2,64,1152]{2,1,0:T(8,128)}, f32[2,64,1152]{2,1,0:T(8,128)S(1)}, u32[]{:S(2)}, u32[]{:S(2)}) collective-permute-start(f32[2,64,1152]{2,1,0:T(8,128)} %collective-permute-done), channel_id=1, source_target_pairs={{2,1},{1,0},{6,5},{5,4},{10,9},{9,8},{14,13},{13,12},{18,17},{17,1... | collective-permute-start | bytes 1769480 | tf_op jit(solution)/shard_map/ppermute | solution.py:17
  73.9 15.9 %all-to-all-start.1 = ((f32[8,32,256]{2,1,0:T(8,128)}), f32[8,32,256]{2,1,0:T(8,128)}, u32[]{:S(2)}, u32[]{:S(2)}) async-start(f32[8,32,256]{2,1,0:T(8,128)} %bitcast.173), calls=%async_computation.1 | async-start | bytes 524288 | tf_op jit(solution)/shard_map/all_to_all | solution.py:225
  78.8 35.8 %collective-permute-start.12 = (f32[576,256]{1,0:T(8,128)}, f32[576,256]{1,0:T(8,128)}, u32[]{:S(2)}, u32[]{:S(2)}) collective-permute-start(f32[576,256]{1,0:T(8,128)} %dynamic-slice_bitcast_fusion), channel_id=1, source_target_pairs={{0,16},{16,0},{1,17},{17,1},{2,18},{18,2},{3,19},{19,3},{4,20},{20... | collective-permute-start | bytes 1769480 | tf_op jit(solution)/shard_map/ppermute | solution.py:21
  91.4 8.2 %collective-permute-start.21 = (f32[32,256]{1,0:T(8,128)}, f32[32,256]{1,0:T(8,128)S(1)}, u32[]{:S(2)}, u32[]{:S(2)}) collective-permute-start(f32[32,256]{1,0:T(8,128)} %reduce_sum.38), channel_id=1, source_target_pairs={{0,3},{1,0},{2,1},{3,2},{4,7},{5,4},{6,5},{7,6},{8,11},{9,8},{10,9... | collective-permute-start | bytes 98312 | tf_op jit(solution)/shard_map/ppermute | solution.py:26
  92.3 7.2 %collective-permute-start.20 = (f32[32,256]{1,0:T(8,128)}, f32[32,256]{1,0:T(8,128)S(1)}, u32[]{:S(2)}, u32[]{:S(2)}) collective-permute-start(f32[32,256]{1,0:T(8,128)} %reduce_sum.38), channel_id=1, source_target_pairs={{0,2},{1,3},{2,0},{3,1},{4,6},{5,7},{6,4},{7,5},{8,10},{9,11},{10,... | collective-permute-start | bytes 98312 | tf_op jit(solution)/shard_map/ppermute | solution.py:26
  95.8 5.9 %collective-permute-start.19 = (f32[32,256]{1,0:T(8,128)}, f32[32,256]{1,0:T(8,128)S(1)}, u32[]{:S(2)}, u32[]{:S(2)}) collective-permute-start(f32[32,256]{1,0:T(8,128)} %reduce_sum.38), channel_id=1, source_target_pairs={{0,1},{1,2},{2,3},{3,0},{4,5},{5,6},{6,7},{7,4},{8,9},{9,10},{10,1... | collective-permute-start | bytes 98312 | tf_op jit(solution)/shard_map/ppermute | solution.py:26
  103.2 10.1 %all-to-all-start.2 = ((f32[8,32,256]{2,1,0:T(8,128)}), f32[8,32,256]{2,1,0:T(8,128)}, u32[]{:S(2)}, u32[]{:S(2)}) async-start(f32[8,32,256]{2,1,0:T(8,128)} %broadcast_in_dim.70), calls=%async_computation.2 | async-start | bytes 524288 | tf_op jit(solution)/shard_map/all_to_all | solution.py:94
  109.2 8.8 %collective-permute-start.4 = (f32[4,32,1152]{2,1,0:T(8,128)}, f32[4,32,1152]{2,1,0:T(8,128)}, u32[]{:S(2)}, u32[]{:S(2)}) collective-permute-start(f32[4,32,1152]{2,1,0:T(8,128)} %dynamic-slice_bitcast_fusion.1), channel_id=1, source_target_pairs={{0,4},{4,0},{8,12},{12,8},{1,5},{5,1},{9,13},{13,9},{2,6},{6,2},{1... | collective-permute-start | bytes 1769480 | tf_op jit(solution)/shard_map/ppermute | solution.py:21
  117.3 9.7 %collective-permute-start.16 = (f32[144,256]{1,0:T(8,128)S(1)}, f32[144,256]{1,0:T(8,128)S(1)}, u32[]{:S(2)}, u32[]{:S(2)}) collective-permute-start(f32[144,256]{1,0:T(8,128)S(1)} %get-tuple-element.11), channel_id=1, source_target_pairs={{3,2},{7,6},{11,10},{15,14},{19,18},{23,22},{27,26},{31,30}} | collective-permute-start | bytes 442376 | tf_op jit(solution)/shard_map/ppermute | solution.py:17
  120.7 7.1 %collective-permute-start.14 = (f32[144,256]{1,0:T(8,128)S(1)}, f32[144,256]{1,0:T(8,128)S(1)}, u32[]{:S(2)}, u32[]{:S(2)}) collective-permute-start(f32[144,256]{1,0:T(8,128)S(1)} %bitcast_add_fusion.4), channel_id=1, source_target_pairs={{0,1},{1,2},{4,5},{5,6},{8,9},{9,10},{12,13},{13,14},{16,17},{17,1... | collective-permute-start | bytes 442376 | tf_op jit(solution)/shard_map/ppermute | solution.py:17
  125.1 11.9 %collective-permute-start.7 = (f32[2,16,1152]{2,1,0:T(8,128)S(1)}, f32[2,16,1152]{2,1,0:T(8,128)S(1)}, u32[]{:S(2)}, u32[]{:S(2)}) collective-permute-start(f32[2,16,1152]{2,1,0:T(8,128)S(1)} %dynamic-slice_bitcast_fusion.8), channel_id=1, source_target_pairs={{0,16},{16,0},{1,17},{17,1},{2,18},{18,2},{3,19},{19,3},{4,20},{20... | collective-permute-start | bytes 442376 | tf_op jit(solution)/shard_map/ppermute | solution.py:21
  127.8 7.9 %collective-permute-start.17 = (f32[144,256]{1,0:T(8,128)S(1)}, f32[144,256]{1,0:T(8,128)S(1)}, u32[]{:S(2)}, u32[]{:S(2)}) collective-permute-start(f32[144,256]{1,0:T(8,128)S(1)} %get-tuple-element.9), channel_id=1, source_target_pairs={{3,2},{2,1},{7,6},{6,5},{11,10},{10,9},{15,14},{14,13},{19,18},{18... | collective-permute-start | bytes 442376 | tf_op jit(solution)/shard_map/ppermute | solution.py:17
  128.5 23.6 %collective-permute-start.5 = (f32[2,16,1152]{2,1,0:T(8,128)S(1)}, f32[2,16,1152]{2,1,0:T(8,128)S(1)}, u32[]{:S(2)}, u32[]{:S(2)}) collective-permute-start(f32[2,16,1152]{2,1,0:T(8,128)S(1)} %dynamic-slice_bitcast_fusion.9), channel_id=1, source_target_pairs={{0,8},{4,12},{8,0},{12,4},{1,9},{5,13},{9,1},{13,5},{2,10},{6,14},... | collective-permute-start | bytes 442376 | tf_op jit(solution)/shard_map/ppermute | solution.py:21
  130.7 7.7 %collective-permute-start.15 = (f32[144,256]{1,0:T(8,128)S(1)}, f32[144,256]{1,0:T(8,128)S(1)}, u32[]{:S(2)}, u32[]{:S(2)}) collective-permute-start(f32[144,256]{1,0:T(8,128)S(1)} %get-tuple-element.8), channel_id=1, source_target_pairs={{0,1},{1,2},{2,3},{4,5},{5,6},{6,7},{8,9},{9,10},{10,11},{12,13},{... | collective-permute-start | bytes 442376 | tf_op jit(solution)/shard_map/ppermute | solution.py:17
  135.7 7.7 %collective-permute-start.18 = (f32[144,256]{1,0:T(8,128)S(1)}, f32[144,256]{1,0:T(8,128)S(1)}, u32[]{:S(2)}, u32[]{:S(2)}) collective-permute-start(f32[144,256]{1,0:T(8,128)S(1)} %bitcast_add_fusion.3), channel_id=1, source_target_pairs={{3,2},{2,1},{1,0},{7,6},{6,5},{5,4},{11,10},{10,9},{9,8},{15,14},{... | collective-permute-start | bytes 442376 | tf_op jit(solution)/shard_map/ppermute | solution.py:17
  146.3 29.0 %all-to-all-start = ((f32[32,4,8,256]{3,2,1,0:T(8,128)}), f32[32,4,8,256]{3,2,1,0:T(8,128)S(1)}, u32[]{:S(2)}, u32[]{:S(2)}) async-start(f32[32,4,8,256]{3,2,1,0:T(8,128)} %copy.56), calls=%async_computation | async-start | bytes 2097152 | tf_op jit(solution)/shard_map/all_to_all | solution.py:176
  150.3 10.4 %collective-permute-start.8 = (f32[16,1152]{1,0:T(8,128)S(1)}, f32[16,1152]{1,0:T(8,128)S(1)}, u32[]{:S(2)}, u32[]{:S(2)}) collective-permute-start(f32[16,1152]{1,0:T(8,128)S(1)} %dynamic-slice_bitcast_fusion.10), channel_id=1, source_target_pairs={{0,8},{4,12},{8,0},{12,4},{1,9},{5,13},{9,1},{13,5},{2,10},{6,14},... | collective-permute-start | bytes 221192 | tf_op jit(solution)/shard_map/ppermute | solution.py:21
  152.1 8.5 %collective-permute-start.6 = (f32[16,1152]{1,0:T(8,128)S(1)}, f32[16,1152]{1,0:T(8,128)S(1)}, u32[]{:S(2)}, u32[]{:S(2)}) collective-permute-start(f32[16,1152]{1,0:T(8,128)S(1)} %dynamic-slice_bitcast_fusion.11), channel_id=1, source_target_pairs={{0,16},{16,0},{1,17},{17,1},{2,18},{18,2},{3,19},{19,3},{4,20},{20... | collective-permute-start | bytes 221192 | tf_op jit(solution)/shard_map/ppermute | solution.py:21
  (18 other events, 279.3 us)

commit v2 on v1

v2 whole, which is shorter than its diff:
```python
import jax
import jax.numpy as jnp
from jax import lax
from jax.experimental import pallas as pl
from jax.experimental.pallas import tpu as pltpu
from jax.sharding import PartitionSpec as P

BLOCKS = 18
HIGH = lax.Precision.HIGH
F32, BF16 = jnp.float32, jnp.bfloat16
LAST, INNER = ((1,), (1,)), ((1,), (0,))
SMEM = pl.BlockSpec(memory_space=pltpu.SMEM)
VMEM = pl.BlockSpec(memory_space=pltpu.VMEM)


def room(mebibytes):
    return pltpu.CompilerParams(vmem_limit_bytes=mebibytes * 2**20)


def halves(x):
    high = x.astype(BF16)
    return high, (x - high.astype(F32)).astype(BF16)


def product(left, right, contract):
    def one(a, b):
        return lax.dot_general(a, b, (contract, ((), ())), preferred_element_type=F32)

    return one(left[0], right[0]) + (one(left[0], right[1]) + one(left[1], right[0]))


QUICK = pl.CostEstimate(flops=0, bytes_accessed=0, transcendentals=0)


def fixed(shape):
    return pl.BlockSpec(shape, lambda i: (0,) * len(shape))


def lower_products(place, weights, tile, blocks, n_pole):
    _, _, rows, depth = tile.shape
    piece = blocks[0].shape[1]
    n_row = len(blocks)
    width = n_row * piece
    steps = 3
    chunk = rows // steps
    part = rows // n_pole

    def kernel(place, weights, tile, *refs):
        blocks, refs = refs[:n_row], refs[n_row:]
        outs, (out_h, out_l, right_h, right_l, whole) = refs[:n_pole], refs[n_pole:]
        step = pl.program_id(0)

        @pl.when(step == 0)
        def _():
            w_re, w_im = weights[0, 0], weights[0, 1]
            for d in range(n_row):
                re, im = blocks[d][0], blocks[d][1]
                re, im = w_re * re - w_im * im, w_re * im + w_im * re
                for side, pair in enumerate(((-im, -re), (re, -im))):
                    at = pl.multiple_of(side * width + (place[3] ^ d) * piece, 16)
                    for j, x in enumerate(pair):
                        cols = slice(j * depth, (j + 1) * depth)
                        right_h[pl.ds(at, piece), cols], right_l[pl.ds(at, piece), cols] = halves(x)

        left = halves(jnp.concatenate([tile[0, 0], tile[0, 1]], 1))
        out = product(left, (right_h[...], right_l[...]), LAST)
        out_h[...], out_l[...] = halves(out)
        whole[pl.ds(pl.multiple_of(step * chunk, 16), chunk), :] = out[:, :width]

        @pl.when(step == steps - 1)
        def _():
            for d in range(n_pole):
                at = pl.multiple_of((place[0] ^ d) * part, 8)
                outs[d][...] = whole[pl.ds(at, part), :]

    out = pl.pallas_call(
        kernel,
        grid=(steps,),
        in_specs=[SMEM, SMEM, pl.BlockSpec((1, 2, chunk, depth), lambda i: (0, 0, i, 0))]
        + [fixed(blocks[0].shape)] * n_row,
        out_specs=[fixed((part, width))] * n_pole + [pl.BlockSpec((chunk, 2 * width), lambda i: (i, 0))] * 2,
        out_shape=[jax.ShapeDtypeStruct((part, width), F32)] * n_pole
        + [jax.ShapeDtypeStruct((rows, 2 * width), BF16)] * 2,
        scratch_shapes=[pltpu.VMEM((2 * width, 2 * depth), BF16)] * 2 + [pltpu.VMEM((rows, width), F32)],
        compiler_params=room(58),
        cost_estimate=QUICK,
    )(place, weights, tile, *blocks)
    return out[:n_pole], out[n_pole:]


def pivot_term(place, weights, blocks, lower, pivot_inverse):
    rows = blocks[0].shape[0]
    n_col = len(blocks) // 2
    width = n_col * rows
    depth = lower[0].shape[0]
    piece_rows, piece_cols = pivot_inverse.shape[2:]

    def kernel(place, weights, *refs):
        blocks, (lower_h, lower_l, inverse, pivot, left_h, left_l) = refs[: 2 * n_col], refs[2 * n_col :]
        for p in range(n_col):
            at = pl.multiple_of(lax.rem(place[4] + p, n_col) * rows, 16)
            for j, x in enumerate((-blocks[2 * p][...], blocks[2 * p + 1][:, :depth])):
                at_j = slice(j * depth, (j + 1) * depth)
                left_h[pl.ds(at, rows), at_j], left_l[pl.ds(at, rows), at_j] = halves(x)
        right = [jnp.concatenate([x[:, :width], x[:, width:]], 0) for x in (lower_h, lower_l)]
        pivot[...] = product((left_h[...], left_l[...]), right, INNER)
        at = pl.multiple_of(place[3] * piece_rows, 8)
        own = weights[0, 0] * inverse[0, 1] + weights[0, 1] * inverse[0, 0]
        for k in range(n_col):

            @pl.when(place[4] == k)
            def _():
                pivot[pl.ds(at, piece_rows), k * piece_cols : (k + 1) * piece_cols] += own

    return pl.pallas_call(
        kernel,
        grid=(1,),
        in_specs=[SMEM, SMEM]
        + [fixed(x.shape) for x in blocks]
        + [fixed(lower[0].shape)] * 2
        + [fixed(pivot_inverse.shape)],
        out_specs=fixed((width, width)),
        out_shape=jax.ShapeDtypeStruct((width, width), F32),
        scratch_shapes=[pltpu.VMEM((width, 2 * depth), BF16)] * 2,
        compiler_params=room(58),
        cost_estimate=QUICK,
    )(place, weights, *blocks, *lower, pivot_inverse)


def upper_products(place, weights, tile, blocks):
    _, _, depth, cols = tile.shape
    rows = blocks[0].shape[0]
    n_col = len(blocks) // 2
    width = n_col * rows
    steps = 3
    chunk = depth // steps

    def kernel(place, weights, tile, *refs):
        blocks, refs = refs[: 2 * n_col], refs[2 * n_col :]
        upper, left_h, left_l = refs
        step = pl.program_id(0)
        w_re, w_im = weights[0, 0], weights[0, 1]

        def fill(combine):
            for p in range(n_col):
                at = pl.multiple_of(lax.rem(place[4] + p, n_col) * rows, 16)
                for j, x in enumerate(combine(blocks[2 * p][...], blocks[2 * p + 1][:, :depth])):
                    at_j = slice(j * depth, (j + 1) * depth)
                    left_h[pl.ds(at, rows), at_j], left_l[pl.ds(at, rows), at_j] = halves(x)

        @pl.when(step == 0)
        def _():
            fill(lambda re, im: (-(w_re * im + w_im * re), w_im * im - w_re * re))
            upper[...] = jnp.zeros_like(upper)

        right = halves(jnp.concatenate([tile[0, 0], tile[0, 1]], 0))
        at = [pl.ds(pl.multiple_of(j * depth + step * chunk, 128), chunk) for j in range(2)]
        left = [jnp.concatenate([ref[:, at[0]], ref[:, at[1]]], 1) for ref in (left_h, left_l)]
        upper[...] += product(left, right, INNER)

    return pl.pallas_call(
        kernel,
        grid=(steps,),
        in_specs=[SMEM, SMEM, pl.BlockSpec((1, 2, chunk, cols), lambda i: (0, 0, i, 0))]
        + [fixed(x.shape) for x in blocks],
        out_specs=fixed((width, cols)),
        out_shape=jax.ShapeDtypeStruct((width, cols), F32),
        scratch_shapes=[pltpu.VMEM((width, 2 * depth), BF16)] * 2,
        compiler_params=room(58),
        cost_estimate=QUICK,
    )(place, weights, tile, *blocks)


def routing(place, block_owners, n_pole, n_row, n_col, capacity):
    owners_here = n_row * n_col
    devices_all = n_pole * owners_here
    blocks, top = block_owners.shape
    lanes = -(-blocks // 128) * 128
    columns = -(-devices_all // 128) * 128

    def earlier(x, at, axis):
        count = jnp.zeros_like(x)
        for k in range(1, BLOCKS):
            count = count + jnp.where(at >= k, jnp.roll(x, k, axis), 0.0)
        return count

    def kernel(place, owners, slots, source):
        named = jnp.concatenate(
            [owners[...].astype(F32), jnp.full((top, lanes - blocks), -1.0, F32)], 1
        ) if lanes > blocks else owners[...].astype(F32)
        number = lax.broadcasted_iota(jnp.int32, (1, lanes), 1)
        within = lax.rem(number, BLOCKS)
        me = place[5].astype(F32)
        hit = jnp.zeros((1, lanes), F32)
        for t in range(top):
            hit = hit + jnp.where(named[t : t + 1] == me, 1.0, 0.0)
        rank = earlier(hit, within, 1)
        value = (within + 1).astype(F32) * hit
        by_slot = jnp.concatenate(
            [jnp.where(rank == s, value, 0.0) for s in range(capacity)]
            + [jnp.zeros((8 - capacity, lanes), F32)],
            0,
        )
        block = lax.broadcasted_iota(jnp.int32, (lanes, columns), 0)
        group = lax.broadcasted_iota(jnp.int32, (lanes, columns), 1)
        inside = jnp.where((block >= group * BLOCKS) & (block < (group + 1) * BLOCKS), 1.0, 0.0)
        slots[...] = jnp.dot(by_slot, inside, preferred_element_type=F32).astype(jnp.int32)
        block = lax.broadcasted_iota(jnp.int32, (lanes, 128), 0)
        at = lax.broadcasted_iota(jnp.int32, (lanes, 128), 1)
        owner = place[0] * owners_here + lax.broadcasted_iota(jnp.int32, (owners_here, 128), 0)
        local = lax.broadcasted_iota(jnp.int32, (owners_here, 128), 1)
        for d in range(n_pole):
            group = (place[3] * n_pole + (place[0] ^ d)) * n_col + place[4]
            own = jnp.where((block == group * BLOCKS + at) & (at < BLOCKS), 1.0, 0.0)
            here = jnp.dot(named + 1.0, own, preferred_element_type=F32) - 1.0
            hit = jnp.zeros((owners_here, 128), F32)
            for t in range(top):
                hit = hit + jnp.where(here[t : t + 1] == owner.astype(F32), 1.0, 0.0)
            rank = earlier(hit, local, 1)
            value = (local + 1).astype(F32) * hit
            out = jnp.zeros((owners_here, 128), F32)
            for s in range(capacity):
                total = jnp.sum(jnp.where(rank == s, value, 0.0), 1, keepdims=True)
                out = out + jnp.where(local == s, total, 0.0)
            source[d] = out.astype(jnp.int32)

    return pl.pallas_call(
        kernel,
        in_specs=[SMEM, VMEM],
        out_specs=[VMEM] * 2,
        out_shape=[
            jax.ShapeDtypeStruct((8, columns), jnp.int32),
            jax.ShapeDtypeStruct((n_pole, owners_here, 128), jnp.int32),
        ],
        cost_estimate=QUICK,
    )(place, block_owners.T)


def routed_blocks(place, slots, blocks, n_pole, n_row, n_col, capacity):
    _, rows, points = blocks.shape

    def kernel(place, slots, blocks, out):
        for row in range(n_row):
            for col in range(n_col):
                for d in range(n_pole):
                    group = (row * n_pole + (place[0] ^ d)) * n_col + col
                    for s in range(capacity):
                        at = jnp.maximum(slots[s, group] - 1, 0)
                        out[row * n_col + col, d * capacity + s] = blocks[group * BLOCKS + at]

    return pl.pallas_call(
        kernel,
        in_specs=[SMEM, SMEM, VMEM],
        out_specs=VMEM,
        out_shape=jax.ShapeDtypeStruct((n_row * n_col, n_pole * capacity, rows, points), F32),
        cost_estimate=QUICK,
    )(place, slots, blocks)


def charge_terms_plain(place, source, rows, pivots, bases, ancestor):
    n_pole, (n_rows, width) = len(rows), rows[0].shape
    n_row, owners, slots, block_rows, points = ancestor.shape
    capacity = slots // n_pole
    left = jnp.concatenate([sum(pivots)] + list(rows), 0)
    terms = []
    for at_row in range(n_row):
        basis = sum(jnp.where((place[3] ^ b) == at_row, x, 0.0) for b, x in bases.items())
        basis = jnp.roll(basis, place[4], 0)
        basis = basis.reshape(owners, basis.shape[1], -1, points).transpose(0, 2, 1, 3).reshape(owners, width, points)
        result = jnp.einsum("ij,kjg->kig", left, basis, precision=lax.Precision.HIGH)
        total = jnp.sum(result[:, :width] * basis, 1)
        blocks = result[:, width:].reshape(owners, n_pole * BLOCKS, block_rows, points)
        at = source[:, at_row * owners : (at_row + 1) * owners, :capacity].transpose(1, 0, 2) - 1
        place_of = jnp.maximum(at, 0) + jnp.arange(n_pole, dtype=jnp.int32)[None, :, None] * BLOCKS
        found = jax.vmap(lambda x, k: x[k])(blocks, place_of.reshape(owners, slots)) * ancestor[at_row]
        found = jnp.where(at.reshape(owners, slots, 1, 1) >= 0, found, 0.0)
        terms.append(total + jnp.sum(found, (1, 2)))
    return jnp.stack(terms)[:, :, None]


def charge_terms(place, source, rows, pivots, bases, ancestor):
    n_pole, (n_rows, width) = len(rows), rows[0].shape
    n_row, owners, slots, block_rows, points = ancestor.shape
    capacity = slots // n_pole
    fold = bases[0].shape[2] // points
    if block_rows % 8:
        return charge_terms_plain(place, source, rows, pivots, bases, ancestor)
    order = sorted(bases)
    n_groups = len(order)

    def kernel(place, source, *refs):
        rows, pivots, refs = refs[:n_pole], refs[n_pole : 2 * n_pole], refs[2 * n_pole :]
        ancestor, bases, (out, held) = refs[0], refs[1 : 1 + n_groups], refs[1 + n_groups :]
        pivot = pivots[0][...]
        for ref in pivots[1:]:
            pivot = pivot + ref[...]
        left = halves(jnp.concatenate([pivot] + [ref[...] for ref in rows], 0))
        for g, b in enumerate(order):
            at_row = place[3] ^ b
            basis = jnp.concatenate(
                [
                    jnp.concatenate([bases[g][k, :, f * points : (f + 1) * points] for f in range(fold)], 0)
                    for k in range(owners)
                ],
                1,
            )
            result = product(left, halves(basis), INNER)
            held[...] = result[width:]
            sums = jnp.sum(result[:width] * basis, 0, keepdims=True)
            for k in range(owners):
                o = lax.rem(place[4] + k, owners)
                lanes = slice(k * points, (k + 1) * points)
                found = jnp.zeros((block_rows, points), F32)
                for d in range(n_pole):
                    for s in range(capacity):
                        at = source[d, at_row * owners + o, s] - 1
                        first = pl.multiple_of(d * n_rows + jnp.maximum(at, 0) * block_rows, block_rows)
                        block = held[pl.ds(first, block_rows), lanes] * ancestor[at_row, o, d * capacity + s]
                        found = found + jnp.where(at >= 0, block, 0.0)
                out[at_row, o] = sums[:, lanes] + jnp.sum(found, 0, keepdims=True)

    return pl.pallas_call(
        kernel,
        in_specs=[SMEM, SMEM] + [VMEM] * (2 * n_pole + 1 + n_groups),
        out_specs=VMEM,
        out_shape=jax.ShapeDtypeStruct((n_row, owners, 1, points), F32),
        scratch_shapes=[pltpu.VMEM((n_pole * n_rows, owners * points), F32)],
        compiler_params=room(58),
        cost_estimate=QUICK,
    )(place, source, *rows, *pivots, ancestor, *[bases[k] for k in order])


def permute(x, axis, pairs):
    return lax.ppermute(x, axis, pairs)


def swap(x, axis, mask):
    return lax.ppermute(x, axis, [(i, i ^ mask) for i in range(lax.axis_size(axis))])


def shift(x, axis, by):
    n = lax.axis_size(axis)
    return lax.ppermute(x, axis, [(i, (i + by) % n) for i in range(n)])


def gather_swapped(x, axis, first):
    n = lax.axis_size(axis)
    held = {0: x}
    bit = n // 2
    while bit:
        for d in list(held):
            held[d ^ bit] = swap(after(held[d], *first) if d else x, axis, bit)
        bit //= 2
    return [held[d] for d in range(n)]


def gather_near(x, axis):
    n = lax.axis_size(axis)
    return [shift(x, axis, -p) for p in (range(1, n) if n != 4 else (1, 3))]


def gather_cyclic(x, near, axis):
    if lax.axis_size(axis) != 4:
        return [x] + near
    one, three = near
    leftward = permute(one, axis, [(2, 1), (1, 0)])
    rightward = permute(three, axis, [(1, 2), (2, 3)])
    return [x, one, (leftward, rightward), three]


def joined(blocks, axis, *ready):
    return [
        jnp.where(lax.axis_index(axis) < 2, after(x[0], *ready), x[1]) if isinstance(x, tuple) else x for x in blocks
    ]


def reduce_scatter_swapped(x, axis, masks):
    total = x[0]
    for term, mask in zip(x[1:], masks, strict=True):
        total = total + swap(term, axis, mask)
    return total


def pick(x, at):
    return lax.dynamic_index_in_dim(x, at, 0, keepdims=False)


def gather_all(x, axes):
    n = 1
    for axis in axes:
        n *= lax.axis_size(axis)
    spread = jnp.broadcast_to(x[None], (n,) + x.shape)
    return lax.all_to_all(spread, axes, split_axis=0, concat_axis=0, tiled=True)


def after(x, *others):
    return lax.optimization_barrier((x,) + others)[0]


def halving(x, axis, before, later):
    n = lax.axis_size(axis)
    me = lax.axis_index(axis)
    held = [pick(x, me ^ d) for d in range(n)]
    bit = 1
    while bit < n:
        away = [d for d in range(0, n, bit) if d & bit]
        out = jnp.stack([held[d] for d in away])
        if bit == 2:
            later = after(later, out)
        arrived = swap(out, axis, bit)
        if bit == 1:
            arrived = after(arrived, *before)
        for j, d in enumerate(away):
            held[d ^ bit] = held[d ^ bit] + arrived[j]
        bit *= 2
    return held[0], later


def body(
    inverse_tile,
    lower_factor,
    upper_factor,
    pivot_inverse,
    pole_weights,
    block_owners,
    basis_ancestor,
    basis_super,
):
    n_pole, n_row, n_col = (lax.axis_size(a) for a in ("pole", "row", "col"))
    pole, row, col = (lax.axis_index(a) for a in ("pole", "row", "col"))
    devices_all = n_pole * n_row * n_col
    tile_rows, tile_cols = inverse_tile.shape[2:]
    width, points = basis_super.shape
    capacity = max(2, (BLOCKS * block_owners.shape[1] + devices_all - 1) // devices_all)
    piece = upper_factor.shape[2]
    rows_here = tile_rows // (n_pole * n_col)
    block_rows = rows_here // BLOCKS
    out_rows = width // (n_pole * n_row)
    groups = n_row * n_pole * n_col
    me = (pole * n_row + row) * n_col + col
    position = (row * n_pole + pole) * n_col + col
    place = jnp.stack([pole, row // 2, row % 2, row, col, me, position]).astype(jnp.int32)

    fold = width // piece
    basis = basis_super.reshape(fold, piece, points).transpose(1, 0, 2).reshape(piece, fold * points)
    upper_own = [upper_factor[0, 0], jnp.concatenate([upper_factor[0, 1], basis], 1)]
    upper_near = [gather_near(x, "col") for x in upper_own]

    slots, source = routing(place, block_owners, n_pole, n_row, n_col, capacity)
    ancestor = routed_blocks(
        place, slots, basis_ancestor.reshape(groups * BLOCKS, block_rows, points), n_pole, n_row, n_col, capacity
    )
    lower = gather_swapped(lower_factor[0], "row", (ancestor, *upper_near[0]))


    parts, beside = lower_products(place, pole_weights, inverse_tile, lower, n_pole)
    upper = [
        gather_cyclic(upper_own[0], upper_near[0], "col"),
        gather_cyclic(upper_own[1], [after(x, parts[0]) for x in upper_near[1]], "col"),
    ]
    half = reduce_scatter_swapped(parts, "pole", list(range(1, n_pole)))
    upper[1] = joined(upper[1], "col")
    ancestor = lax.all_to_all(
        after(ancestor, upper[1][n_col // 2]), ("row", "col"), split_axis=0, concat_axis=0, tiled=True
    ).reshape(n_row, n_col, -1, block_rows, points)

    line = jnp.stack([x[:, tile_rows:] for x in upper[1]])
    bases = {b: swap(line, "row", b) if b else line for b in range(0, n_row, 2)}
    upper[0] = joined(upper[0], "col", half)
    upper = [x for pair in zip(*upper, strict=True) for x in pair]

    pivot = pivot_term(place, pole_weights, upper, beside, pivot_inverse)
    pivots = [pivot] + [swap(pivot, "pole", d) for d in range(1, n_pole)]
    product_upper = upper_products(place, after(pole_weights, pivot), inverse_tile, upper)
    for b in list(bases):
        bases[b + 1] = swap(bases[b], "row", 1)
    rows, product_upper = halving(half.reshape(n_col, rows_here, width), "col", (product_upper, pivots[-1]), product_upper)
    rows = [rows] + [swap(rows, "pole", d) for d in range(1, n_pole)]
    arrived = lax.all_to_all(
        product_upper.reshape(n_pole * n_row, -1, tile_cols),
        ("pole", "row"),
        split_axis=0,
        concat_axis=0,
        tiled=True,
    )

    terms = charge_terms(place, source, rows, pivots, bases, ancestor)
    terms = lax.all_to_all(
        after(terms, arrived).reshape(n_row * n_col, 1, points),
        ("row", "col"),
        split_axis=0,
        concat_axis=0,
        tiled=True,
    )
    return (jnp.sum(arrived, 0), jnp.sum(terms, (0, 1)))


def solution(mesh):
    placed = (
        P("pole", None, "row", "col"),
        P("pole", None, "row", "col"),
        P("pole", None, "col", "row"),
        P("pole", None, "row", "col"),
        P("pole", None),
        P(),
        P(None, ("pole", "row", "col")),
        P(None, ("pole", "row", "col")),
    )
    return jax.shard_map(
        body,
        mesh=mesh,
        in_specs=placed,
        out_specs=(P(("pole", "row"), "col"), P(("pole", "row", "col"))),
        check_vma=False,
    )
```

time: 179 us -> 132 us (0.74); the launches traced: 176 us -> 131 us
  Pallas kernels: 0 us -> 38 us
  matrix products: 33.1 us -> 0 us
  local copies, waits for them, and re-layouts: 29.6 us -> 7.07 us
  starting transfers between devices: 50 us -> 38.4 us
  other arithmetic: 16 us -> 6.5 us
  waiting for transfers between devices: 46.2 us -> 40.3 us
    pallas_call x0 -> x6, Pallas kernels: none -> 38 us  [the longest x1 13.9 us: lower_products(): pl.pallas_call(kernel, grid=(steps,), in_specs=[SMEM, SMEM, pl.BlockSpec(...]
    dot_general x10 -> x0, matrix products: 33.1 us -> none  [the longest x9 32.6 us: dot(): lax.dot_general(left, right, (contract, ((), ())), precision=HIGH, prefer...]
    ppermute x8 -> x4, starting transfers between devices: 15.6 us -> 4.66 us  [permute(): return lax.ppermute(x, axis, pairs)]
    squeeze x16 -> x1, local copies, waits for them, and re-layouts: 9.82 us -> 1.09 us  [body(): upper_factor[0, 1]]
    all_to_all x3, waiting for transfers between devices: 14.2 us -> 5.65 us  [the longest x1 5.64 us: body(): lax.all_to_all(after(terms, arrived).reshape(n_row * n_col, 1, points), (...]
    ppermute x9 -> x11, waiting for transfers between devices: 6.97 us -> 13.1 us  [swap(): lax.ppermute(x, axis, [(i, i ^ mask) for i in range(lax.axis_size(axis))])]
    add x2 -> x0, local copies, waits for them, and re-layouts: 4.16 us -> none  [the longest x1 2.78 us: body(): pivot = pivot + placed]
    ppermute x5 -> x4, waiting for transfers between devices: 13.8 us -> 9.97 us  [shift(): return lax.ppermute(x, axis, [(i, (i + by) % n) for i in range(n)])]
  transfers between devices with their start and end apart: 25 -> 22, of which waited for: 11 -> 7; matrix products, arithmetic and copies ran while one was open for 31% -> 8% of each run, Pallas kernels for 0% -> 29%
where the time goes in v2:
time: 132 us; the launch traced here: 131 us
  waiting for transfers between devices  40.3 us (31%)
  starting transfers between devices  38.4 us (29%)
  Pallas kernels  38 us (29%)
  local copies, waits for them, and re-layouts  7.07 us (5%)
  other arithmetic  6.5 us (5%)
    pallas_call x1, Pallas kernels, lower_products(): pl.pallas_call(kernel, grid=(steps,), in_specs=[SMEM, SMEM, pl.BlockSpec(...  13.9 us
    ppermute x11, starting transfers between devices, swap(): lax.ppermute(x, axis, [(i, i ^ mask) for i in range(lax.axis_size(axis))])  13.3 us
    ppermute x11, waiting for transfers between devices, swap(): lax.ppermute(x, axis, [(i, i ^ mask) for i in range(lax.axis_size(axis))])  13.1 us
    ppermute x4, waiting for transfers between devices, permute(): return lax.ppermute(x, axis, pairs)  11.6 us
    pallas_call x1, Pallas kernels, upper_products(): pl.pallas_call(kernel, grid=(steps,), in_specs=[SMEM, SMEM, pl.BlockSpec(...  10.1 us
    ppermute x4, waiting for transfers between devices, shift(): return lax.ppermute(x, axis, [(i, (i + by) % n) for i in range(n)])  9.97 us
    all_to_all x1, starting transfers between devices, body(): lax.all_to_all(after(ancestor, upper[1][n_col // 2]), ('row', 'col'), spl...  6.25 us
    ppermute x4, starting transfers between devices, shift(): return lax.ppermute(x, axis, [(i, (i + by) % n) for i in range(n)])  5.74 us
  transfers between devices with their start and end apart: 22, of which 7 were waited for; matrix products, arithmetic and copies ran while one was open for 8% of the time, Pallas kernels for 29%

profile of v2, /device:TPU:0, one launch (start us, length us, event | category | flops | bytes accessed | tf_op | source)
XLA Modules:
  0.0 131.3 jit_solution(10653037961917874791)
XLA Ops:
  0.7 3.0 %collective-permute-start.3 = (f32[2,64,1152]{2,1,0:T(8,128)}, f32[2,64,1152]{2,1,0:T(8,128)S(1)}, u32[]{:S(2)}, u32[]{:S(2)}) collective-permute-start(f32[2,64,1152]{2,1,0:T(8,128)} %bitcast.44), channel_id=1, source_target_pairs={{0,8},{4,12},{8,0},{12,4},{1,9},{5,13},{9,1},{13,5},{2,10},{6,14},... | collective-permute-start | bytes 1769480 | tf_op jit(solution)/shard_map/ppermute | solution.py:338
  4.8 3.7 %collective-permute-start = (f32[64,1152]{1,0:T(8,128)S(1)}, f32[64,1152]{1,0:T(8,128)S(1)}, u32[]{:S(2)}, u32[]{:S(2)}) collective-permute-start(f32[64,1152]{1,0:T(8,128)S(1)} %get-tuple-element.35.refs_0_), channel_id=1, source_target_pairs={{0,3},{1,0},{2,1},{3,2},{4,7},{5,4},{6,5},{7,6},{8,11},{9,8},{10,9... | collective-permute-start | bytes 884744 | tf_op jit(solution)/shard_map/ppermute | solution.py:343
  9.3 1.9 %shard_map.95 = (s32[8,128]{1,0:T(8,128)}, s32[2,16,128]{2,1,0:T(8,128)}) custom-call(s32[7]{0:T(128)} %stack.49.place, s32[6,576]{1,0:T(8,128)} %bitcast.50), custom_call_target="tpu_custom_call" | custom-call | tf_op jit(solution)/shard_map/pallas_call | solution.py:227
  11.2 2.8 %shard_map.96 = f32[16,8,8,128]{3,2,1,0:T(8,128)} custom-call(s32[7]{0:T(128)} %stack.49.place, s32[8,128]{1,0:T(8,128)} %get-tuple-element.17.slots, f32[576,8,128]{2,1,0:T(8,128)} %bitcast.40), custom_call_target="tpu_custom_call" | custom-call | tf_op jit(solution)/shard_map/pallas_call | solution.py:251
  14.0 1.9 %collective-permute-done.refs_2_ = f32[64,1152]{1,0:T(8,128)S(1)} collective-permute-done((f32[64,1152]{1,0:T(8,128)S(1)}, f32[64,1152]{1,0:T(8,128)S(1)}, u32[]{:S(2)}, u32[]{:S(2)}) %collective-permute-start) | collective-permute-done | bytes 294944 | tf_op jit(solution)/shard_map/ppermute | solution.py:343
  15.9 5.8 %collective-permute-done.4.refs_6_ = f32[64,1152]{1,0:T(8,128)S(1)} collective-permute-done((f32[64,1152]{1,0:T(8,128)S(1)}, f32[64,1152]{1,0:T(8,128)S(1)}, u32[]{:S(2)}, u32[]{:S(2)}) %collective-permute-start.4) | collective-permute-done | bytes 294944 | tf_op jit(solution)/shard_map/ppermute | solution.py:343
  21.8 1.8 %collective-permute-start.1 = (f32[64,1664]{1,0:T(8,128)S(1)}, f32[64,1664]{1,0:T(8,128)S(1)}, u32[]{:S(2)}, u32[]{:S(2)}) collective-permute-start(f32[64,1664]{1,0:T(8,128)S(1)} %pad_maximum_fusion.1.refs_1_), channel_id=1, source_target_pairs={{0,3},{1,0},{2,1},{3,2},{4,7},{5,4},{6,5},{7,6},{8,11},{9,8},{10,9... | collective-permute-start | bytes 1277960 | tf_op jit(solution)/shard_map/ppermute | solution.py:343
  27.3 13.9 %shard_map.97 = (f32[576,256]{1,0:T(8,128)}, f32[576,256]{1,0:T(8,128)}, bf16[1152,512]{1,0:T(8,128)(2,1)}, bf16[1152,512]{1,0:T(8,128)(2,1)}) custom-call(s32[7]{0:T(128)} %stack.49.place, f32[1,2]{1,0:T(1,128)} %weights.4, f32[1,2,1152,1152]{3,2,1,0:T(8,128)} %tile.3, f32[2,64,1152]{2,1,0:T(8,128)} %bitcast.45, ...), custom_call_target="tpu_custom_call" | custom-call | tf_op jit(solution)/shard_map/pallas_call | solution.py:76
  41.2 2.4 %collective-permute-done.1.refs_3_ = f32[64,1664]{1,0:T(8,128)S(1)} collective-permute-done((f32[64,1664]{1,0:T(8,128)S(1)}, f32[64,1664]{1,0:T(8,128)S(1)}, u32[]{:S(2)}, u32[]{:S(2)}) %collective-permute-start.1) | collective-permute-done | bytes 426016 | tf_op jit(solution)/shard_map/ppermute | solution.py:343
  48.4 11.6 %collective-permute-done.9 = f32[64,1664]{1,0:T(8,128)S(1)} collective-permute-done((f32[64,1664]{1,0:T(8,128)S(1)}, f32[64,1664]{1,0:T(8,128)S(1)}, u32[]{:S(2)}, u32[]{:S(2)}) %collective-permute-start.9) | collective-permute-done | bytes 426016 | tf_op jit(solution)/shard_map/ppermute | solution.py:334
  60.8 6.3 %all-to-all-start.1 = ((f32[16,8,8,128]{3,2,1,0:T(8,128)}), f32[16,8,8,128]{3,2,1,0:T(8,128)S(1)}, u32[]{:S(2)}, u32[]{:S(2)}) async-start(f32[16,8,8,128]{3,2,1,0:T(8,128)} %shard_map.96), calls=%async_computation.1 | async-start | bytes 1048576 | tf_op jit(solution)/shard_map/all_to_all | solution.py:463
  67.2 2.0 %collective-permute-start.12 = (f32[2,144,256]{2,1,0:T(8,128)S(1)}, f32[2,144,256]{2,1,0:T(8,128)}, u32[]{:S(2)}, u32[]{:S(2)}) collective-permute-start(f32[2,144,256]{2,1,0:T(8,128)S(1)} %pad_maximum_fusion.2), channel_id=1, source_target_pairs={{0,1},{1,0},{2,3},{3,2},{4,5},{5,4},{6,7},{7,6},{8,9},{9,8},{10,11... | collective-permute-start | bytes 884744 | tf_op jit(solution)/shard_map/ppermute | solution.py:338
  69.2 1.7 %broadcast_select_fusion.1.refs_4_ = f32[64,1152]{1,0:T(8,128)} fusion(f32[64,1152]{1,0:T(8,128)} %collective-permute-done.6, f32[64,1152]{1,0:T(8,128)} %collective-permute-done.8, pred[]{:T(512)S(6)} %lt.24), kind=kLoop, calls=%fused_computation.8 | loop fusion | flops 73728 | bytes 884737 | tf_op jit(solution)/shard_map/jit(_where)/select_n | solution.py:373
  70.9 4.6 %shard_map.98.refs_2_ = f32[256,256]{1,0:T(8,128)} custom-call(s32[7]{0:T(128)} %stack.49.place, f32[1,2]{1,0:T(1,128)} %weights.4, f32[64,1152]{1,0:T(8,128)} %copy-done.1, f32[64,1664]{1,0:T(8,128)} %copy-done, f32[64,1152]{1,0:T(8,128)} %copy-done.6, f32[64,1664]{1,0:T(8,128)} %copy-done.2, f32[64,1152]{1,0:T(8,128)} %broadcast_select_fusion.1.refs_4_, ...), custom_call_target="tpu_custom_call" | custom-call | tf_op jit(solution)/shard_map/pallas_call | solution.py:115
  78.6 10.1 %shard_map.99 = f32[256,1152]{1,0:T(8,128)} custom-call(s32[7]{0:T(128)} %stack.49.place, f32[1,2]{1,0:T(1,128)} %weights.4, f32[1,2,1152,1152]{3,2,1,0:T(8,128)} %tile.3, f32[64,1152]{1,0:T(8,128)} %copy-done.1, f32[64,1664]{1,0:T(8,128)} %copy-done, f32[64,1152]{1,0:T(8,128)} %copy-done.6, f32[64,1664]{1,0:T(8,128)} %copy-done.2, ...), custom_call_target="tpu_custom_call" | custom-call | tf_op jit(solution)/shard_map/pallas_call | solution.py:161
  89.5 1.6 %slice_add_fusion = f32[1,144,256]{2,1,0:T(8,128)} fusion(f32[2,144,256]{2,1,0:T(8,128)} %collective-permute-done.12, f32[4,144,256]{2,1,0:T(8,128)S(1)} %bitcast.38, s32[]{:T(128)S(6)} %select_n.46), kind=kLoop, calls=%fused_computation.7 | loop fusion | flops 36864 | bytes 442372 | tf_op jit(solution)/shard_map/add | solution.py:414
  91.9 3.7 %all-to-all-start = ((f32[8,32,1152]{2,1,0:T(8,128)}), f32[8,32,1152]{2,1,0:T(8,128)S(1)}, u32[]{:S(2)}, u32[]{:S(2)}) async-start(f32[8,32,1152]{2,1,0:T(8,128)} %bitcast.36), calls=%async_computation | async-start | bytes 2359296 | tf_op jit(solution)/shard_map/all_to_all | solution.py:479
  95.6 2.4 %collective-permute-start.14 = (f32[1,144,256]{2,1,0:T(8,128)}, f32[1,144,256]{2,1,0:T(8,128)S(1)}, u32[]{:S(2)}, u32[]{:S(2)}) collective-permute-start(f32[1,144,256]{2,1,0:T(8,128)} %slice_add_fusion), channel_id=1, source_target_pairs={{0,2},{1,3},{2,0},{3,1},{4,6},{5,7},{6,4},{7,5},{8,10},{9,11},{10,... | collective-permute-start | bytes 442376 | tf_op jit(solution)/shard_map/ppermute | solution.py:338
  98.6 7.3 %collective-permute-done.14 = f32[1,144,256]{2,1,0:T(8,128)S(1)} collective-permute-done((f32[1,144,256]{2,1,0:T(8,128)}, f32[1,144,256]{2,1,0:T(8,128)S(1)}, u32[]{:S(2)}, u32[]{:S(2)}) %collective-permute-start.14) | collective-permute-done | bytes 147488 | tf_op jit(solution)/shard_map/ppermute | solution.py:338
  106.8 1.8 %collective-permute-start.15 = (f32[144,256]{1,0:T(8,128)S(1)}, f32[144,256]{1,0:T(8,128)S(1)}, u32[]{:S(2)}, u32[]{:S(2)}) collective-permute-start(f32[144,256]{1,0:T(8,128)S(1)} %add_bitcast_fusion.refs_0_), channel_id=1, source_target_pairs={{0,16},{16,0},{1,17},{17,1},{2,18},{18,2},{3,19},{19,3},{4,20},{20... | collective-permute-start | bytes 442376 | tf_op jit(solution)/shard_map/ppermute | solution.py:338
  108.6 5.8 %collective-permute-done.15.refs_1_ = f32[144,256]{1,0:T(8,128)S(1)} collective-permute-done((f32[144,256]{1,0:T(8,128)S(1)}, f32[144,256]{1,0:T(8,128)S(1)}, u32[]{:S(2)}, u32[]{:S(2)}) %collective-permute-start.15) | collective-permute-done | bytes 147488 | tf_op jit(solution)/shard_map/ppermute | solution.py:338
  115.1 4.6 %shard_map.100 = f32[4,4,1,128]{3,2,1,0:T(1,128)} custom-call(s32[7]{0:T(128)} %stack.49.place, s32[2,16,128]{2,1,0:T(8,128)} %get-tuple-element.29.source, f32[144,256]{1,0:T(8,128)} %copy-done.11, f32[144,256]{1,0:T(8,128)} %copy-done.17, f32[256,256]{1,0:T(8,128)} %shard_map.98.refs_2_, f32[256,256]{1,0:T(8,128)} %copy-done.16, ...), custom_call_target="tpu_custom_call" | custom-call | tf_op jit(solution)/shard_map/pallas_call | solution.py:322
  119.6 4.7 %all-to-all-start.2 = ((f32[16,1,128]{2,1,0:T(1,128)}), f32[16,1,128]{2,1,0:T(1,128)S(1)}, u32[]{:S(2)}, u32[]{:S(2)}) async-start(f32[16,1,128]{2,1,0:T(1,128)} %bitcast.49), calls=%async_computation.2 | async-start | bytes 16384 | tf_op jit(solution)/shard_map/all_to_all | solution.py:488
  125.1 5.6 %all-to-all-done.2 = f32[16,1,128]{2,1,0:T(1,128)S(1)} async-done(((f32[16,1,128]{2,1,0:T(1,128)}), f32[16,1,128]{2,1,0:T(1,128)S(1)}, u32[]{:S(2)}, u32[]{:S(2)}) %all-to-all-start.2) | async-done | bytes 8224 | tf_op jit(solution)/shard_map/all_to_all | solution.py:488
  (83 shorter events, 19.4 us)
Async XLA Ops:
  0.7 21.0 %collective-permute-start.3 = (f32[2,64,1152]{2,1,0:T(8,128)}, f32[2,64,1152]{2,1,0:T(8,128)S(1)}, u32[]{:S(2)}, u32[]{:S(2)}) collective-permute-start(f32[2,64,1152]{2,1,0:T(8,128)} %bitcast.44), channel_id=1, source_target_pairs={{0,8},{4,12},{8,0},{12,4},{1,9},{5,13},{9,1},{13,5},{2,10},{6,14},... | collective-permute-start | bytes 1769480 | tf_op jit(solution)/shard_map/ppermute | solution.py:338
  4.8 11.1 %collective-permute-start = (f32[64,1152]{1,0:T(8,128)S(1)}, f32[64,1152]{1,0:T(8,128)S(1)}, u32[]{:S(2)}, u32[]{:S(2)}) collective-permute-start(f32[64,1152]{1,0:T(8,128)S(1)} %get-tuple-element.35.refs_0_), channel_id=1, source_target_pairs={{0,3},{1,0},{2,1},{3,2},{4,7},{5,4},{6,5},{7,6},{8,11},{9,8},{10,9... | collective-permute-start | bytes 884744 | tf_op jit(solution)/shard_map/ppermute | solution.py:343
  8.4 13.2 %collective-permute-start.4 = (f32[64,1152]{1,0:T(8,128)S(1)}, f32[64,1152]{1,0:T(8,128)S(1)}, u32[]{:S(2)}, u32[]{:S(2)}) collective-permute-start(f32[64,1152]{1,0:T(8,128)S(1)} %get-tuple-element.35.refs_0_), channel_id=1, source_target_pairs={{0,1},{1,2},{2,3},{3,0},{4,5},{5,6},{6,7},{7,4},{8,9},{9,10},{10,1... | collective-permute-start | bytes 884744 | tf_op jit(solution)/shard_map/ppermute | solution.py:343
  8.4 17.4 %collective-permute-start.2 = (f32[2,64,1152]{2,1,0:T(8,128)S(1)}, f32[2,64,1152]{2,1,0:T(8,128)}, u32[]{:S(2)}, u32[]{:S(2)}) collective-permute-start(f32[2,64,1152]{2,1,0:T(8,128)S(1)} %bitcast.46), channel_id=1, source_target_pairs={{0,4},{4,0},{8,12},{12,8},{1,5},{5,1},{9,13},{13,9},{2,6},{6,2},{1... | collective-permute-start | bytes 1769480 | tf_op jit(solution)/shard_map/ppermute | solution.py:338
  15.9 25.3 %copy-start.6 = (f32[64,1152]{1,0:T(8,128)}, f32[64,1152]{1,0:T(8,128)S(1)}, u32[]{:S(2)}) copy-start(f32[64,1152]{1,0:T(8,128)S(1)} %collective-permute-done.refs_2_) | copy-start | bytes 884740
  21.7 5.6 %collective-permute-start.5 = (f32[2,64,1152]{2,1,0:T(8,128)S(1)}, f32[2,64,1152]{2,1,0:T(8,128)}, u32[]{:S(2)}, u32[]{:S(2)}) collective-permute-start(f32[2,64,1152]{2,1,0:T(8,128)S(1)} %collective-permute-done.3.refs_2_), channel_id=1, source_target_pairs={{0,4},{4,0},{8,12},{12,8},{1,5},{5,1},{9,13},{13,9},{2,6},{6,2},{1... | collective-permute-start | bytes 1769480 | tf_op jit(solution)/shard_map/ppermute | solution.py:338
  21.8 21.8 %collective-permute-start.1 = (f32[64,1664]{1,0:T(8,128)S(1)}, f32[64,1664]{1,0:T(8,128)S(1)}, u32[]{:S(2)}, u32[]{:S(2)}) collective-permute-start(f32[64,1664]{1,0:T(8,128)S(1)} %pad_maximum_fusion.1.refs_1_), channel_id=1, source_target_pairs={{0,3},{1,0},{2,1},{3,2},{4,7},{5,4},{6,5},{7,6},{8,11},{9,8},{10,9... | collective-permute-start | bytes 1277960 | tf_op jit(solution)/shard_map/ppermute | solution.py:343
  23.6 22.8 %collective-permute-start.10 = (f32[64,1664]{1,0:T(8,128)S(1)}, f32[64,1664]{1,0:T(8,128)S(1)}, u32[]{:S(2)}, u32[]{:S(2)}) collective-permute-start(f32[64,1664]{1,0:T(8,128)S(1)} %pad_maximum_fusion.1.refs_1_), channel_id=1, source_target_pairs={{0,1},{1,2},{2,3},{3,0},{4,5},{5,6},{6,7},{7,4},{8,9},{9,10},{10,1... | collective-permute-start | bytes 1277960 | tf_op jit(solution)/shard_map/ppermute | solution.py:343
  24.6 42.5 %collective-permute-start.6 = (f32[64,1152]{1,0:T(8,128)S(1)}, f32[64,1152]{1,0:T(8,128)}, u32[]{:S(2)}, u32[]{:S(2)}) collective-permute-start(f32[64,1152]{1,0:T(8,128)S(1)} %collective-permute-done.refs_2_), channel_id=1, source_target_pairs={{2,1},{1,0},{6,5},{5,4},{10,9},{9,8},{14,13},{13,12},{18,17},{17,1... | collective-permute-start | bytes 884744 | tf_op jit(solution)/shard_map/ppermute | solution.py:334
  25.9 43.3 %collective-permute-start.8 = (f32[64,1152]{1,0:T(8,128)S(1)}, f32[64,1152]{1,0:T(8,128)}, u32[]{:S(2)}, u32[]{:S(2)}) collective-permute-start(f32[64,1152]{1,0:T(8,128)S(1)} %collective-permute-done.4.refs_6_), channel_id=1, source_target_pairs={{1,2},{2,3},{5,6},{6,7},{9,10},{10,11},{13,14},{14,15},{17,18},{18... | collective-permute-start | bytes 884744 | tf_op jit(solution)/shard_map/ppermute | solution.py:334
  43.6 23.4 %collective-permute-start.7 = (f32[576,256]{1,0:T(8,128)}, f32[576,256]{1,0:T(8,128)S(1)}, u32[]{:S(2)}, u32[]{:S(2)}) collective-permute-start(f32[576,256]{1,0:T(8,128)} %get-tuple-element.21), channel_id=1, source_target_pairs={{0,16},{16,0},{1,17},{17,1},{2,18},{18,2},{3,19},{19,3},{4,20},{20... | collective-permute-start | bytes 1769480 | tf_op jit(solution)/shard_map/ppermute | solution.py:338
  45.1 14.9 %collective-permute-start.9 = (f32[64,1664]{1,0:T(8,128)S(1)}, f32[64,1664]{1,0:T(8,128)S(1)}, u32[]{:S(2)}, u32[]{:S(2)}) collective-permute-start(f32[64,1664]{1,0:T(8,128)S(1)} %collective-permute-done.1.refs_3_), channel_id=1, source_target_pairs={{2,1},{1,0},{6,5},{5,4},{10,9},{9,8},{14,13},{13,12},{18,17},{17,1... | collective-permute-start | bytes 1277960 | tf_op jit(solution)/shard_map/ppermute | solution.py:334
  46.4 13.6 %collective-permute-start.11 = (f32[64,1664]{1,0:T(8,128)S(1)}, f32[64,1664]{1,0:T(8,128)S(1)}, u32[]{:S(2)}, u32[]{:S(2)}) collective-permute-start(f32[64,1664]{1,0:T(8,128)S(1)} %collective-permute-done.10.refs_7_), channel_id=1, source_target_pairs={{1,2},{2,3},{5,6},{6,7},{9,10},{10,11},{13,14},{14,15},{17,18},{18... | collective-permute-start | bytes 1277960 | tf_op jit(solution)/shard_map/ppermute | solution.py:334
  60.8 30.3 %all-to-all-start.1 = ((f32[16,8,8,128]{3,2,1,0:T(8,128)}), f32[16,8,8,128]{3,2,1,0:T(8,128)S(1)}, u32[]{:S(2)}, u32[]{:S(2)}) async-start(f32[16,8,8,128]{3,2,1,0:T(8,128)} %shard_map.96), calls=%async_computation.1 | async-start | bytes 1048576 | tf_op jit(solution)/shard_map/all_to_all | solution.py:463
  67.2 21.6 %collective-permute-start.12 = (f32[2,144,256]{2,1,0:T(8,128)S(1)}, f32[2,144,256]{2,1,0:T(8,128)}, u32[]{:S(2)}, u32[]{:S(2)}) collective-permute-start(f32[2,144,256]{2,1,0:T(8,128)S(1)} %pad_maximum_fusion.2), channel_id=1, source_target_pairs={{0,1},{1,0},{2,3},{3,2},{4,5},{5,4},{6,7},{7,6},{8,9},{9,8},{10,11... | collective-permute-start | bytes 884744 | tf_op jit(solution)/shard_map/ppermute | solution.py:338
  75.6 13.2 %collective-permute-start.13 = (f32[256,256]{1,0:T(8,128)}, f32[256,256]{1,0:T(8,128)S(1)}, u32[]{:S(2)}, u32[]{:S(2)}) collective-permute-start(f32[256,256]{1,0:T(8,128)} %shard_map.98.refs_2_), channel_id=1, source_target_pairs={{0,16},{16,0},{1,17},{17,1},{2,18},{18,2},{3,19},{19,3},{4,20},{20... | collective-permute-start | bytes 786440 | tf_op jit(solution)/shard_map/ppermute | solution.py:338
  77.1 21.0 %copy-start.5 = (f32[4,64,512]{2,1,0:T(8,128)}, f32[4,64,512]{2,1,0:T(8,128)S(1)}, u32[]{:S(2)}) copy-start(f32[4,64,512]{2,1,0:T(8,128)S(1)} %pad_maximum_fusion.refs_5_) | copy-start | bytes 1572868
  77.1 21.0 %collective-permute-start.17 = (f32[4,64,512]{2,1,0:T(8,128)S(1)}, f32[4,64,512]{2,1,0:T(8,128)S(1)}, u32[]{:S(2)}, u32[]{:S(2)}) collective-permute-start(f32[4,64,512]{2,1,0:T(8,128)S(1)} %pad_maximum_fusion.refs_5_), channel_id=1, source_target_pairs={{0,8},{4,12},{8,0},{12,4},{1,9},{5,13},{9,1},{13,5},{2,10},{6,14},... | collective-permute-start | bytes 1572872 | tf_op jit(solution)/shard_map/ppermute | solution.py:338
  91.9 27.8 %all-to-all-start = ((f32[8,32,1152]{2,1,0:T(8,128)}), f32[8,32,1152]{2,1,0:T(8,128)S(1)}, u32[]{:S(2)}, u32[]{:S(2)}) async-start(f32[8,32,1152]{2,1,0:T(8,128)} %bitcast.36), calls=%async_computation | async-start | bytes 2359296 | tf_op jit(solution)/shard_map/all_to_all | solution.py:479
  95.6 10.2 %collective-permute-start.14 = (f32[1,144,256]{2,1,0:T(8,128)}, f32[1,144,256]{2,1,0:T(8,128)S(1)}, u32[]{:S(2)}, u32[]{:S(2)}) collective-permute-start(f32[1,144,256]{2,1,0:T(8,128)} %slice_add_fusion), channel_id=1, source_target_pairs={{0,2},{1,3},{2,0},{3,1},{4,6},{5,7},{6,4},{7,5},{8,10},{9,11},{10,... | collective-permute-start | bytes 442376 | tf_op jit(solution)/shard_map/ppermute | solution.py:338
  98.1 10.5 %collective-permute-start.16 = (f32[4,64,512]{2,1,0:T(8,128)S(1)}, f32[4,64,512]{2,1,0:T(8,128)}, u32[]{:S(2)}, u32[]{:S(2)}) collective-permute-start(f32[4,64,512]{2,1,0:T(8,128)S(1)} %pad_maximum_fusion.refs_5_), channel_id=1, source_target_pairs={{0,4},{4,0},{8,12},{12,8},{1,5},{5,1},{9,13},{13,9},{2,6},{6,2},{1... | collective-permute-start | bytes 1572872 | tf_op jit(solution)/shard_map/ppermute | solution.py:338
  98.1 16.3 %collective-permute-start.18 = (f32[4,64,512]{2,1,0:T(8,128)S(1)}, f32[4,64,512]{2,1,0:T(8,128)}, u32[]{:S(2)}, u32[]{:S(2)}) collective-permute-start(f32[4,64,512]{2,1,0:T(8,128)S(1)} %collective-permute-done.17.refs_7_), channel_id=1, source_target_pairs={{0,4},{4,0},{8,12},{12,8},{1,5},{5,1},{9,13},{13,9},{2,6},{6,2},{1... | collective-permute-start | bytes 1572872 | tf_op jit(solution)/shard_map/ppermute | solution.py:338
  106.8 7.6 %collective-permute-start.15 = (f32[144,256]{1,0:T(8,128)S(1)}, f32[144,256]{1,0:T(8,128)S(1)}, u32[]{:S(2)}, u32[]{:S(2)}) collective-permute-start(f32[144,256]{1,0:T(8,128)S(1)} %add_bitcast_fusion.refs_0_), channel_id=1, source_target_pairs={{0,16},{16,0},{1,17},{17,1},{2,18},{18,2},{3,19},{19,3},{4,20},{20... | collective-permute-start | bytes 442376 | tf_op jit(solution)/shard_map/ppermute | solution.py:338
  119.6 11.1 %all-to-all-start.2 = ((f32[16,1,128]{2,1,0:T(1,128)}), f32[16,1,128]{2,1,0:T(1,128)S(1)}, u32[]{:S(2)}, u32[]{:S(2)}) async-start(f32[16,1,128]{2,1,0:T(1,128)} %bitcast.49), calls=%async_computation.2 | async-start | bytes 16384 | tf_op jit(solution)/shard_map/all_to_all | solution.py:488
  (17 other events, 164.2 us)

commit v3 on v2

--- a/solution.py
+++ b/solution.py
@@ -88,18 +88,35 @@
     return out[:n_pole], out[n_pole:]
 
 
+def flattened(blocks):
+    pairs = [x if isinstance(x, tuple) else (x,) for x in blocks]
+    return [y for x in pairs for y in x], [len(x) for x in pairs]
+
+
+def loaded(refs, counts, col, depth):
+    out, at = [], 0
+    for count in counts:
+        x = refs[at][:, :depth]
+        out.append(x if count == 1 else jnp.where(col < 2, x, refs[at + 1][:, :depth]))
+        at += count
+    return out
+
+
 def pivot_term(place, weights, blocks, lower, pivot_inverse):
     rows = blocks[0].shape[0]
     n_col = len(blocks) // 2
+    flat, counts = flattened(blocks)
     width = n_col * rows
     depth = lower[0].shape[0]
     piece_rows, piece_cols = pivot_inverse.shape[2:]
 
     def kernel(place, weights, *refs):
-        blocks, (lower_h, lower_l, inverse, pivot, left_h, left_l) = refs[: 2 * n_col], refs[2 * n_col :]
+        blocks, refs = refs[: len(flat)], refs[len(flat) :]
+        lower_h, lower_l, inverse, pivot, left_h, left_l = refs
+        blocks = loaded(blocks, counts, place[4], depth)
         for p in range(n_col):
             at = pl.multiple_of(lax.rem(place[4] + p, n_col) * rows, 16)
-            for j, x in enumerate((-blocks[2 * p][...], blocks[2 * p + 1][:, :depth])):
+            for j, x in enumerate((-blocks[2 * p], blocks[2 * p + 1])):
                 at_j = slice(j * depth, (j + 1) * depth)
                 left_h[pl.ds(at, rows), at_j], left_l[pl.ds(at, rows), at_j] = halves(x)
         right = [jnp.concatenate([x[:, :width], x[:, width:]], 0) for x in (lower_h, lower_l)]
@@ -116,7 +133,7 @@
         kernel,
         grid=(1,),
         in_specs=[SMEM, SMEM]
-        + [fixed(x.shape) for x in blocks]
+        + [fixed(x.shape) for x in flat]
         + [fixed(lower[0].shape)] * 2
         + [fixed(pivot_inverse.shape)],
         out_specs=fixed((width, width)),
@@ -124,27 +141,29 @@
         scratch_shapes=[pltpu.VMEM((width, 2 * depth), BF16)] * 2,
         compiler_params=room(58),
         cost_estimate=QUICK,
-    )(place, weights, *blocks, *lower, pivot_inverse)
-
-
-def upper_products(place, weights, tile, blocks):
+    )(place, weights, *flat, *lower, pivot_inverse)
+
+
+def upper_products(place, weights, tile, blocks, n_groups):
     _, _, depth, cols = tile.shape
     rows = blocks[0].shape[0]
     n_col = len(blocks) // 2
+    flat, counts = flattened(blocks)
     width = n_col * rows
     steps = 3
     chunk = depth // steps
 
     def kernel(place, weights, tile, *refs):
-        blocks, refs = refs[: 2 * n_col], refs[2 * n_col :]
-        upper, left_h, left_l = refs
+        blocks, refs = refs[: len(flat)], refs[len(flat) :]
+        keep, send, left_h, left_l, upper = refs
         step = pl.program_id(0)
         w_re, w_im = weights[0, 0], weights[0, 1]
 
         def fill(combine):
+            held = loaded(blocks, counts, place[4], depth)
             for p in range(n_col):
                 at = pl.multiple_of(lax.rem(place[4] + p, n_col) * rows, 16)
-                for j, x in enumerate(combine(blocks[2 * p][...], blocks[2 * p + 1][:, :depth])):
+                for j, x in enumerate(combine(held[2 * p], held[2 * p + 1])):
                     at_j = slice(j * depth, (j + 1) * depth)
                     left_h[pl.ds(at, rows), at_j], left_l[pl.ds(at, rows), at_j] = halves(x)
 
@@ -156,19 +175,28 @@
         right = halves(jnp.concatenate([tile[0, 0], tile[0, 1]], 0))
         at = [pl.ds(pl.multiple_of(j * depth + step * chunk, 128), chunk) for j in range(2)]
         left = [jnp.concatenate([ref[:, at[0]], ref[:, at[1]]], 1) for ref in (left_h, left_l)]
-        upper[...] += product(left, right, INNER)
+        total = upper[...] + product(left, right, INNER)
+        upper[...] = total
+
+        @pl.when(step == steps - 1)
+        def _():
+            pairs = total.reshape(n_groups // 2, 2, width // n_groups, cols)
+            keep[...] = jnp.where(place[2] == 0, pairs[:, 0], pairs[:, 1])
+            send[...] = jnp.where(place[2] == 0, pairs[:, 1], pairs[:, 0])
+
+    part = (n_groups // 2, width // n_groups, cols)
 
     return pl.pallas_call(
         kernel,
         grid=(steps,),
         in_specs=[SMEM, SMEM, pl.BlockSpec((1, 2, chunk, cols), lambda i: (0, 0, i, 0))]
-        + [fixed(x.shape) for x in blocks],
-        out_specs=fixed((width, cols)),
-        out_shape=jax.ShapeDtypeStruct((width, cols), F32),
-        scratch_shapes=[pltpu.VMEM((width, 2 * depth), BF16)] * 2,
+        + [fixed(x.shape) for x in flat],
+        out_specs=[fixed(part)] * 2,
+        out_shape=[jax.ShapeDtypeStruct(part, F32)] * 2,
+        scratch_shapes=[pltpu.VMEM((width, 2 * depth), BF16)] * 2 + [pltpu.VMEM((width, cols), F32)],
         compiler_params=room(58),
         cost_estimate=QUICK,
-    )(place, weights, tile, *blocks)
+    )(place, weights, tile, *flat)
 
 
 def routing(place, block_owners, n_pole, n_row, n_col, capacity):
@@ -258,10 +286,10 @@
 
 
 def charge_terms_plain(place, source, rows, pivots, bases, ancestor):
-    n_pole, (n_rows, width) = len(rows), rows[0].shape
+    n_pole, (n_rows, width) = len(rows), rows[0][0].shape
     n_row, owners, slots, block_rows, points = ancestor.shape
     capacity = slots // n_pole
-    left = jnp.concatenate([sum(pivots)] + list(rows), 0)
+    left = jnp.concatenate([sum(pivots)] + [sum(x) for x in rows], 0)
     terms = []
     for at_row in range(n_row):
         basis = sum(jnp.where((place[3] ^ b) == at_row, x, 0.0) for b, x in bases.items())
@@ -279,9 +307,10 @@
 
 
 def charge_terms(place, source, rows, pivots, bases, ancestor):
-    n_pole, (n_rows, width) = len(rows), rows[0].shape
+    n_pole, (n_rows, width) = len(rows), rows[0][0].shape
     n_row, owners, slots, block_rows, points = ancestor.shape
     capacity = slots // n_pole
+    n_terms = len(rows[0])
     fold = bases[0].shape[2] // points
     if block_rows % 8:
         return charge_terms_plain(place, source, rows, pivots, bases, ancestor)
@@ -289,12 +318,13 @@
     n_groups = len(order)
 
     def kernel(place, source, *refs):
-        rows, pivots, refs = refs[:n_pole], refs[n_pole : 2 * n_pole], refs[2 * n_pole :]
+        rows, pivots, refs = refs[: n_pole * n_terms], refs[n_pole * n_terms :][:n_pole], refs[n_pole * (n_terms + 1) :]
+        rows = [sum(ref[...] for ref in rows[d * n_terms : (d + 1) * n_terms]) for d in range(n_pole)]
         ancestor, bases, (out, held) = refs[0], refs[1 : 1 + n_groups], refs[1 + n_groups :]
         pivot = pivots[0][...]
         for ref in pivots[1:]:
             pivot = pivot + ref[...]
-        left = halves(jnp.concatenate([pivot] + [ref[...] for ref in rows], 0))
+        left = halves(jnp.concatenate([pivot] + rows, 0))
         for g, b in enumerate(order):
             at_row = place[3] ^ b
             basis = jnp.concatenate(
@@ -321,13 +351,13 @@
 
     return pl.pallas_call(
         kernel,
-        in_specs=[SMEM, SMEM] + [VMEM] * (2 * n_pole + 1 + n_groups),
+        in_specs=[SMEM, SMEM] + [VMEM] * (n_pole * (n_terms + 1) + 1 + n_groups),
         out_specs=VMEM,
         out_shape=jax.ShapeDtypeStruct((n_row, owners, 1, points), F32),
         scratch_shapes=[pltpu.VMEM((n_pole * n_rows, owners * points), F32)],
         compiler_params=room(58),
         cost_estimate=QUICK,
-    )(place, source, *rows, *pivots, ancestor, *[bases[k] for k in order])
+    )(place, source, *[x for terms in rows for x in terms], *pivots, ancestor, *[bases[k] for k in order])
 
 
 def permute(x, axis, pairs):
@@ -368,10 +398,8 @@
     return [x, one, (leftward, rightward), three]
 
 
-def joined(blocks, axis, *ready):
-    return [
-        jnp.where(lax.axis_index(axis) < 2, after(x[0], *ready), x[1]) if isinstance(x, tuple) else x for x in blocks
-    ]
+def joined(blocks, axis):
+    return [jnp.where(lax.axis_index(axis) < 2, x[0], x[1]) if isinstance(x, tuple) else x for x in blocks]
 
 
 def reduce_scatter_swapped(x, axis, masks):
@@ -397,23 +425,35 @@
     return lax.optimization_barrier((x,) + others)[0]
 
 
-def halving(x, axis, before, later):
-    n = lax.axis_size(axis)
-    me = lax.axis_index(axis)
-    held = [pick(x, me ^ d) for d in range(n)]
+def swap_both(x, axes, masks):
+    first, second = (lax.axis_size(a) for a in axes)
+    pairs = [
+        (i * second + j, (i ^ masks[0]) * second + (j ^ masks[1])) for i in range(first) for j in range(second)
+    ]
+    return lax.ppermute(x, axes, pairs)
+
+
+def rows_by_pole(x, before, later):
+    n_pole, n_col = lax.axis_size("pole"), lax.axis_size("col")
+    me = lax.axis_index("col")
+    held = [pick(x, me ^ d) for d in range(n_col)]
     bit = 1
-    while bit < n:
-        away = [d for d in range(0, n, bit) if d & bit]
-        out = jnp.stack([held[d] for d in away])
-        if bit == 2:
-            later = after(later, out)
-        arrived = swap(out, axis, bit)
+    while bit < n_col:
+        away = [d for d in range(0, n_col, bit) if d & bit]
+        if bit == 2 and n_col == 4:
+            mine, other = held[0], held[2]
+            later = after(later, other)
+            rows = [[mine, swap(other, "col", 2)]]
+            for d in range(1, n_pole):
+                rows.append([swap(mine, "pole", d), swap_both(other, ("pole", "col"), (d, 2))])
+            return rows, later
+        arrived = swap(jnp.stack([held[d] for d in away]), "col", bit)
         if bit == 1:
             arrived = after(arrived, *before)
         for j, d in enumerate(away):
             held[d ^ bit] = held[d ^ bit] + arrived[j]
         bit *= 2
-    return held[0], later
+    return [[held[0]]] + [[swap(held[0], "pole", d)] for d in range(1, n_pole)], later
 
 
 def body(
@@ -458,41 +498,40 @@
         gather_cyclic(upper_own[0], upper_near[0], "col"),
         gather_cyclic(upper_own[1], [after(x, parts[0]) for x in upper_near[1]], "col"),
     ]
+    ancestor = lax.all_to_all(
+        after(ancestor, parts[0], upper_near[1][-1]), ("row", "col"), split_axis=0, concat_axis=0, tiled=True
+    ).reshape(n_row, n_col, -1, block_rows, points)
     half = reduce_scatter_swapped(parts, "pole", list(range(1, n_pole)))
-    upper[1] = joined(upper[1], "col")
-    ancestor = lax.all_to_all(
-        after(ancestor, upper[1][n_col // 2]), ("row", "col"), split_axis=0, concat_axis=0, tiled=True
-    ).reshape(n_row, n_col, -1, block_rows, points)
-
-    line = jnp.stack([x[:, tile_rows:] for x in upper[1]])
+
+    line = jnp.stack(joined([jax.tree.map(lambda y: y[:, tile_rows:], x) for x in upper[1]], "col"))
     bases = {b: swap(line, "row", b) if b else line for b in range(0, n_row, 2)}
-    upper[0] = joined(upper[0], "col", half)
     upper = [x for pair in zip(*upper, strict=True) for x in pair]
 
-    pivot = pivot_term(place, pole_weights, upper, beside, pivot_inverse)
+    pivot = pivot_term(place, pole_weights, upper, beside, after(pivot_inverse, half))
     pivots = [pivot] + [swap(pivot, "pole", d) for d in range(1, n_pole)]
-    product_upper = upper_products(place, after(pole_weights, pivot), inverse_tile, upper)
+    keep, send = upper_products(place, after(pole_weights, pivot), inverse_tile, upper, n_pole * n_row)
     for b in list(bases):
         bases[b + 1] = swap(bases[b], "row", 1)
-    rows, product_upper = halving(half.reshape(n_col, rows_here, width), "col", (product_upper, pivots[-1]), product_upper)
-    rows = [rows] + [swap(rows, "pole", d) for d in range(1, n_pole)]
-    arrived = lax.all_to_all(
-        product_upper.reshape(n_pole * n_row, -1, tile_cols),
-        ("pole", "row"),
-        split_axis=0,
-        concat_axis=0,
-        tiled=True,
-    )
+    rows, send = rows_by_pole(half.reshape(n_col, rows_here, width), (keep,), send)
+    near = (keep + swap(send, "row", 1)).reshape(n_pole, n_row // 2, -1, tile_cols)
+    upper_density, arrived = 0.0, []
+    for a in range(n_pole):
+        for b in range(n_row // 2):
+            part = pick(pick(near, pole ^ a), (row // 2) ^ b)
+            if a or b:
+                arrived.append(swap_both(part, ("pole", "row"), (a, 2 * b)))
+            else:
+                upper_density = part
 
     terms = charge_terms(place, source, rows, pivots, bases, ancestor)
     terms = lax.all_to_all(
-        after(terms, arrived).reshape(n_row * n_col, 1, points),
+        after(terms, *arrived).reshape(n_row * n_col, 1, points),
         ("row", "col"),
         split_axis=0,
         concat_axis=0,
         tiled=True,
     )
-    return (jnp.sum(arrived, 0), jnp.sum(terms, (0, 1)))
+    return (upper_density + sum(arrived), jnp.sum(terms, (0, 1)))
 
 
 def solution(mesh):

time: 132 us -> 123 us (0.932)
  waiting for transfers between devices: 40.3 us -> 18.7 us
  starting transfers between devices: 38.4 us -> 54.6 us
  local copies, waits for them, and re-layouts: 7.07 us -> 4.39 us
  other arithmetic: 6.5 us -> 4.49 us
    ppermute x11 -> x12, waiting for transfers between devices: 13.1 us -> 0.03 us  [swap(): lax.ppermute(x, axis, [(i, i ^ mask) for i in range(lax.axis_size(axis))])]
    ppermute x4, waiting for transfers between devices: 11.6 us -> 2.07 us  [permute(): return lax.ppermute(x, axis, pairs)]
    ppermute x0 -> x4, starting transfers between devices: none -> 9.46 us  [swap_both(): return lax.ppermute(x, axes, pairs)]
    ppermute x11 -> x12, starting transfers between devices: 13.3 us -> 20.4 us  [swap(): lax.ppermute(x, axis, [(i, i ^ mask) for i in range(lax.axis_size(axis))])]
    ppermute x0 -> x4, waiting for transfers between devices: none -> 3.16 us  [swap_both(): return lax.ppermute(x, axes, pairs)]
    another operation x4 -> x2, local copies, waits for them, and re-layouts: 2.95 us -> 0.07 us  [body(): jnp.stack(joined([jax.tree.map(lambda y: y[:, tile_rows:], x) for x in up...]
    select_n x2 -> x0, other arithmetic: 2.54 us -> none  [joined(): jnp.where(lax.axis_index(axis) < 2, after(x[0], *ready), x[1])]
    ppermute x4, waiting for transfers between devices: 9.97 us -> 7.83 us  [shift(): return lax.ppermute(x, axis, [(i, (i + by) % n) for i in range(n)])]
  transfers between devices with their start and end apart: 22 -> 26, of which waited for: 7 -> 5; matrix products, arithmetic and copies ran while one was open for 8% -> 5% of each run, Pallas kernels for 29% -> 32%
where the time goes in v3:
time: 123 us; the launch traced here: 122 us
  starting transfers between devices  54.6 us (44%)
  Pallas kernels  38.8 us (32%)
  waiting for transfers between devices  18.7 us (15%)
  other arithmetic  4.49 us (4%)
  local copies, waits for them, and re-layouts  4.39 us (4%)
    ppermute x12, starting transfers between devices, swap(): lax.ppermute(x, axis, [(i, i ^ mask) for i in range(lax.axis_size(axis))])  20.4 us
    pallas_call x1, Pallas kernels, lower_products(): pl.pallas_call(kernel, grid=(steps,), in_specs=[SMEM, SMEM, pl.BlockSpec(...  13.9 us
    all_to_all x1, starting transfers between devices, body(): lax.all_to_all(after(ancestor, parts[0], upper_near[1][-1]), ('row', 'col...  10.8 us
    pallas_call x1, Pallas kernels, upper_products(): pl.pallas_call(kernel, grid=(steps,), in_specs=[SMEM, SMEM, pl.BlockSpec(...  10.5 us
    ppermute x4, starting transfers between devices, swap_both(): return lax.ppermute(x, axes, pairs)  9.46 us
    ppermute x4, waiting for transfers between devices, shift(): return lax.ppermute(x, axis, [(i, (i + by) % n) for i in range(n)])  7.83 us
    ppermute x4, starting transfers between devices, shift(): return lax.ppermute(x, axis, [(i, (i + by) % n) for i in range(n)])  5.74 us
    all_to_all x1, waiting for transfers between devices, body(): lax.all_to_all(after(terms, *arrived).reshape(n_row * n_col, 1, points),...  5.62 us
  transfers between devices with their start and end apart: 26, of which 5 were waited for; matrix products, arithmetic and copies ran while one was open for 5% of the time, Pallas kernels for 32%

profile of v3, /device:TPU:0, one launch (start us, length us, event | category | flops | bytes accessed | tf_op | source)
XLA Modules:
  0.0 122.0 jit_solution(37037571329993926)
XLA Ops:
  0.6 3.0 %collective-permute-start.3 = (f32[2,64,1152]{2,1,0:T(8,128)}, f32[2,64,1152]{2,1,0:T(8,128)}, u32[]{:S(2)}, u32[]{:S(2)}) collective-permute-start(f32[2,64,1152]{2,1,0:T(8,128)} %bitcast.54), channel_id=1, source_target_pairs={{0,8},{4,12},{8,0},{12,4},{1,9},{5,13},{9,1},{13,5},{2,10},{6,14},... | collective-permute-start | bytes 1769480 | tf_op jit(solution)/shard_map/ppermute | solution.py:368
  4.8 3.7 %collective-permute-start = (f32[64,1152]{1,0:T(8,128)S(1)}, f32[64,1152]{1,0:T(8,128)S(1)}, u32[]{:S(2)}, u32[]{:S(2)}) collective-permute-start(f32[64,1152]{1,0:T(8,128)S(1)} %get-tuple-element.44.refs_0_), channel_id=1, source_target_pairs={{0,3},{1,0},{2,1},{3,2},{4,7},{5,4},{6,5},{7,6},{8,11},{9,8},{10,9... | collective-permute-start | bytes 884744 | tf_op jit(solution)/shard_map/ppermute | solution.py:373
  9.1 1.9 %shard_map.95 = (s32[8,128]{1,0:T(8,128)}, s32[2,16,128]{2,1,0:T(8,128)}) custom-call(s32[7]{0:T(128)} %stack.48.place, s32[6,576]{1,0:T(8,128)} %bitcast.60), custom_call_target="tpu_custom_call" | custom-call | tf_op jit(solution)/shard_map/pallas_call | solution.py:255
  11.0 2.8 %shard_map.96 = f32[16,8,8,128]{3,2,1,0:T(8,128)} custom-call(s32[7]{0:T(128)} %stack.48.place, s32[8,128]{1,0:T(8,128)} %get-tuple-element.19.slots, f32[576,8,128]{2,1,0:T(8,128)} %bitcast.50), custom_call_target="tpu_custom_call" | custom-call | tf_op jit(solution)/shard_map/pallas_call | solution.py:279
  13.8 2.1 %collective-permute-done.refs_2_ = f32[64,1152]{1,0:T(8,128)S(1)} collective-permute-done((f32[64,1152]{1,0:T(8,128)S(1)}, f32[64,1152]{1,0:T(8,128)S(1)}, u32[]{:S(2)}, u32[]{:S(2)}) %collective-permute-start) | collective-permute-done | bytes 294944 | tf_op jit(solution)/shard_map/ppermute | solution.py:373
  15.9 5.8 %collective-permute-done.4.refs_8_ = f32[64,1152]{1,0:T(8,128)S(1)} collective-permute-done((f32[64,1152]{1,0:T(8,128)S(1)}, f32[64,1152]{1,0:T(8,128)S(1)}, u32[]{:S(2)}, u32[]{:S(2)}) %collective-permute-start.4) | collective-permute-done | bytes 294944 | tf_op jit(solution)/shard_map/ppermute | solution.py:373
  21.8 1.8 %collective-permute-start.1 = (f32[64,1664]{1,0:T(8,128)S(1)}, f32[64,1664]{1,0:T(8,128)S(1)}, u32[]{:S(2)}, u32[]{:S(2)}) collective-permute-start(f32[64,1664]{1,0:T(8,128)S(1)} %pad_maximum_fusion.1.refs_1_), channel_id=1, source_target_pairs={{0,3},{1,0},{2,1},{3,2},{4,7},{5,4},{6,5},{7,6},{8,11},{9,8},{10,9... | collective-permute-start | bytes 1277960 | tf_op jit(solution)/shard_map/ppermute | solution.py:373
  24.7 13.9 %shard_map.97 = (f32[576,256]{1,0:T(8,128)}, f32[576,256]{1,0:T(8,128)}, bf16[1152,512]{1,0:T(8,128)(2,1)}, bf16[1152,512]{1,0:T(8,128)(2,1)}) custom-call(s32[7]{0:T(128)} %stack.48.place, f32[1,2]{1,0:T(1,128)} %weights.4, f32[1,2,1152,1152]{3,2,1,0:T(8,128)} %tile.3, f32[2,64,1152]{2,1,0:T(8,128)} %bitcast.56, ...), custom_call_target="tpu_custom_call" | custom-call | tf_op jit(solution)/shard_map/pallas_call | solution.py:76
  38.6 1.6 %collective-permute-start.11 = (f32[576,256]{1,0:T(8,128)}, f32[576,256]{1,0:T(8,128)}, u32[]{:S(2)}, u32[]{:S(2)}) collective-permute-start(f32[576,256]{1,0:T(8,128)} %get-tuple-element.26), channel_id=1, source_target_pairs={{0,16},{16,0},{1,17},{17,1},{2,18},{18,2},{3,19},{19,3},{4,20},{20... | collective-permute-start | bytes 1769480 | tf_op jit(solution)/shard_map/ppermute | solution.py:368
  41.6 1.4 %collective-permute-start.7 = (f32[64,1152]{1,0:T(8,128)S(1)}, f32[64,1152]{1,0:T(8,128)}, u32[]{:S(2)}, u32[]{:S(2)}) collective-permute-start(f32[64,1152]{1,0:T(8,128)S(1)} %collective-permute-done.4.refs_8_), channel_id=1, source_target_pairs={{1,2},{2,3},{5,6},{6,7},{9,10},{10,11},{13,14},{14,15},{17,18},{18... | collective-permute-start | bytes 884744 | tf_op jit(solution)/shard_map/ppermute | solution.py:364
  45.0 10.8 %all-to-all-start = ((f32[16,8,8,128]{3,2,1,0:T(8,128)}), f32[16,8,8,128]{3,2,1,0:T(8,128)S(1)}, u32[]{:S(2)}, u32[]{:S(2)}) async-start(f32[16,8,8,128]{3,2,1,0:T(8,128)} %shard_map.96), calls=%async_computation | async-start | bytes 1048576 | tf_op jit(solution)/shard_map/all_to_all | solution.py:501
  55.9 1.3 %add.95 = f32[576,256]{1,0:T(8,128)S(1)} add(f32[576,256]{1,0:T(8,128)} %get-tuple-element.21, f32[576,256]{1,0:T(8,128)} %collective-permute-done.11) | non-fusion elementwise | flops 147456 | bytes 1769472 | tf_op jit(solution)/shard_map/add | solution.py:408
  57.3 2.2 %collective-permute-start.12 = (f32[2,144,256]{2,1,0:T(8,128)S(1)}, f32[2,144,256]{2,1,0:T(8,128)S(1)}, u32[]{:S(2)}, u32[]{:S(2)}) collective-permute-start(f32[2,144,256]{2,1,0:T(8,128)S(1)} %pad_maximum_fusion.2), channel_id=1, source_target_pairs={{0,1},{1,0},{2,3},{3,2},{4,5},{5,4},{6,7},{7,6},{8,9},{9,8},{10,11... | collective-permute-start | bytes 884744 | tf_op jit(solution)/shard_map/ppermute | solution.py:368
  59.4 2.1 %collective-permute-done.8.refs_6_ = f32[64,1664]{1,0:T(8,128)S(1)} collective-permute-done((f32[64,1664]{1,0:T(8,128)S(1)}, f32[64,1664]{1,0:T(8,128)S(1)}, u32[]{:S(2)}, u32[]{:S(2)}) %collective-permute-start.8) | collective-permute-done | bytes 426016 | tf_op jit(solution)/shard_map/ppermute | solution.py:364
  62.6 5.0 %shard_map.98.refs_4_ = f32[256,256]{1,0:T(8,128)} custom-call(s32[7]{0:T(128)} %stack.48.place, f32[1,2]{1,0:T(1,128)} %weights.4, f32[64,1152]{1,0:T(8,128)} %copy-done.1, f32[64,1664]{1,0:T(8,128)} %copy-done, f32[64,1152]{1,0:T(8,128)} %copy-done.8, f32[64,1664]{1,0:T(8,128)} %copy-done.2, f32[64,1152]{1,0:T(8,128)} %copy-done.10, ...), custom_call_target="tpu_custom_call" | custom-call | tf_op jit(solution)/shard_map/pallas_call | solution.py:132
  67.6 10.5 %shard_map.99 = (f32[4,32,1152]{2,1,0:T(8,128)}, f32[4,32,1152]{2,1,0:T(8,128)}) custom-call(s32[7]{0:T(128)} %stack.48.place, f32[1,2]{1,0:T(1,128)} %weights.4, f32[1,2,1152,1152]{3,2,1,0:T(8,128)} %tile.3, f32[64,1152]{1,0:T(8,128)} %copy-done.1, f32[64,1664]{1,0:T(8,128)} %copy-done, f32[64,1152]{1,0:T(8,128)} %copy-done.8, f32[64,1664]{1,0:T(8,128)} %copy-done.2, ...), custom_call_target="tpu_custom_call" | custom-call | tf_op jit(solution)/shard_map/pallas_call | solution.py:189
  80.0 11.0 %collective-permute-start.17 = (f32[144,256]{1,0:T(8,128)}, f32[144,256]{1,0:T(8,128)S(1)}, u32[]{:S(2)}, u32[]{:S(2)}) collective-permute-start(f32[144,256]{1,0:T(8,128)} %get-tuple-element.37), channel_id=1, source_target_pairs={{0,2},{1,3},{2,0},{3,1},{4,6},{5,7},{6,4},{7,5},{8,10},{9,11},{10,... | collective-permute-start | bytes 442376 | tf_op jit(solution)/shard_map/ppermute | solution.py:368
  90.9 1.5 %collective-permute-start.18 = (f32[144,256]{1,0:T(8,128)S(1)}, f32[144,256]{1,0:T(8,128)S(1)}, u32[]{:S(2)}, u32[]{:S(2)}) collective-permute-start(f32[144,256]{1,0:T(8,128)S(1)} %get-tuple-element.36.refs_0_), channel_id=1, source_target_pairs={{0,16},{16,0},{1,17},{17,1},{2,18},{18,2},{3,19},{19,3},{4,20},{20... | collective-permute-start | bytes 442376 | tf_op jit(solution)/shard_map/ppermute | solution.py:368
  93.6 6.0 %collective-permute-start.19 = (f32[144,256]{1,0:T(8,128)}, f32[144,256]{1,0:T(8,128)S(1)}, u32[]{:S(2)}, u32[]{:S(2)}) collective-permute-start(f32[144,256]{1,0:T(8,128)} %get-tuple-element.37), channel_id=1, source_target_pairs={{0,18},{1,19},{2,16},{3,17},{16,2},{17,3},{18,0},{19,1},{4,22},{5,... | collective-permute-start | bytes 442376 | tf_op jit(solution)/shard_map/ppermute | solution.py:433
  99.6 2.5 %collective-permute-start.16 = (f32[32,1152]{1,0:T(8,128)S(1)}, f32[32,1152]{1,0:T(8,128)S(1)}, u32[]{:S(2)}, u32[]{:S(2)}) collective-permute-start(f32[32,1152]{1,0:T(8,128)S(1)} %get-tuple-element.39), channel_id=1, source_target_pairs={{0,24},{4,28},{8,16},{12,20},{16,8},{20,12},{24,0},{28,4},{1,25},{... | collective-permute-start | bytes 442376 | tf_op jit(solution)/shard_map/ppermute | solution.py:433
  103.1 3.2 %collective-permute-done.19.refs_3_ = f32[144,256]{1,0:T(8,128)S(1)} collective-permute-done((f32[144,256]{1,0:T(8,128)}, f32[144,256]{1,0:T(8,128)S(1)}, u32[]{:S(2)}, u32[]{:S(2)}) %collective-permute-start.19) | collective-permute-done | bytes 147488 | tf_op jit(solution)/shard_map/ppermute | solution.py:433
  106.9 4.7 %shard_map.100 = f32[4,4,1,128]{3,2,1,0:T(1,128)} custom-call(s32[7]{0:T(128)} %stack.48.place, s32[2,16,128]{2,1,0:T(8,128)} %get-tuple-element.33.source, f32[144,256]{1,0:T(8,128)} %copy-done.13, f32[144,256]{1,0:T(8,128)} %copy-done.15, f32[144,256]{1,0:T(8,128)} %copy-done.16, f32[144,256]{1,0:T(8,128)} %copy-done.17, f32[256,256]{1,0:T(8,128)} %shard_map.98.refs_4_, ...), custom_call_target="tpu_custom_call" | custom-call | tf_op jit(solution)/shard_map/pallas_call | solution.py:352
  111.7 3.5 %all-to-all-start.1 = ((f32[16,1,128]{2,1,0:T(1,128)}), f32[16,1,128]{2,1,0:T(1,128)S(1)}, u32[]{:S(2)}, u32[]{:S(2)}) async-start(f32[16,1,128]{2,1,0:T(1,128)} %bitcast.59), calls=%async_computation.1 | async-start | bytes 16384 | tf_op jit(solution)/shard_map/all_to_all | solution.py:527
  115.8 5.6 %all-to-all-done.1 = f32[16,1,128]{2,1,0:T(1,128)S(1)} async-done(((f32[16,1,128]{2,1,0:T(1,128)}), f32[16,1,128]{2,1,0:T(1,128)S(1)}, u32[]{:S(2)}, u32[]{:S(2)}) %all-to-all-start.1) | async-done | bytes 8224 | tf_op jit(solution)/shard_map/all_to_all | solution.py:527
  (89 shorter events, 13.4 us)
Async XLA Ops:
  0.6 21.0 %collective-permute-start.3 = (f32[2,64,1152]{2,1,0:T(8,128)}, f32[2,64,1152]{2,1,0:T(8,128)}, u32[]{:S(2)}, u32[]{:S(2)}) collective-permute-start(f32[2,64,1152]{2,1,0:T(8,128)} %bitcast.54), channel_id=1, source_target_pairs={{0,8},{4,12},{8,0},{12,4},{1,9},{5,13},{9,1},{13,5},{2,10},{6,14},... | collective-permute-start | bytes 1769480 | tf_op jit(solution)/shard_map/ppermute | solution.py:368
  4.8 11.1 %collective-permute-start = (f32[64,1152]{1,0:T(8,128)S(1)}, f32[64,1152]{1,0:T(8,128)S(1)}, u32[]{:S(2)}, u32[]{:S(2)}) collective-permute-start(f32[64,1152]{1,0:T(8,128)S(1)} %get-tuple-element.44.refs_0_), channel_id=1, source_target_pairs={{0,3},{1,0},{2,1},{3,2},{4,7},{5,4},{6,5},{7,6},{8,11},{9,8},{10,9... | collective-permute-start | bytes 884744 | tf_op jit(solution)/shard_map/ppermute | solution.py:373
  8.4 13.2 %collective-permute-start.4 = (f32[64,1152]{1,0:T(8,128)S(1)}, f32[64,1152]{1,0:T(8,128)S(1)}, u32[]{:S(2)}, u32[]{:S(2)}) collective-permute-start(f32[64,1152]{1,0:T(8,128)S(1)} %get-tuple-element.44.refs_0_), channel_id=1, source_target_pairs={{0,1},{1,2},{2,3},{3,0},{4,5},{5,6},{6,7},{7,4},{8,9},{9,10},{10,1... | collective-permute-start | bytes 884744 | tf_op jit(solution)/shard_map/ppermute | solution.py:373
  8.4 15.5 %collective-permute-start.2 = (f32[2,64,1152]{2,1,0:T(8,128)}, f32[2,64,1152]{2,1,0:T(8,128)}, u32[]{:S(2)}, u32[]{:S(2)}) collective-permute-start(f32[2,64,1152]{2,1,0:T(8,128)} %bitcast.55), channel_id=1, source_target_pairs={{0,4},{4,0},{8,12},{12,8},{1,5},{5,1},{9,13},{13,9},{2,6},{6,2},{1... | collective-permute-start | bytes 1769480 | tf_op jit(solution)/shard_map/ppermute | solution.py:368
  21.8 21.2 %collective-permute-start.1 = (f32[64,1664]{1,0:T(8,128)S(1)}, f32[64,1664]{1,0:T(8,128)S(1)}, u32[]{:S(2)}, u32[]{:S(2)}) collective-permute-start(f32[64,1664]{1,0:T(8,128)S(1)} %pad_maximum_fusion.1.refs_1_), channel_id=1, source_target_pairs={{0,3},{1,0},{2,1},{3,2},{4,7},{5,4},{6,5},{7,6},{8,11},{9,8},{10,9... | collective-permute-start | bytes 1277960 | tf_op jit(solution)/shard_map/ppermute | solution.py:373
  23.6 20.7 %collective-permute-start.9 = (f32[64,1664]{1,0:T(8,128)S(1)}, f32[64,1664]{1,0:T(8,128)S(1)}, u32[]{:S(2)}, u32[]{:S(2)}) collective-permute-start(f32[64,1664]{1,0:T(8,128)S(1)} %pad_maximum_fusion.1.refs_1_), channel_id=1, source_target_pairs={{0,1},{1,2},{2,3},{3,0},{4,5},{5,6},{6,7},{7,4},{8,9},{9,10},{10,1... | collective-permute-start | bytes 1277960 | tf_op jit(solution)/shard_map/ppermute | solution.py:373
  38.6 17.2 %collective-permute-start.11 = (f32[576,256]{1,0:T(8,128)}, f32[576,256]{1,0:T(8,128)}, u32[]{:S(2)}, u32[]{:S(2)}) collective-permute-start(f32[576,256]{1,0:T(8,128)} %get-tuple-element.26), channel_id=1, source_target_pairs={{0,16},{16,0},{1,17},{17,1},{2,18},{18,2},{3,19},{19,3},{4,20},{20... | collective-permute-start | bytes 1769480 | tf_op jit(solution)/shard_map/ppermute | solution.py:368
  40.3 21.4 %collective-permute-start.6 = (f32[64,1152]{1,0:T(8,128)S(1)}, f32[64,1152]{1,0:T(8,128)S(1)}, u32[]{:S(2)}, u32[]{:S(2)}) collective-permute-start(f32[64,1152]{1,0:T(8,128)S(1)} %collective-permute-done.refs_2_), channel_id=1, source_target_pairs={{2,1},{1,0},{6,5},{5,4},{10,9},{9,8},{14,13},{13,12},{18,17},{17,1... | collective-permute-start | bytes 884744 | tf_op jit(solution)/shard_map/ppermute | solution.py:364
  41.6 20.1 %collective-permute-start.7 = (f32[64,1152]{1,0:T(8,128)S(1)}, f32[64,1152]{1,0:T(8,128)}, u32[]{:S(2)}, u32[]{:S(2)}) collective-permute-start(f32[64,1152]{1,0:T(8,128)S(1)} %collective-permute-done.4.refs_8_), channel_id=1, source_target_pairs={{1,2},{2,3},{5,6},{6,7},{9,10},{10,11},{13,14},{14,15},{17,18},{18... | collective-permute-start | bytes 884744 | tf_op jit(solution)/shard_map/ppermute | solution.py:364
  43.0 18.5 %collective-permute-start.8 = (f32[64,1664]{1,0:T(8,128)S(1)}, f32[64,1664]{1,0:T(8,128)S(1)}, u32[]{:S(2)}, u32[]{:S(2)}) collective-permute-start(f32[64,1664]{1,0:T(8,128)S(1)} %collective-permute-done.1.refs_3_), channel_id=1, source_target_pairs={{2,1},{1,0},{6,5},{5,4},{10,9},{9,8},{14,13},{13,12},{18,17},{17,1... | collective-permute-start | bytes 1277960 | tf_op jit(solution)/shard_map/ppermute | solution.py:364
  44.3 17.2 %collective-permute-start.10 = (f32[64,1664]{1,0:T(8,128)S(1)}, f32[64,1664]{1,0:T(8,128)S(1)}, u32[]{:S(2)}, u32[]{:S(2)}) collective-permute-start(f32[64,1664]{1,0:T(8,128)S(1)} %collective-permute-done.9.refs_9_), channel_id=1, source_target_pairs={{1,2},{2,3},{5,6},{6,7},{9,10},{10,11},{13,14},{14,15},{17,18},{18... | collective-permute-start | bytes 1277960 | tf_op jit(solution)/shard_map/ppermute | solution.py:364
  45.0 58.1 %all-to-all-start = ((f32[16,8,8,128]{3,2,1,0:T(8,128)}), f32[16,8,8,128]{3,2,1,0:T(8,128)S(1)}, u32[]{:S(2)}, u32[]{:S(2)}) async-start(f32[16,8,8,128]{3,2,1,0:T(8,128)} %shard_map.96), calls=%async_computation | async-start | bytes 1048576 | tf_op jit(solution)/shard_map/all_to_all | solution.py:501
  57.3 20.8 %collective-permute-start.12 = (f32[2,144,256]{2,1,0:T(8,128)S(1)}, f32[2,144,256]{2,1,0:T(8,128)S(1)}, u32[]{:S(2)}, u32[]{:S(2)}) collective-permute-start(f32[2,144,256]{2,1,0:T(8,128)S(1)} %pad_maximum_fusion.2), channel_id=1, source_target_pairs={{0,1},{1,0},{2,3},{3,2},{4,5},{5,4},{6,7},{7,6},{8,9},{9,8},{10,11... | collective-permute-start | bytes 884744 | tf_op jit(solution)/shard_map/ppermute | solution.py:368
  61.6 17.7 %collective-permute-start.22 = (f32[4,64,512]{2,1,0:T(8,128)S(1)}, f32[4,64,512]{2,1,0:T(8,128)}, u32[]{:S(2)}, u32[]{:S(2)}) collective-permute-start(f32[4,64,512]{2,1,0:T(8,128)S(1)} %pad_maximum_fusion.refs_7_), channel_id=1, source_target_pairs={{0,8},{4,12},{8,0},{12,4},{1,9},{5,13},{9,1},{13,5},{2,10},{6,14},... | collective-permute-start | bytes 1572872 | tf_op jit(solution)/shard_map/ppermute | solution.py:368
  78.8 12.1 %collective-permute-start.13 = (f32[4,32,1152]{2,1,0:T(8,128)}, f32[4,32,1152]{2,1,0:T(8,128)S(1)}, u32[]{:S(2)}, u32[]{:S(2)}) collective-permute-start(f32[4,32,1152]{2,1,0:T(8,128)} %get-tuple-element.32), channel_id=1, source_target_pairs={{0,4},{4,0},{8,12},{12,8},{1,5},{5,1},{9,13},{13,9},{2,6},{6,2},{1... | collective-permute-start | bytes 1769480 | tf_op jit(solution)/shard_map/ppermute | solution.py:368
  78.8 20.8 %collective-permute-start.21 = (f32[4,64,512]{2,1,0:T(8,128)S(1)}, f32[4,64,512]{2,1,0:T(8,128)S(1)}, u32[]{:S(2)}, u32[]{:S(2)}) collective-permute-start(f32[4,64,512]{2,1,0:T(8,128)S(1)} %pad_maximum_fusion.refs_7_), channel_id=1, source_target_pairs={{0,4},{4,0},{8,12},{12,8},{1,5},{5,1},{9,13},{13,9},{2,6},{6,2},{1... | collective-permute-start | bytes 1572872 | tf_op jit(solution)/shard_map/ppermute | solution.py:368
  79.3 26.9 %collective-permute-start.23 = (f32[4,64,512]{2,1,0:T(8,128)}, f32[4,64,512]{2,1,0:T(8,128)}, u32[]{:S(2)}, u32[]{:S(2)}) collective-permute-start(f32[4,64,512]{2,1,0:T(8,128)} %collective-permute-done.22.refs_9_), channel_id=1, source_target_pairs={{0,4},{4,0},{8,12},{12,8},{1,5},{5,1},{9,13},{13,9},{2,6},{6,2},{1... | collective-permute-start | bytes 1572872 | tf_op jit(solution)/shard_map/ppermute | solution.py:368
  79.4 14.2 %collective-permute-start.20 = (f32[256,256]{1,0:T(8,128)S(1)}, f32[256,256]{1,0:T(8,128)}, u32[]{:S(2)}, u32[]{:S(2)}) collective-permute-start(f32[256,256]{1,0:T(8,128)S(1)} %copy-done.11), channel_id=1, source_target_pairs={{0,16},{16,0},{1,17},{17,1},{2,18},{18,2},{3,19},{19,3},{4,20},{20... | collective-permute-start | bytes 786440 | tf_op jit(solution)/shard_map/ppermute | solution.py:368
  80.0 22.1 %collective-permute-start.17 = (f32[144,256]{1,0:T(8,128)}, f32[144,256]{1,0:T(8,128)S(1)}, u32[]{:S(2)}, u32[]{:S(2)}) collective-permute-start(f32[144,256]{1,0:T(8,128)} %get-tuple-element.37), channel_id=1, source_target_pairs={{0,2},{1,3},{2,0},{3,1},{4,6},{5,7},{6,4},{7,5},{8,10},{9,11},{10,... | collective-permute-start | bytes 442376 | tf_op jit(solution)/shard_map/ppermute | solution.py:368
  90.9 11.6 %collective-permute-start.18 = (f32[144,256]{1,0:T(8,128)S(1)}, f32[144,256]{1,0:T(8,128)S(1)}, u32[]{:S(2)}, u32[]{:S(2)}) collective-permute-start(f32[144,256]{1,0:T(8,128)S(1)} %get-tuple-element.36.refs_0_), channel_id=1, source_target_pairs={{0,16},{16,0},{1,17},{17,1},{2,18},{18,2},{3,19},{19,3},{4,20},{20... | collective-permute-start | bytes 442376 | tf_op jit(solution)/shard_map/ppermute | solution.py:368
  93.6 12.6 %collective-permute-start.19 = (f32[144,256]{1,0:T(8,128)}, f32[144,256]{1,0:T(8,128)S(1)}, u32[]{:S(2)}, u32[]{:S(2)}) collective-permute-start(f32[144,256]{1,0:T(8,128)} %get-tuple-element.37), channel_id=1, source_target_pairs={{0,18},{1,19},{2,16},{3,17},{16,2},{17,3},{18,0},{19,1},{4,22},{5,... | collective-permute-start | bytes 442376 | tf_op jit(solution)/shard_map/ppermute | solution.py:433
  99.6 12.0 %collective-permute-start.16 = (f32[32,1152]{1,0:T(8,128)S(1)}, f32[32,1152]{1,0:T(8,128)S(1)}, u32[]{:S(2)}, u32[]{:S(2)}) collective-permute-start(f32[32,1152]{1,0:T(8,128)S(1)} %get-tuple-element.39), channel_id=1, source_target_pairs={{0,24},{4,28},{8,16},{12,20},{16,8},{20,12},{24,0},{28,4},{1,25},{... | collective-permute-start | bytes 442376 | tf_op jit(solution)/shard_map/ppermute | solution.py:433
  102.1 9.6 %collective-permute-start.14 = (f32[32,1152]{1,0:T(8,128)S(1)}, f32[32,1152]{1,0:T(8,128)S(1)}, u32[]{:S(2)}, u32[]{:S(2)}) collective-permute-start(f32[32,1152]{1,0:T(8,128)S(1)} %get-tuple-element.40), channel_id=1, source_target_pairs={{0,8},{4,12},{8,0},{12,4},{16,24},{20,28},{24,16},{28,20},{1,9},{5... | collective-permute-start | bytes 442376 | tf_op jit(solution)/shard_map/ppermute | solution.py:433
  111.7 9.8 %all-to-all-start.1 = ((f32[16,1,128]{2,1,0:T(1,128)}), f32[16,1,128]{2,1,0:T(1,128)S(1)}, u32[]{:S(2)}, u32[]{:S(2)}) async-start(f32[16,1,128]{2,1,0:T(1,128)} %bitcast.59), calls=%async_computation.1 | async-start | bytes 16384 | tf_op jit(solution)/shard_map/all_to_all | solution.py:527
  (21 other events, 241.6 us)

commit v4 on v3

--- a/solution.py
+++ b/solution.py
@@ -139,7 +139,7 @@
         out_specs=fixed((width, width)),
         out_shape=jax.ShapeDtypeStruct((width, width), F32),
         scratch_shapes=[pltpu.VMEM((width, 2 * depth), BF16)] * 2,
-        compiler_params=room(58),
+        compiler_params=room(24),
         cost_estimate=QUICK,
     )(place, weights, *flat, *lower, pivot_inverse)
 
@@ -355,7 +355,7 @@
         out_specs=VMEM,
         out_shape=jax.ShapeDtypeStruct((n_row, owners, 1, points), F32),
         scratch_shapes=[pltpu.VMEM((n_pole * n_rows, owners * points), F32)],
-        compiler_params=room(58),
+        compiler_params=room(24),
         cost_estimate=QUICK,
     )(place, source, *[x for terms in rows for x in terms], *pivots, ancestor, *[bases[k] for k in order])
 

time: 123 us -> 124 us (level)
  other arithmetic: 4.49 us -> 8.58 us
  Pallas kernels: 38.8 us -> 36.4 us
  waiting for transfers between devices: 18.7 us -> 16.4 us
    ppermute x4, waiting for transfers between devices: 2.07 us -> 0.01 us  [permute(): return lax.ppermute(x, axis, pairs)]
    pallas_call x1, Pallas kernels: 4.96 us -> 3.5 us  [pivot_term(): pl.pallas_call(kernel, grid=(1,), in_specs=[SMEM, SMEM] + [fixed(x.shape)...]
  transfers between devices with their start and end apart: 26 -> 26, of which waited for: 5 -> 5; matrix products, arithmetic and copies ran while one was open for 5% -> 9% of each run, Pallas kernels for 32% -> 30%
where the time goes in v4:
time: 124 us; the launch traced here: 123 us
  starting transfers between devices  55.8 us (45%)
  Pallas kernels  36.4 us (29%)
  waiting for transfers between devices  16.4 us (13%)
  other arithmetic  8.58 us (7%)
  local copies, waits for them, and re-layouts  5.15 us (4%)
    ppermute x12, starting transfers between devices, swap(): lax.ppermute(x, axis, [(i, i ^ mask) for i in range(lax.axis_size(axis))])  21.6 us
    pallas_call x1, Pallas kernels, lower_products(): pl.pallas_call(kernel, grid=(steps,), in_specs=[SMEM, SMEM, pl.BlockSpec(...  13.9 us
    all_to_all x1, starting transfers between devices, body(): lax.all_to_all(after(ancestor, parts[0], upper_near[1][-1]), ('row', 'col...  11.5 us
    pallas_call x1, Pallas kernels, upper_products(): pl.pallas_call(kernel, grid=(steps,), in_specs=[SMEM, SMEM, pl.BlockSpec(...  10.5 us
    ppermute x4, starting transfers between devices, swap_both(): return lax.ppermute(x, axes, pairs)  8.77 us
    ppermute x4, waiting for transfers between devices, shift(): return lax.ppermute(x, axis, [(i, (i + by) % n) for i in range(n)])  7.89 us
    ppermute x4, starting transfers between devices, shift(): return lax.ppermute(x, axis, [(i, (i + by) % n) for i in range(n)])  5.74 us
    ppermute x4, starting transfers between devices, permute(): return lax.ppermute(x, axis, pairs)  4.62 us
  transfers between devices with their start and end apart: 26, of which 5 were waited for; matrix products, arithmetic and copies ran while one was open for 9% of the time, Pallas kernels for 30%

profile of v4, /device:TPU:0, one launch (start us, length us, event | category | flops | bytes accessed | tf_op | source)
XLA Modules:
  0.0 123.3 jit_solution(18298983589461234281)
XLA Ops:
  0.6 3.0 %collective-permute-start.3 = (f32[2,64,1152]{2,1,0:T(8,128)}, f32[2,64,1152]{2,1,0:T(8,128)S(1)}, u32[]{:S(2)}, u32[]{:S(2)}) collective-permute-start(f32[2,64,1152]{2,1,0:T(8,128)} %bitcast.54), channel_id=1, source_target_pairs={{0,8},{4,12},{8,0},{12,4},{1,9},{5,13},{9,1},{13,5},{2,10},{6,14},... | collective-permute-start | bytes 1769480 | tf_op jit(solution)/shard_map/ppermute | solution.py:368
  4.8 3.7 %collective-permute-start = (f32[64,1152]{1,0:T(8,128)S(1)}, f32[64,1152]{1,0:T(8,128)}, u32[]{:S(2)}, u32[]{:S(2)}) collective-permute-start(f32[64,1152]{1,0:T(8,128)S(1)} %get-tuple-element.44.refs_0_), channel_id=1, source_target_pairs={{0,3},{1,0},{2,1},{3,2},{4,7},{5,4},{6,5},{7,6},{8,11},{9,8},{10,9... | collective-permute-start | bytes 884744 | tf_op jit(solution)/shard_map/ppermute | solution.py:373
  9.1 1.9 %shard_map.95 = (s32[8,128]{1,0:T(8,128)}, s32[2,16,128]{2,1,0:T(8,128)}) custom-call(s32[7]{0:T(128)} %stack.48.place, s32[6,576]{1,0:T(8,128)} %bitcast.59), custom_call_target="tpu_custom_call" | custom-call | tf_op jit(solution)/shard_map/pallas_call | solution.py:255
  11.0 2.8 %shard_map.96 = f32[16,8,8,128]{3,2,1,0:T(8,128)} custom-call(s32[7]{0:T(128)} %stack.48.place, s32[8,128]{1,0:T(8,128)} %get-tuple-element.19.slots, f32[576,8,128]{2,1,0:T(8,128)} %bitcast.51), custom_call_target="tpu_custom_call" | custom-call | tf_op jit(solution)/shard_map/pallas_call | solution.py:279
  13.9 2.0 %collective-permute-done.refs_2_ = f32[64,1152]{1,0:T(8,128)} collective-permute-done((f32[64,1152]{1,0:T(8,128)S(1)}, f32[64,1152]{1,0:T(8,128)}, u32[]{:S(2)}, u32[]{:S(2)}) %collective-permute-start) | collective-permute-done | bytes 294944 | tf_op jit(solution)/shard_map/ppermute | solution.py:373
  15.9 5.9 %collective-permute-done.4.refs_8_ = f32[64,1152]{1,0:T(8,128)} collective-permute-done((f32[64,1152]{1,0:T(8,128)S(1)}, f32[64,1152]{1,0:T(8,128)}, u32[]{:S(2)}, u32[]{:S(2)}) %collective-permute-start.4) | collective-permute-done | bytes 294944 | tf_op jit(solution)/shard_map/ppermute | solution.py:373
  21.9 1.8 %collective-permute-start.1 = (f32[64,1664]{1,0:T(8,128)S(1)}, f32[64,1664]{1,0:T(8,128)S(1)}, u32[]{:S(2)}, u32[]{:S(2)}) collective-permute-start(f32[64,1664]{1,0:T(8,128)S(1)} %pad_maximum_fusion.1.refs_1_), channel_id=1, source_target_pairs={{0,3},{1,0},{2,1},{3,2},{4,7},{5,4},{6,5},{7,6},{8,11},{9,8},{10,9... | collective-permute-start | bytes 1277960 | tf_op jit(solution)/shard_map/ppermute | solution.py:373
  25.7 13.9 %shard_map.97 = (f32[576,256]{1,0:T(8,128)}, f32[576,256]{1,0:T(8,128)}, bf16[1152,512]{1,0:T(8,128)(2,1)}, bf16[1152,512]{1,0:T(8,128)(2,1)}) custom-call(s32[7]{0:T(128)} %stack.48.place, f32[1,2]{1,0:T(1,128)} %weights.4, f32[1,2,1152,1152]{3,2,1,0:T(8,128)} %tile.3, f32[2,64,1152]{2,1,0:T(8,128)} %bitcast.56, f32[2,64,1152]{2,1,0:T(8,128)} %copy-done.15, ...), custom_call_target="tpu_custom_call" | custom-call | tf_op jit(solution)/shard_map/pallas_call | solution.py:76
  39.6 1.5 %collective-permute-start.11 = (f32[576,256]{1,0:T(8,128)}, f32[576,256]{1,0:T(8,128)}, u32[]{:S(2)}, u32[]{:S(2)}) collective-permute-start(f32[576,256]{1,0:T(8,128)} %get-tuple-element.26), channel_id=1, source_target_pairs={{0,16},{16,0},{1,17},{17,1},{2,18},{18,2},{3,19},{19,3},{4,20},{20... | collective-permute-start | bytes 1769480 | tf_op jit(solution)/shard_map/ppermute | solution.py:368
  46.5 11.5 %all-to-all-start = ((f32[16,8,8,128]{3,2,1,0:T(8,128)}), f32[16,8,8,128]{3,2,1,0:T(8,128)S(1)}, u32[]{:S(2)}, u32[]{:S(2)}) async-start(f32[16,8,8,128]{3,2,1,0:T(8,128)} %shard_map.96), calls=%async_computation | async-start | bytes 1048576 | tf_op jit(solution)/shard_map/all_to_all | solution.py:501
  58.1 1.5 %add.95 = f32[576,256]{1,0:T(8,128)S(1)} add(f32[576,256]{1,0:T(8,128)} %get-tuple-element.21, f32[576,256]{1,0:T(8,128)} %collective-permute-done.11) | non-fusion elementwise | flops 147456 | bytes 1769472 | tf_op jit(solution)/shard_map/add | solution.py:408
  60.4 2.1 %collective-permute-start.12 = (f32[2,144,256]{2,1,0:T(8,128)}, f32[2,144,256]{2,1,0:T(8,128)}, u32[]{:S(2)}, u32[]{:S(2)}) collective-permute-start(f32[2,144,256]{2,1,0:T(8,128)} %pad_maximum_fusion.2), channel_id=1, source_target_pairs={{0,1},{1,0},{2,3},{3,2},{4,5},{5,4},{6,7},{7,6},{8,9},{9,8},{10,11... | collective-permute-start | bytes 884744 | tf_op jit(solution)/shard_map/ppermute | solution.py:368
  65.0 3.5 %shard_map.98.refs_4_ = f32[256,256]{1,0:T(8,128)} custom-call(s32[7]{0:T(128)S(1)} %copy-done.9, f32[1,2]{1,0:T(1,128)S(1)} %copy-done.12, f32[64,1152]{1,0:T(8,128)S(1)} %get-tuple-element.44.refs_0_, f32[64,1664]{1,0:T(8,128)S(1)} %pad_maximum_fusion.1.refs_1_, f32[64,1152]{1,0:T(8,128)} %collective-permute-done.refs_2_, ...), custom_call_target="tpu_custom_call" | custom-call | tf_op jit(solution)/shard_map/pallas_call | solution.py:132
  68.6 10.5 %shard_map.99 = (f32[4,32,1152]{2,1,0:T(8,128)}, f32[4,32,1152]{2,1,0:T(8,128)}) custom-call(s32[7]{0:T(128)} %stack.48.place, f32[1,2]{1,0:T(1,128)} %weights.4, f32[1,2,1152,1152]{3,2,1,0:T(8,128)} %tile.3, f32[64,1152]{1,0:T(8,128)} %copy-done.1, f32[64,1664]{1,0:T(8,128)} %copy-done, f32[64,1152]{1,0:T(8,128)} %collective-permute-done.refs_2_, ...), custom_call_target="tpu_custom_call" | custom-call | tf_op jit(solution)/shard_map/pallas_call | solution.py:189
  79.1 1.7 %add_bitcast_fusion = (f32[144,256]{1,0:T(8,128)S(1)}, f32[144,256]{1,0:T(8,128)}) fusion(f32[2,144,256]{2,1,0:T(8,128)} %collective-permute-done.12, f32[4,144,256]{2,1,0:T(8,128)S(1)} %bitcast.50, s32[]{:T(128)S(6)} %select_n.75, s32[]{:T(128)S(6)} %select_n.64), kind=kLoop, calls=%fused_computation.6 | loop fusion | flops 73728 | bytes 884744 | tf_op jit(solution)/shard_map/add | solution.py:454
  81.8 11.1 %collective-permute-start.17 = (f32[144,256]{1,0:T(8,128)}, f32[144,256]{1,0:T(8,128)S(1)}, u32[]{:S(2)}, u32[]{:S(2)}) collective-permute-start(f32[144,256]{1,0:T(8,128)} %get-tuple-element.37), channel_id=1, source_target_pairs={{0,2},{1,3},{2,0},{3,1},{4,6},{5,7},{6,4},{7,5},{8,10},{9,11},{10,... | collective-permute-start | bytes 442376 | tf_op jit(solution)/shard_map/ppermute | solution.py:368
  92.9 1.5 %collective-permute-start.18 = (f32[144,256]{1,0:T(8,128)S(1)}, f32[144,256]{1,0:T(8,128)S(1)}, u32[]{:S(2)}, u32[]{:S(2)}) collective-permute-start(f32[144,256]{1,0:T(8,128)S(1)} %get-tuple-element.36.refs_0_), channel_id=1, source_target_pairs={{0,16},{16,0},{1,17},{17,1},{2,18},{18,2},{3,19},{19,3},{4,20},{20... | collective-permute-start | bytes 442376 | tf_op jit(solution)/shard_map/ppermute | solution.py:368
  96.4 5.3 %collective-permute-start.19 = (f32[144,256]{1,0:T(8,128)}, f32[144,256]{1,0:T(8,128)S(1)}, u32[]{:S(2)}, u32[]{:S(2)}) collective-permute-start(f32[144,256]{1,0:T(8,128)} %get-tuple-element.37), channel_id=1, source_target_pairs={{0,18},{1,19},{2,16},{3,17},{16,2},{17,3},{18,0},{19,1},{4,22},{5,... | collective-permute-start | bytes 442376 | tf_op jit(solution)/shard_map/ppermute | solution.py:433
  101.6 2.4 %collective-permute-start.16 = (f32[32,1152]{1,0:T(8,128)}, f32[32,1152]{1,0:T(8,128)}, u32[]{:S(2)}, u32[]{:S(2)}) collective-permute-start(f32[32,1152]{1,0:T(8,128)} %get-tuple-element.39), channel_id=1, source_target_pairs={{0,24},{4,28},{8,16},{12,20},{16,8},{20,12},{24,0},{28,4},{1,25},{... | collective-permute-start | bytes 442376 | tf_op jit(solution)/shard_map/ppermute | solution.py:433
  105.1 3.3 %collective-permute-done.19.refs_3_ = f32[144,256]{1,0:T(8,128)S(1)} collective-permute-done((f32[144,256]{1,0:T(8,128)}, f32[144,256]{1,0:T(8,128)S(1)}, u32[]{:S(2)}, u32[]{:S(2)}) %collective-permute-start.19) | collective-permute-done | bytes 147488 | tf_op jit(solution)/shard_map/ppermute | solution.py:433
  108.5 3.8 %shard_map.100 = f32[4,4,1,128]{3,2,1,0:T(1,128)} custom-call(s32[7]{0:T(128)S(1)} %copy-done.10, s32[2,16,128]{2,1,0:T(8,128)S(1)} %copy-done.11, f32[144,256]{1,0:T(8,128)S(1)} %get-tuple-element.36.refs_0_, f32[144,256]{1,0:T(8,128)S(1)} %collective-permute-done.17.refs_1_, f32[144,256]{1,0:T(8,128)S(1)} %collective-permute-done.18.refs_2_, ...), custom_call_target="tpu_custom_call" | custom-call | tf_op jit(solution)/shard_map/pallas_call | solution.py:352
  112.8 3.5 %all-to-all-start.1 = ((f32[16,1,128]{2,1,0:T(1,128)}), f32[16,1,128]{2,1,0:T(1,128)S(1)}, u32[]{:S(2)}, u32[]{:S(2)}) async-start(f32[16,1,128]{2,1,0:T(1,128)} %bitcast.27), calls=%async_computation.1 | async-start | bytes 16384 | tf_op jit(solution)/shard_map/all_to_all | solution.py:527
  116.4 1.8 %bitcast_add_fusion = f32[32,1152]{1,0:T(8,128)} fusion(f32[32,1152]{1,0:T(8,128)} %collective-permute-done.16, f32[32,1152]{1,0:T(8,128)} %collective-permute-done.14, f32[32,1152]{1,0:T(8,128)} %collective-permute-done.15, f32[2,2,32,1152]{3,2,1,0:T(8,128)} %bitcast.48, s32[]{:T(128)S(6)} %select_n.68, s32[]{:T(128)S(6)} %select_n.70), kind=kLoop, calls=%fused_computation.5 | loop fusion | flops 110592 | bytes 737288 | tf_op jit(solution)/shard_map/add | solution.py:534
  118.2 4.6 %all-to-all-done.1 = f32[16,1,128]{2,1,0:T(1,128)S(1)} async-done(((f32[16,1,128]{2,1,0:T(1,128)}), f32[16,1,128]{2,1,0:T(1,128)S(1)}, u32[]{:S(2)}, u32[]{:S(2)}) %all-to-all-start.1) | async-done | bytes 8224 | tf_op jit(solution)/shard_map/all_to_all | solution.py:527
  (87 shorter events, 17.7 us)
Async XLA Ops:
  0.6 21.1 %collective-permute-start.3 = (f32[2,64,1152]{2,1,0:T(8,128)}, f32[2,64,1152]{2,1,0:T(8,128)S(1)}, u32[]{:S(2)}, u32[]{:S(2)}) collective-permute-start(f32[2,64,1152]{2,1,0:T(8,128)} %bitcast.54), channel_id=1, source_target_pairs={{0,8},{4,12},{8,0},{12,4},{1,9},{5,13},{9,1},{13,5},{2,10},{6,14},... | collective-permute-start | bytes 1769480 | tf_op jit(solution)/shard_map/ppermute | solution.py:368
  4.8 11.1 %collective-permute-start = (f32[64,1152]{1,0:T(8,128)S(1)}, f32[64,1152]{1,0:T(8,128)}, u32[]{:S(2)}, u32[]{:S(2)}) collective-permute-start(f32[64,1152]{1,0:T(8,128)S(1)} %get-tuple-element.44.refs_0_), channel_id=1, source_target_pairs={{0,3},{1,0},{2,1},{3,2},{4,7},{5,4},{6,5},{7,6},{8,11},{9,8},{10,9... | collective-permute-start | bytes 884744 | tf_op jit(solution)/shard_map/ppermute | solution.py:373
  8.4 13.3 %collective-permute-start.4 = (f32[64,1152]{1,0:T(8,128)S(1)}, f32[64,1152]{1,0:T(8,128)}, u32[]{:S(2)}, u32[]{:S(2)}) collective-permute-start(f32[64,1152]{1,0:T(8,128)S(1)} %get-tuple-element.44.refs_0_), channel_id=1, source_target_pairs={{0,1},{1,2},{2,3},{3,0},{4,5},{5,6},{6,7},{7,4},{8,9},{9,10},{10,1... | collective-permute-start | bytes 884744 | tf_op jit(solution)/shard_map/ppermute | solution.py:373
  8.4 15.6 %collective-permute-start.2 = (f32[2,64,1152]{2,1,0:T(8,128)}, f32[2,64,1152]{2,1,0:T(8,128)S(1)}, u32[]{:S(2)}, u32[]{:S(2)}) collective-permute-start(f32[2,64,1152]{2,1,0:T(8,128)} %bitcast.55), channel_id=1, source_target_pairs={{0,4},{4,0},{8,12},{12,8},{1,5},{5,1},{9,13},{13,9},{2,6},{6,2},{1... | collective-permute-start | bytes 1769480 | tf_op jit(solution)/shard_map/ppermute | solution.py:368
  21.9 22.5 %collective-permute-start.1 = (f32[64,1664]{1,0:T(8,128)S(1)}, f32[64,1664]{1,0:T(8,128)S(1)}, u32[]{:S(2)}, u32[]{:S(2)}) collective-permute-start(f32[64,1664]{1,0:T(8,128)S(1)} %pad_maximum_fusion.1.refs_1_), channel_id=1, source_target_pairs={{0,3},{1,0},{2,1},{3,2},{4,7},{5,4},{6,5},{7,6},{8,11},{9,8},{10,9... | collective-permute-start | bytes 1277960 | tf_op jit(solution)/shard_map/ppermute | solution.py:373
  23.7 22.0 %collective-permute-start.9 = (f32[64,1664]{1,0:T(8,128)S(1)}, f32[64,1664]{1,0:T(8,128)S(1)}, u32[]{:S(2)}, u32[]{:S(2)}) collective-permute-start(f32[64,1664]{1,0:T(8,128)S(1)} %pad_maximum_fusion.1.refs_1_), channel_id=1, source_target_pairs={{0,1},{1,2},{2,3},{3,0},{4,5},{5,6},{6,7},{7,4},{8,9},{9,10},{10,1... | collective-permute-start | bytes 1277960 | tf_op jit(solution)/shard_map/ppermute | solution.py:373
  39.6 18.5 %collective-permute-start.11 = (f32[576,256]{1,0:T(8,128)}, f32[576,256]{1,0:T(8,128)}, u32[]{:S(2)}, u32[]{:S(2)}) collective-permute-start(f32[576,256]{1,0:T(8,128)} %get-tuple-element.26), channel_id=1, source_target_pairs={{0,16},{16,0},{1,17},{17,1},{2,18},{18,2},{3,19},{19,3},{4,20},{20... | collective-permute-start | bytes 1769480 | tf_op jit(solution)/shard_map/ppermute | solution.py:368
  41.8 23.2 %collective-permute-start.6 = (f32[64,1152]{1,0:T(8,128)}, f32[64,1152]{1,0:T(8,128)}, u32[]{:S(2)}, u32[]{:S(2)}) collective-permute-start(f32[64,1152]{1,0:T(8,128)} %collective-permute-done.refs_2_), channel_id=1, source_target_pairs={{2,1},{1,0},{6,5},{5,4},{10,9},{9,8},{14,13},{13,12},{18,17},{17,1... | collective-permute-start | bytes 884744 | tf_op jit(solution)/shard_map/ppermute | solution.py:364
  43.1 21.9 %collective-permute-start.7 = (f32[64,1152]{1,0:T(8,128)}, f32[64,1152]{1,0:T(8,128)}, u32[]{:S(2)}, u32[]{:S(2)}) collective-permute-start(f32[64,1152]{1,0:T(8,128)} %collective-permute-done.4.refs_8_), channel_id=1, source_target_pairs={{1,2},{2,3},{5,6},{6,7},{9,10},{10,11},{13,14},{14,15},{17,18},{18... | collective-permute-start | bytes 884744 | tf_op jit(solution)/shard_map/ppermute | solution.py:364
  44.5 18.0 %collective-permute-start.8 = (f32[64,1664]{1,0:T(8,128)S(1)}, f32[64,1664]{1,0:T(8,128)S(1)}, u32[]{:S(2)}, u32[]{:S(2)}) collective-permute-start(f32[64,1664]{1,0:T(8,128)S(1)} %collective-permute-done.1.refs_3_), channel_id=1, source_target_pairs={{2,1},{1,0},{6,5},{5,4},{10,9},{9,8},{14,13},{13,12},{18,17},{17,1... | collective-permute-start | bytes 1277960 | tf_op jit(solution)/shard_map/ppermute | solution.py:364
  45.8 16.7 %collective-permute-start.10 = (f32[64,1664]{1,0:T(8,128)S(1)}, f32[64,1664]{1,0:T(8,128)S(1)}, u32[]{:S(2)}, u32[]{:S(2)}) collective-permute-start(f32[64,1664]{1,0:T(8,128)S(1)} %collective-permute-done.9.refs_9_), channel_id=1, source_target_pairs={{1,2},{2,3},{5,6},{6,7},{9,10},{10,11},{13,14},{14,15},{17,18},{18... | collective-permute-start | bytes 1277960 | tf_op jit(solution)/shard_map/ppermute | solution.py:364
  46.5 58.7 %all-to-all-start = ((f32[16,8,8,128]{3,2,1,0:T(8,128)}), f32[16,8,8,128]{3,2,1,0:T(8,128)S(1)}, u32[]{:S(2)}, u32[]{:S(2)}) async-start(f32[16,8,8,128]{3,2,1,0:T(8,128)} %shard_map.96), calls=%async_computation | async-start | bytes 1048576 | tf_op jit(solution)/shard_map/all_to_all | solution.py:501
  60.4 18.7 %collective-permute-start.12 = (f32[2,144,256]{2,1,0:T(8,128)}, f32[2,144,256]{2,1,0:T(8,128)}, u32[]{:S(2)}, u32[]{:S(2)}) collective-permute-start(f32[2,144,256]{2,1,0:T(8,128)} %pad_maximum_fusion.2), channel_id=1, source_target_pairs={{0,1},{1,0},{2,3},{3,2},{4,5},{5,4},{6,7},{7,6},{8,9},{9,8},{10,11... | collective-permute-start | bytes 884744 | tf_op jit(solution)/shard_map/ppermute | solution.py:368
  63.6 17.7 %collective-permute-start.22 = (f32[4,64,512]{2,1,0:T(8,128)S(1)}, f32[4,64,512]{2,1,0:T(8,128)}, u32[]{:S(2)}, u32[]{:S(2)}) collective-permute-start(f32[4,64,512]{2,1,0:T(8,128)S(1)} %pad_maximum_fusion.refs_7_), channel_id=1, source_target_pairs={{0,8},{4,12},{8,0},{12,4},{1,9},{5,13},{9,1},{13,5},{2,10},{6,14},... | collective-permute-start | bytes 1572872 | tf_op jit(solution)/shard_map/ppermute | solution.py:368
  80.8 12.1 %collective-permute-start.13 = (f32[4,32,1152]{2,1,0:T(8,128)}, f32[4,32,1152]{2,1,0:T(8,128)S(1)}, u32[]{:S(2)}, u32[]{:S(2)}) collective-permute-start(f32[4,32,1152]{2,1,0:T(8,128)} %get-tuple-element.32), channel_id=1, source_target_pairs={{0,4},{4,0},{8,12},{12,8},{1,5},{5,1},{9,13},{13,9},{2,6},{6,2},{1... | collective-permute-start | bytes 1769480 | tf_op jit(solution)/shard_map/ppermute | solution.py:368
  80.8 20.9 %collective-permute-start.21 = (f32[4,64,512]{2,1,0:T(8,128)S(1)}, f32[4,64,512]{2,1,0:T(8,128)S(1)}, u32[]{:S(2)}, u32[]{:S(2)}) collective-permute-start(f32[4,64,512]{2,1,0:T(8,128)S(1)} %pad_maximum_fusion.refs_7_), channel_id=1, source_target_pairs={{0,4},{4,0},{8,12},{12,8},{1,5},{5,1},{9,13},{13,9},{2,6},{6,2},{1... | collective-permute-start | bytes 1572872 | tf_op jit(solution)/shard_map/ppermute | solution.py:368
  81.3 27.2 %collective-permute-start.23 = (f32[4,64,512]{2,1,0:T(8,128)}, f32[4,64,512]{2,1,0:T(8,128)S(1)}, u32[]{:S(2)}, u32[]{:S(2)}) collective-permute-start(f32[4,64,512]{2,1,0:T(8,128)} %collective-permute-done.22.refs_9_), channel_id=1, source_target_pairs={{0,4},{4,0},{8,12},{12,8},{1,5},{5,1},{9,13},{13,9},{2,6},{6,2},{1... | collective-permute-start | bytes 1572872 | tf_op jit(solution)/shard_map/ppermute | solution.py:368
  81.3 15.1 %collective-permute-start.20 = (f32[256,256]{1,0:T(8,128)}, f32[256,256]{1,0:T(8,128)S(1)}, u32[]{:S(2)}, u32[]{:S(2)}) collective-permute-start(f32[256,256]{1,0:T(8,128)} %shard_map.98.refs_4_), channel_id=1, source_target_pairs={{0,16},{16,0},{1,17},{17,1},{2,18},{18,2},{3,19},{19,3},{4,20},{20... | collective-permute-start | bytes 786440 | tf_op jit(solution)/shard_map/ppermute | solution.py:368
  81.8 22.3 %collective-permute-start.17 = (f32[144,256]{1,0:T(8,128)}, f32[144,256]{1,0:T(8,128)S(1)}, u32[]{:S(2)}, u32[]{:S(2)}) collective-permute-start(f32[144,256]{1,0:T(8,128)} %get-tuple-element.37), channel_id=1, source_target_pairs={{0,2},{1,3},{2,0},{3,1},{4,6},{5,7},{6,4},{7,5},{8,10},{9,11},{10,... | collective-permute-start | bytes 442376 | tf_op jit(solution)/shard_map/ppermute | solution.py:368
  92.9 11.7 %collective-permute-start.18 = (f32[144,256]{1,0:T(8,128)S(1)}, f32[144,256]{1,0:T(8,128)S(1)}, u32[]{:S(2)}, u32[]{:S(2)}) collective-permute-start(f32[144,256]{1,0:T(8,128)S(1)} %get-tuple-element.36.refs_0_), channel_id=1, source_target_pairs={{0,16},{16,0},{1,17},{17,1},{2,18},{18,2},{3,19},{19,3},{4,20},{20... | collective-permute-start | bytes 442376 | tf_op jit(solution)/shard_map/ppermute | solution.py:368
  96.4 12.1 %collective-permute-start.19 = (f32[144,256]{1,0:T(8,128)}, f32[144,256]{1,0:T(8,128)S(1)}, u32[]{:S(2)}, u32[]{:S(2)}) collective-permute-start(f32[144,256]{1,0:T(8,128)} %get-tuple-element.37), channel_id=1, source_target_pairs={{0,18},{1,19},{2,16},{3,17},{16,2},{17,3},{18,0},{19,1},{4,22},{5,... | collective-permute-start | bytes 442376 | tf_op jit(solution)/shard_map/ppermute | solution.py:433
  101.6 10.6 %collective-permute-start.16 = (f32[32,1152]{1,0:T(8,128)}, f32[32,1152]{1,0:T(8,128)}, u32[]{:S(2)}, u32[]{:S(2)}) collective-permute-start(f32[32,1152]{1,0:T(8,128)} %get-tuple-element.39), channel_id=1, source_target_pairs={{0,24},{4,28},{8,16},{12,20},{16,8},{20,12},{24,0},{28,4},{1,25},{... | collective-permute-start | bytes 442376 | tf_op jit(solution)/shard_map/ppermute | solution.py:433
  104.6 8.2 %collective-permute-start.15 = (f32[32,1152]{1,0:T(8,128)S(1)}, f32[32,1152]{1,0:T(8,128)}, u32[]{:S(2)}, u32[]{:S(2)}) collective-permute-start(f32[32,1152]{1,0:T(8,128)S(1)} %get-tuple-element.38), channel_id=1, source_target_pairs={{0,16},{4,20},{8,24},{12,28},{16,0},{20,4},{24,8},{28,12},{1,17},{... | collective-permute-start | bytes 442376 | tf_op jit(solution)/shard_map/ppermute | solution.py:433
  112.8 9.9 %all-to-all-start.1 = ((f32[16,1,128]{2,1,0:T(1,128)}), f32[16,1,128]{2,1,0:T(1,128)S(1)}, u32[]{:S(2)}, u32[]{:S(2)}) async-start(f32[16,1,128]{2,1,0:T(1,128)} %bitcast.27), calls=%async_computation.1 | async-start | bytes 16384 | tf_op jit(solution)/shard_map/all_to_all | solution.py:527
  (20 other events, 293.8 us)

commit v5 on v3

--- a/solution.py
+++ b/solution.py
@@ -433,7 +433,7 @@
     return lax.ppermute(x, axes, pairs)
 
 
-def rows_by_pole(x, before, later):
+def rows_by_pole(x, before, between):
     n_pole, n_col = lax.axis_size("pole"), lax.axis_size("col")
     me = lax.axis_index("col")
     held = [pick(x, me ^ d) for d in range(n_col)]
@@ -442,18 +442,18 @@
         away = [d for d in range(0, n_col, bit) if d & bit]
         if bit == 2 and n_col == 4:
             mine, other = held[0], held[2]
-            later = after(later, other)
+            other = after(other, between)
             rows = [[mine, swap(other, "col", 2)]]
             for d in range(1, n_pole):
                 rows.append([swap(mine, "pole", d), swap_both(other, ("pole", "col"), (d, 2))])
-            return rows, later
+            return rows
         arrived = swap(jnp.stack([held[d] for d in away]), "col", bit)
         if bit == 1:
-            arrived = after(arrived, *before)
+            arrived = after(arrived, before)
         for j, d in enumerate(away):
             held[d ^ bit] = held[d ^ bit] + arrived[j]
         bit *= 2
-    return [[held[0]]] + [[swap(held[0], "pole", d)] for d in range(1, n_pole)], later
+    return [[held[0]]] + [[swap(held[0], "pole", d)] for d in range(1, n_pole)]
 
 
 def body(
@@ -512,8 +512,8 @@
     keep, send = upper_products(place, after(pole_weights, pivot), inverse_tile, upper, n_pole * n_row)
     for b in list(bases):
         bases[b + 1] = swap(bases[b], "row", 1)
-    rows, send = rows_by_pole(half.reshape(n_col, rows_here, width), (keep,), send)
     near = (keep + swap(send, "row", 1)).reshape(n_pole, n_row // 2, -1, tile_cols)
+    rows = rows_by_pole(half.reshape(n_col, rows_here, width), keep, near)
     upper_density, arrived = 0.0, []
     for a in range(n_pole):
         for b in range(n_row // 2):

time: 123 us -> 135 us (1.098)
  waiting for transfers between devices: 18.7 us -> 32 us
  starting transfers between devices: 54.6 us -> 52.4 us
    ppermute x12, waiting for transfers between devices: 0.03 us -> 14.4 us  [swap(): lax.ppermute(x, axis, [(i, i ^ mask) for i in range(lax.axis_size(axis))])]
    ppermute x4, starting transfers between devices: 9.46 us -> 3.54 us  [swap_both(): return lax.ppermute(x, axes, pairs)]
    ppermute x4, waiting for transfers between devices: 2.07 us -> 0.01 us  [permute(): return lax.ppermute(x, axis, pairs)]
    ppermute x4, waiting for transfers between devices: 7.83 us -> 9.65 us  [shift(): return lax.ppermute(x, axis, [(i, (i + by) % n) for i in range(n)])]
    ppermute x12, starting transfers between devices: 20.4 us -> 22.2 us  [swap(): lax.ppermute(x, axis, [(i, i ^ mask) for i in range(lax.axis_size(axis))])]
    all_to_all x1, starting transfers between devices: 10.8 us -> 12.5 us  [body(): lax.all_to_all(after(ancestor, parts[0], upper_near[1][-1]), ('row', 'col...]
  transfers between devices with their start and end apart: 26 -> 26, of which waited for: 5 -> 7; matrix products, arithmetic and copies ran while one was open for 5% -> 5% of each run, Pallas kernels for 32% -> 29%
where the time goes in v5:
time: 135 us; the launch traced here: 134 us
  starting transfers between devices  52.4 us (39%)
  Pallas kernels  38.9 us (29%)
  waiting for transfers between devices  32 us (24%)
  local copies, waits for them, and re-layouts  5.12 us (4%)
  other arithmetic  4.94 us (4%)
    ppermute x12, starting transfers between devices, swap(): lax.ppermute(x, axis, [(i, i ^ mask) for i in range(lax.axis_size(axis))])  22.2 us
    ppermute x12, waiting for transfers between devices, swap(): lax.ppermute(x, axis, [(i, i ^ mask) for i in range(lax.axis_size(axis))])  14.4 us
    pallas_call x1, Pallas kernels, lower_products(): pl.pallas_call(kernel, grid=(steps,), in_specs=[SMEM, SMEM, pl.BlockSpec(...  13.9 us
    all_to_all x1, starting transfers between devices, body(): lax.all_to_all(after(ancestor, parts[0], upper_near[1][-1]), ('row', 'col...  12.5 us
    pallas_call x1, Pallas kernels, upper_products(): pl.pallas_call(kernel, grid=(steps,), in_specs=[SMEM, SMEM, pl.BlockSpec(...  10.5 us
    ppermute x4, waiting for transfers between devices, shift(): return lax.ppermute(x, axis, [(i, (i + by) % n) for i in range(n)])  9.65 us
    ppermute x4, starting transfers between devices, shift(): return lax.ppermute(x, axis, [(i, (i + by) % n) for i in range(n)])  5.74 us
    all_to_all x1, waiting for transfers between devices, body(): lax.all_to_all(after(terms, *arrived).reshape(n_row * n_col, 1, points),...  5.67 us
  transfers between devices with their start and end apart: 26, of which 7 were waited for; matrix products, arithmetic and copies ran while one was open for 5% of the time, Pallas kernels for 29%

profile of v5, /device:TPU:0, one launch (start us, length us, event | category | flops | bytes accessed | tf_op | source)
XLA Modules:
  0.0 134.4 jit_solution(452473639546935032)
XLA Ops:
  0.6 3.0 %collective-permute-start.3 = (f32[2,64,1152]{2,1,0:T(8,128)}, f32[2,64,1152]{2,1,0:T(8,128)S(1)}, u32[]{:S(2)}, u32[]{:S(2)}) collective-permute-start(f32[2,64,1152]{2,1,0:T(8,128)} %bitcast.54), channel_id=1, source_target_pairs={{0,8},{4,12},{8,0},{12,4},{1,9},{5,13},{9,1},{13,5},{2,10},{6,14},... | collective-permute-start | bytes 1769480 | tf_op jit(solution)/shard_map/ppermute | solution.py:368
  4.8 3.7 %collective-permute-start = (f32[64,1152]{1,0:T(8,128)S(1)}, f32[64,1152]{1,0:T(8,128)}, u32[]{:S(2)}, u32[]{:S(2)}) collective-permute-start(f32[64,1152]{1,0:T(8,128)S(1)} %get-tuple-element.44.refs_0_), channel_id=1, source_target_pairs={{0,3},{1,0},{2,1},{3,2},{4,7},{5,4},{6,5},{7,6},{8,11},{9,8},{10,9... | collective-permute-start | bytes 884744 | tf_op jit(solution)/shard_map/ppermute | solution.py:373
  10.0 1.9 %shard_map.95 = (s32[8,128]{1,0:T(8,128)}, s32[2,16,128]{2,1,0:T(8,128)}) custom-call(s32[7]{0:T(128)} %stack.48.place, s32[6,576]{1,0:T(8,128)} %bitcast.60), custom_call_target="tpu_custom_call" | custom-call | tf_op jit(solution)/shard_map/pallas_call | solution.py:255
  11.9 2.8 %shard_map.96 = f32[16,8,8,128]{3,2,1,0:T(8,128)} custom-call(s32[7]{0:T(128)} %stack.48.place, s32[8,128]{1,0:T(8,128)} %get-tuple-element.19.slots, f32[576,8,128]{2,1,0:T(8,128)} %bitcast.50), custom_call_target="tpu_custom_call" | custom-call | tf_op jit(solution)/shard_map/pallas_call | solution.py:279
  15.9 5.9 %collective-permute-done.4.refs_8_ = f32[64,1152]{1,0:T(8,128)} collective-permute-done((f32[64,1152]{1,0:T(8,128)S(1)}, f32[64,1152]{1,0:T(8,128)}, u32[]{:S(2)}, u32[]{:S(2)}) %collective-permute-start.4) | collective-permute-done | bytes 294944 | tf_op jit(solution)/shard_map/ppermute | solution.py:373
  21.8 1.8 %collective-permute-start.1 = (f32[64,1664]{1,0:T(8,128)S(1)}, f32[64,1664]{1,0:T(8,128)S(1)}, u32[]{:S(2)}, u32[]{:S(2)}) collective-permute-start(f32[64,1664]{1,0:T(8,128)S(1)} %pad_maximum_fusion.1.refs_1_), channel_id=1, source_target_pairs={{0,3},{1,0},{2,1},{3,2},{4,7},{5,4},{6,5},{7,6},{8,11},{9,8},{10,9... | collective-permute-start | bytes 1277960 | tf_op jit(solution)/shard_map/ppermute | solution.py:373
  25.5 13.9 %shard_map.97 = (f32[576,256]{1,0:T(8,128)}, f32[576,256]{1,0:T(8,128)}, bf16[1152,512]{1,0:T(8,128)(2,1)}, bf16[1152,512]{1,0:T(8,128)(2,1)}) custom-call(s32[7]{0:T(128)} %stack.48.place, f32[1,2]{1,0:T(1,128)} %weights.4, f32[1,2,1152,1152]{3,2,1,0:T(8,128)} %tile.3, f32[2,64,1152]{2,1,0:T(8,128)} %bitcast.56, f32[2,64,1152]{2,1,0:T(8,128)} %copy-done.10, ...), custom_call_target="tpu_custom_call" | custom-call | tf_op jit(solution)/shard_map/pallas_call | solution.py:76
  40.8 2.7 %collective-permute-done.9.refs_9_ = f32[64,1664]{1,0:T(8,128)S(1)} collective-permute-done((f32[64,1664]{1,0:T(8,128)S(1)}, f32[64,1664]{1,0:T(8,128)S(1)}, u32[]{:S(2)}, u32[]{:S(2)}) %collective-permute-start.9) | collective-permute-done | bytes 426016 | tf_op jit(solution)/shard_map/ppermute | solution.py:373
  46.9 1.5 %collective-permute-start.11 = (f32[576,256]{1,0:T(8,128)}, f32[576,256]{1,0:T(8,128)}, u32[]{:S(2)}, u32[]{:S(2)}) collective-permute-start(f32[576,256]{1,0:T(8,128)} %get-tuple-element.26), channel_id=1, source_target_pairs={{0,16},{16,0},{1,17},{17,1},{2,18},{18,2},{3,19},{19,3},{4,20},{20... | collective-permute-start | bytes 1769480 | tf_op jit(solution)/shard_map/ppermute | solution.py:368
  48.4 12.5 %all-to-all-start = ((f32[16,8,8,128]{3,2,1,0:T(8,128)}), f32[16,8,8,128]{3,2,1,0:T(8,128)S(1)}, u32[]{:S(2)}, u32[]{:S(2)}) async-start(f32[16,8,8,128]{3,2,1,0:T(8,128)} %shard_map.96), calls=%async_computation | async-start | bytes 1048576 | tf_op jit(solution)/shard_map/all_to_all | solution.py:501
  61.1 2.0 %collective-permute-start.22 = (f32[4,64,512]{2,1,0:T(8,128)S(1)}, f32[4,64,512]{2,1,0:T(8,128)}, u32[]{:S(2)}, u32[]{:S(2)}) collective-permute-start(f32[4,64,512]{2,1,0:T(8,128)S(1)} %pad_maximum_fusion.refs_7_), channel_id=1, source_target_pairs={{0,8},{4,12},{8,0},{12,4},{1,9},{5,13},{9,1},{13,5},{2,10},{6,14},... | collective-permute-start | bytes 1572872 | tf_op jit(solution)/shard_map/ppermute | solution.py:368
  64.3 5.0 %shard_map.98.refs_4_ = f32[256,256]{1,0:T(8,128)} custom-call(s32[7]{0:T(128)} %stack.48.place, f32[1,2]{1,0:T(1,128)} %weights.4, f32[64,1152]{1,0:T(8,128)} %copy-done.1, f32[64,1664]{1,0:T(8,128)} %copy-done, f32[64,1152]{1,0:T(8,128)} %collective-permute-done.refs_2_, f32[64,1664]{1,0:T(8,128)} %copy-done.2, f32[64,1152]{1,0:T(8,128)} %collective-permute-done.6.refs_4_, ...), custom_call_target="tpu_custom_call" | custom-call | tf_op jit(solution)/shard_map/pallas_call | solution.py:132
  69.3 10.5 %shard_map.99 = (f32[4,32,1152]{2,1,0:T(8,128)}, f32[4,32,1152]{2,1,0:T(8,128)}) custom-call(s32[7]{0:T(128)} %stack.48.place, f32[1,2]{1,0:T(1,128)} %weights.4, f32[1,2,1152,1152]{3,2,1,0:T(8,128)} %tile.3, f32[64,1152]{1,0:T(8,128)} %copy-done.1, f32[64,1664]{1,0:T(8,128)} %copy-done, f32[64,1152]{1,0:T(8,128)} %collective-permute-done.refs_2_, ...), custom_call_target="tpu_custom_call" | custom-call | tf_op jit(solution)/shard_map/pallas_call | solution.py:189
  80.7 9.2 %collective-permute-start.16 = (f32[2,144,256]{2,1,0:T(8,128)}, f32[2,144,256]{2,1,0:T(8,128)}, u32[]{:S(2)}, u32[]{:S(2)}) collective-permute-start(f32[2,144,256]{2,1,0:T(8,128)} %pad_maximum_fusion.2), channel_id=1, source_target_pairs={{0,1},{1,0},{2,3},{3,2},{4,5},{5,4},{6,7},{7,6},{8,9},{9,8},{10,11... | collective-permute-start | bytes 884744 | tf_op jit(solution)/shard_map/ppermute | solution.py:368
  90.0 1.5 %collective-permute-start.20 = (f32[256,256]{1,0:T(8,128)S(1)}, f32[256,256]{1,0:T(8,128)S(1)}, u32[]{:S(2)}, u32[]{:S(2)}) collective-permute-start(f32[256,256]{1,0:T(8,128)S(1)} %copy-done.8), channel_id=1, source_target_pairs={{0,16},{16,0},{1,17},{17,1},{2,18},{18,2},{3,19},{19,3},{4,20},{20... | collective-permute-start | bytes 786440 | tf_op jit(solution)/shard_map/ppermute | solution.py:368
  91.5 6.3 %collective-permute-done.16 = f32[2,144,256]{2,1,0:T(8,128)} collective-permute-done((f32[2,144,256]{2,1,0:T(8,128)}, f32[2,144,256]{2,1,0:T(8,128)}, u32[]{:S(2)}, u32[]{:S(2)}) %collective-permute-start.16) | collective-permute-done | bytes 294944 | tf_op jit(solution)/shard_map/ppermute | solution.py:368
  97.8 1.7 %add_bitcast_fusion = (f32[144,256]{1,0:T(8,128)}, f32[144,256]{1,0:T(8,128)S(1)}) fusion(f32[2,144,256]{2,1,0:T(8,128)} %collective-permute-done.16, f32[4,144,256]{2,1,0:T(8,128)S(1)} %bitcast.49, s32[]{:T(128)S(6)} %select_n.75, s32[]{:T(128)S(6)} %select_n.72), kind=kLoop, calls=%fused_computation.6 | loop fusion | flops 73728 | bytes 884744 | tf_op jit(solution)/shard_map/add | solution.py:454
  101.1 3.3 %collective-permute-start.17 = (f32[144,256]{1,0:T(8,128)}, f32[144,256]{1,0:T(8,128)S(1)}, u32[]{:S(2)}, u32[]{:S(2)}) collective-permute-start(f32[144,256]{1,0:T(8,128)} %get-tuple-element.33), channel_id=1, source_target_pairs={{0,2},{1,3},{2,0},{3,1},{4,6},{5,7},{6,4},{7,5},{8,10},{9,11},{10,... | collective-permute-start | bytes 442376 | tf_op jit(solution)/shard_map/ppermute | solution.py:368
  105.9 1.5 %collective-permute-start.13 = (f32[32,1152]{1,0:T(8,128)S(1)}, f32[32,1152]{1,0:T(8,128)S(1)}, u32[]{:S(2)}, u32[]{:S(2)}) collective-permute-start(f32[32,1152]{1,0:T(8,128)S(1)} %get-tuple-element.42), channel_id=1, source_target_pairs={{0,8},{4,12},{8,0},{12,4},{16,24},{20,28},{24,16},{28,20},{1,9},{5... | collective-permute-start | bytes 442376 | tf_op jit(solution)/shard_map/ppermute | solution.py:433
  107.4 8.1 %collective-permute-done.17.refs_1_ = f32[144,256]{1,0:T(8,128)S(1)} collective-permute-done((f32[144,256]{1,0:T(8,128)}, f32[144,256]{1,0:T(8,128)S(1)}, u32[]{:S(2)}, u32[]{:S(2)}) %collective-permute-start.17) | collective-permute-done | bytes 147488 | tf_op jit(solution)/shard_map/ppermute | solution.py:368
  116.0 2.3 %collective-permute-done.19.refs_3_ = f32[144,256]{1,0:T(8,128)S(1)} collective-permute-done((f32[144,256]{1,0:T(8,128)}, f32[144,256]{1,0:T(8,128)S(1)}, u32[]{:S(2)}, u32[]{:S(2)}) %collective-permute-start.19) | collective-permute-done | bytes 147488 | tf_op jit(solution)/shard_map/ppermute | solution.py:433
  119.0 4.7 %shard_map.100 = f32[4,4,1,128]{3,2,1,0:T(1,128)} custom-call(s32[7]{0:T(128)} %stack.48.place, s32[2,16,128]{2,1,0:T(8,128)} %get-tuple-element.31.source, f32[144,256]{1,0:T(8,128)} %copy-done.14, f32[144,256]{1,0:T(8,128)} %copy-done.17, f32[144,256]{1,0:T(8,128)} %copy-done.16, f32[144,256]{1,0:T(8,128)} %copy-done.18, f32[256,256]{1,0:T(8,128)} %shard_map.98.refs_4_, ...), custom_call_target="tpu_custom_call" | custom-call | tf_op jit(solution)/shard_map/pallas_call | solution.py:352
  123.7 3.8 %all-to-all-start.1 = ((f32[16,1,128]{2,1,0:T(1,128)}), f32[16,1,128]{2,1,0:T(1,128)S(1)}, u32[]{:S(2)}, u32[]{:S(2)}) async-start(f32[16,1,128]{2,1,0:T(1,128)} %bitcast.59), calls=%async_computation.1 | async-start | bytes 16384 | tf_op jit(solution)/shard_map/all_to_all | solution.py:527
  128.2 5.7 %all-to-all-done.1 = f32[16,1,128]{2,1,0:T(1,128)S(1)} async-done(((f32[16,1,128]{2,1,0:T(1,128)}), f32[16,1,128]{2,1,0:T(1,128)S(1)}, u32[]{:S(2)}, u32[]{:S(2)}) %all-to-all-start.1) | async-done | bytes 8224 | tf_op jit(solution)/shard_map/all_to_all | solution.py:527
  (89 shorter events, 18.2 us)
Async XLA Ops:
  0.6 21.1 %collective-permute-start.3 = (f32[2,64,1152]{2,1,0:T(8,128)}, f32[2,64,1152]{2,1,0:T(8,128)S(1)}, u32[]{:S(2)}, u32[]{:S(2)}) collective-permute-start(f32[2,64,1152]{2,1,0:T(8,128)} %bitcast.54), channel_id=1, source_target_pairs={{0,8},{4,12},{8,0},{12,4},{1,9},{5,13},{9,1},{13,5},{2,10},{6,14},... | collective-permute-start | bytes 1769480 | tf_op jit(solution)/shard_map/ppermute | solution.py:368
  4.8 11.1 %collective-permute-start = (f32[64,1152]{1,0:T(8,128)S(1)}, f32[64,1152]{1,0:T(8,128)}, u32[]{:S(2)}, u32[]{:S(2)}) collective-permute-start(f32[64,1152]{1,0:T(8,128)S(1)} %get-tuple-element.44.refs_0_), channel_id=1, source_target_pairs={{0,3},{1,0},{2,1},{3,2},{4,7},{5,4},{6,5},{7,6},{8,11},{9,8},{10,9... | collective-permute-start | bytes 884744 | tf_op jit(solution)/shard_map/ppermute | solution.py:373
  8.4 13.3 %collective-permute-start.4 = (f32[64,1152]{1,0:T(8,128)S(1)}, f32[64,1152]{1,0:T(8,128)}, u32[]{:S(2)}, u32[]{:S(2)}) collective-permute-start(f32[64,1152]{1,0:T(8,128)S(1)} %get-tuple-element.44.refs_0_), channel_id=1, source_target_pairs={{0,1},{1,2},{2,3},{3,0},{4,5},{5,6},{6,7},{7,4},{8,9},{9,10},{10,1... | collective-permute-start | bytes 884744 | tf_op jit(solution)/shard_map/ppermute | solution.py:373
  8.4 15.5 %collective-permute-start.2 = (f32[2,64,1152]{2,1,0:T(8,128)}, f32[2,64,1152]{2,1,0:T(8,128)S(1)}, u32[]{:S(2)}, u32[]{:S(2)}) collective-permute-start(f32[2,64,1152]{2,1,0:T(8,128)} %bitcast.55), channel_id=1, source_target_pairs={{0,4},{4,0},{8,12},{12,8},{1,5},{5,1},{9,13},{13,9},{2,6},{6,2},{1... | collective-permute-start | bytes 1769480 | tf_op jit(solution)/shard_map/ppermute | solution.py:368
  21.8 17.7 %collective-permute-start.1 = (f32[64,1664]{1,0:T(8,128)S(1)}, f32[64,1664]{1,0:T(8,128)S(1)}, u32[]{:S(2)}, u32[]{:S(2)}) collective-permute-start(f32[64,1664]{1,0:T(8,128)S(1)} %pad_maximum_fusion.1.refs_1_), channel_id=1, source_target_pairs={{0,3},{1,0},{2,1},{3,2},{4,7},{5,4},{6,5},{7,6},{8,11},{9,8},{10,9... | collective-permute-start | bytes 1277960 | tf_op jit(solution)/shard_map/ppermute | solution.py:373
  23.6 19.9 %collective-permute-start.9 = (f32[64,1664]{1,0:T(8,128)S(1)}, f32[64,1664]{1,0:T(8,128)S(1)}, u32[]{:S(2)}, u32[]{:S(2)}) collective-permute-start(f32[64,1664]{1,0:T(8,128)S(1)} %pad_maximum_fusion.1.refs_1_), channel_id=1, source_target_pairs={{0,1},{1,2},{2,3},{3,0},{4,5},{5,6},{6,7},{7,4},{8,9},{9,10},{10,1... | collective-permute-start | bytes 1277960 | tf_op jit(solution)/shard_map/ppermute | solution.py:373
  39.5 21.5 %collective-permute-start.8 = (f32[64,1664]{1,0:T(8,128)S(1)}, f32[64,1664]{1,0:T(8,128)S(1)}, u32[]{:S(2)}, u32[]{:S(2)}) collective-permute-start(f32[64,1664]{1,0:T(8,128)S(1)} %collective-permute-done.1.refs_3_), channel_id=1, source_target_pairs={{2,1},{1,0},{6,5},{5,4},{10,9},{9,8},{14,13},{13,12},{18,17},{17,1... | collective-permute-start | bytes 1277960 | tf_op jit(solution)/shard_map/ppermute | solution.py:364
  43.5 17.6 %collective-permute-start.10 = (f32[64,1664]{1,0:T(8,128)S(1)}, f32[64,1664]{1,0:T(8,128)S(1)}, u32[]{:S(2)}, u32[]{:S(2)}) collective-permute-start(f32[64,1664]{1,0:T(8,128)S(1)} %collective-permute-done.9.refs_9_), channel_id=1, source_target_pairs={{1,2},{2,3},{5,6},{6,7},{9,10},{10,11},{13,14},{14,15},{17,18},{18... | collective-permute-start | bytes 1277960 | tf_op jit(solution)/shard_map/ppermute | solution.py:364
  44.2 20.0 %collective-permute-start.6 = (f32[64,1152]{1,0:T(8,128)}, f32[64,1152]{1,0:T(8,128)}, u32[]{:S(2)}, u32[]{:S(2)}) collective-permute-start(f32[64,1152]{1,0:T(8,128)} %collective-permute-done.refs_2_), channel_id=1, source_target_pairs={{2,1},{1,0},{6,5},{5,4},{10,9},{9,8},{14,13},{13,12},{18,17},{17,1... | collective-permute-start | bytes 884744 | tf_op jit(solution)/shard_map/ppermute | solution.py:364
  45.5 18.8 %collective-permute-start.7 = (f32[64,1152]{1,0:T(8,128)}, f32[64,1152]{1,0:T(8,128)}, u32[]{:S(2)}, u32[]{:S(2)}) collective-permute-start(f32[64,1152]{1,0:T(8,128)} %collective-permute-done.4.refs_8_), channel_id=1, source_target_pairs={{1,2},{2,3},{5,6},{6,7},{9,10},{10,11},{13,14},{14,15},{17,18},{18... | collective-permute-start | bytes 884744 | tf_op jit(solution)/shard_map/ppermute | solution.py:364
  46.9 16.2 %collective-permute-start.11 = (f32[576,256]{1,0:T(8,128)}, f32[576,256]{1,0:T(8,128)}, u32[]{:S(2)}, u32[]{:S(2)}) collective-permute-start(f32[576,256]{1,0:T(8,128)} %get-tuple-element.26), channel_id=1, source_target_pairs={{0,16},{16,0},{1,17},{17,1},{2,18},{18,2},{3,19},{19,3},{4,20},{20... | collective-permute-start | bytes 1769480 | tf_op jit(solution)/shard_map/ppermute | solution.py:368
  48.4 67.6 %all-to-all-start = ((f32[16,8,8,128]{3,2,1,0:T(8,128)}), f32[16,8,8,128]{3,2,1,0:T(8,128)S(1)}, u32[]{:S(2)}, u32[]{:S(2)}) async-start(f32[16,8,8,128]{3,2,1,0:T(8,128)} %shard_map.96), calls=%async_computation | async-start | bytes 1048576 | tf_op jit(solution)/shard_map/all_to_all | solution.py:501
  61.1 36.7 %collective-permute-start.22 = (f32[4,64,512]{2,1,0:T(8,128)S(1)}, f32[4,64,512]{2,1,0:T(8,128)}, u32[]{:S(2)}, u32[]{:S(2)}) collective-permute-start(f32[4,64,512]{2,1,0:T(8,128)S(1)} %pad_maximum_fusion.refs_7_), channel_id=1, source_target_pairs={{0,8},{4,12},{8,0},{12,4},{1,9},{5,13},{9,1},{13,5},{2,10},{6,14},... | collective-permute-start | bytes 1572872 | tf_op jit(solution)/shard_map/ppermute | solution.py:368
  79.8 21.2 %collective-permute-start.12 = (f32[4,32,1152]{2,1,0:T(8,128)}, f32[4,32,1152]{2,1,0:T(8,128)S(1)}, u32[]{:S(2)}, u32[]{:S(2)}) collective-permute-start(f32[4,32,1152]{2,1,0:T(8,128)} %get-tuple-element.30), channel_id=1, source_target_pairs={{0,4},{4,0},{8,12},{12,8},{1,5},{5,1},{9,13},{13,9},{2,6},{6,2},{1... | collective-permute-start | bytes 1769480 | tf_op jit(solution)/shard_map/ppermute | solution.py:368
  80.7 17.1 %collective-permute-start.16 = (f32[2,144,256]{2,1,0:T(8,128)}, f32[2,144,256]{2,1,0:T(8,128)}, u32[]{:S(2)}, u32[]{:S(2)}) collective-permute-start(f32[2,144,256]{2,1,0:T(8,128)} %pad_maximum_fusion.2), channel_id=1, source_target_pairs={{0,1},{1,0},{2,3},{3,2},{4,5},{5,4},{6,7},{7,6},{8,9},{9,8},{10,11... | collective-permute-start | bytes 884744 | tf_op jit(solution)/shard_map/ppermute | solution.py:368
  89.8 14.6 %collective-permute-start.21 = (f32[4,64,512]{2,1,0:T(8,128)S(1)}, f32[4,64,512]{2,1,0:T(8,128)}, u32[]{:S(2)}, u32[]{:S(2)}) collective-permute-start(f32[4,64,512]{2,1,0:T(8,128)S(1)} %pad_maximum_fusion.refs_7_), channel_id=1, source_target_pairs={{0,4},{4,0},{8,12},{12,8},{1,5},{5,1},{9,13},{13,9},{2,6},{6,2},{1... | collective-permute-start | bytes 1572872 | tf_op jit(solution)/shard_map/ppermute | solution.py:368
  90.0 14.3 %collective-permute-start.20 = (f32[256,256]{1,0:T(8,128)S(1)}, f32[256,256]{1,0:T(8,128)S(1)}, u32[]{:S(2)}, u32[]{:S(2)}) collective-permute-start(f32[256,256]{1,0:T(8,128)S(1)} %copy-done.8), channel_id=1, source_target_pairs={{0,16},{16,0},{1,17},{17,1},{2,18},{18,2},{3,19},{19,3},{4,20},{20... | collective-permute-start | bytes 786440 | tf_op jit(solution)/shard_map/ppermute | solution.py:368
  97.8 20.5 %collective-permute-start.23 = (f32[4,64,512]{2,1,0:T(8,128)}, f32[4,64,512]{2,1,0:T(8,128)}, u32[]{:S(2)}, u32[]{:S(2)}) collective-permute-start(f32[4,64,512]{2,1,0:T(8,128)} %collective-permute-done.22.refs_9_), channel_id=1, source_target_pairs={{0,4},{4,0},{8,12},{12,8},{1,5},{5,1},{9,13},{13,9},{2,6},{6,2},{1... | collective-permute-start | bytes 1572872 | tf_op jit(solution)/shard_map/ppermute | solution.py:368
  101.1 14.4 %collective-permute-start.17 = (f32[144,256]{1,0:T(8,128)}, f32[144,256]{1,0:T(8,128)S(1)}, u32[]{:S(2)}, u32[]{:S(2)}) collective-permute-start(f32[144,256]{1,0:T(8,128)} %get-tuple-element.33), channel_id=1, source_target_pairs={{0,2},{1,3},{2,0},{3,1},{4,6},{5,7},{6,4},{7,5},{8,10},{9,11},{10,... | collective-permute-start | bytes 442376 | tf_op jit(solution)/shard_map/ppermute | solution.py:368
  104.4 13.9 %collective-permute-start.19 = (f32[144,256]{1,0:T(8,128)}, f32[144,256]{1,0:T(8,128)S(1)}, u32[]{:S(2)}, u32[]{:S(2)}) collective-permute-start(f32[144,256]{1,0:T(8,128)} %get-tuple-element.33), channel_id=1, source_target_pairs={{0,18},{1,19},{2,16},{3,17},{16,2},{17,3},{18,0},{19,1},{4,22},{5,... | collective-permute-start | bytes 442376 | tf_op jit(solution)/shard_map/ppermute | solution.py:433
  104.5 19.2 %collective-permute-start.15 = (f32[32,1152]{1,0:T(8,128)S(1)}, f32[32,1152]{1,0:T(8,128)S(1)}, u32[]{:S(2)}, u32[]{:S(2)}) collective-permute-start(f32[32,1152]{1,0:T(8,128)S(1)} %get-tuple-element.41), channel_id=1, source_target_pairs={{0,24},{4,28},{8,16},{12,20},{16,8},{20,12},{24,0},{28,4},{1,25},{... | collective-permute-start | bytes 442376 | tf_op jit(solution)/shard_map/ppermute | solution.py:433
  105.9 17.8 %collective-permute-start.13 = (f32[32,1152]{1,0:T(8,128)S(1)}, f32[32,1152]{1,0:T(8,128)S(1)}, u32[]{:S(2)}, u32[]{:S(2)}) collective-permute-start(f32[32,1152]{1,0:T(8,128)S(1)} %get-tuple-element.42), channel_id=1, source_target_pairs={{0,8},{4,12},{8,0},{12,4},{16,24},{20,28},{24,16},{28,20},{1,9},{5... | collective-permute-start | bytes 442376 | tf_op jit(solution)/shard_map/ppermute | solution.py:433
  115.5 8.2 %collective-permute-start.14 = (f32[32,1152]{1,0:T(8,128)S(1)}, f32[32,1152]{1,0:T(8,128)S(1)}, u32[]{:S(2)}, u32[]{:S(2)}) collective-permute-start(f32[32,1152]{1,0:T(8,128)S(1)} %get-tuple-element.40), channel_id=1, source_target_pairs={{0,16},{4,20},{8,24},{12,28},{16,0},{20,4},{24,8},{28,12},{1,17},{... | collective-permute-start | bytes 442376 | tf_op jit(solution)/shard_map/ppermute | solution.py:433
  123.7 10.1 %all-to-all-start.1 = ((f32[16,1,128]{2,1,0:T(1,128)}), f32[16,1,128]{2,1,0:T(1,128)S(1)}, u32[]{:S(2)}, u32[]{:S(2)}) async-start(f32[16,1,128]{2,1,0:T(1,128)} %bitcast.59), calls=%async_computation.1 | async-start | bytes 16384 | tf_op jit(solution)/shard_map/all_to_all | solution.py:527
  (21 other events, 237.9 us)
